TPU v7x, 32 devices: a whole 2x2x4 slice. The times are simulated.
32 devices in a mesh: section: 2 (over core), frame: 2 (over y), tile: 8 (over z, x).
Axes of the slice: x: 2, y: 2, z: 4, core: 2. Of those that a mesh axis runs over, the one named last changes fastest.
Arguments:
- queries: bfloat16 [2, 8, 256, 1536], P('frame', 'tile', None, 'section'), may hold values from -5 to 5
- key_rows: bfloat16 [2, 8, 256, 1536], P('frame', 'tile', None, 'section'), may hold values from -5 to 5
- value_rows: bfloat16 [2, 8, 256, 1536], P('frame', 'tile', None, 'section'), may hold values from -6 to 6
- grad_rows: bfloat16 [2, 8, 256, 1536], P('frame', 'tile', 'section'), may hold values from -6 to 6
- offsets: int32 [12, 9, 3], P('section'), may hold values from -1 to 1, as said below
- counts: int32 [2, 8], replicated, may hold values from 8 to 256, as said below
Outputs:
- grad_query: bfloat16 [2, 8, 256, 1536], P('frame', 'tile', None, 'section')
- grad_key: bfloat16 [2, 8, 256, 1536], P('frame', 'tile', None, 'section')
- grad_value: bfloat16 [2, 8, 256, 1536], P('frame', 'tile', None, 'section')
Inputs may be any that keep to these rules, and one draw needn't show every extreme that they name: `offsets`: of heads 2m and 2m + 1, one lists the nine tiles (0, a, b) and the other the nine tiles (a, b, 0), for a and b each of -1, 0, 1, each head in an order of its own. `counts`: the real tokens of a tile fill its first slots; tiles outside the last block of frames and the last row of spatial tiles are full; the last tile of the grid holds 8; a tile holds a multiple of 8 real tokens.
All inputs are finite; a program needn't handle non-finite values.
Results may differ from a plain program's by a relative error of at most 0.008.
Values may be sent and summed in bfloat16 or wider, within the bound.
No kernel may reach another device: no remote copies, remote signals or barrier semaphores. Data moves between devices by JAX's collectives and lax.ppermute only.
A program may use at most 128 MiB of HBM per device.

v0:
```python
import math

import jax
import jax.numpy as jnp
from jax import lax
from jax.sharding import PartitionSpec as P

NCT = 4


plane_steps = [(row_step, col_step) for row_step in (-1, 0, 1) for col_step in (-1, 0, 1)]
frame_steps = [(frame_step, row_step) for frame_step in (-1, 0, 1) for row_step in (-1, 0, 1)]


def from_behind(block, axis, distance):
    devices = range(lax.axis_size(axis))
    route = [(i - distance, i) for i in devices if i - distance in devices]
    return lax.ppermute(block, axis, route)


def tile_count(counts, frame_pos, row_pos, col_pos, col_count):
    frame_count = counts.shape[0]
    row_count = counts.shape[1] // col_count
    inside = (
        (frame_pos >= 0)
        & (frame_pos < frame_count)
        & (row_pos >= 0)
        & (row_pos < row_count)
        & (col_pos >= 0)
        & (col_pos < col_count)
    )
    spot_pos = jnp.clip(row_pos, 0, row_count - 1) * col_count + jnp.clip(col_pos, 0, col_count - 1)
    stored = counts[jnp.clip(frame_pos, 0, frame_count - 1), spot_pos]
    return jnp.where(inside, stored, 0)


def head_columns(values, head_at, head_dim):
    return lax.dynamic_slice_in_dim(values, head_at * head_dim, head_dim, values.ndim - 1)


def pick_heads(values, chosen, head_dim):
    split = values.reshape(values.shape[0], values.shape[1] // head_dim, head_dim)
    return jnp.take(split, chosen, axis=1).reshape(values.shape[0], chosen.shape[0] * head_dim)


def unpack_heads(first_part, second_part, restore, head_dim):
    joined = jnp.concatenate([first_part, second_part], axis=1)
    split = joined.reshape(joined.shape[0], joined.shape[1] // head_dim, head_dim)
    return jnp.take(split, restore, axis=1).reshape(joined.shape[0], joined.shape[1])


def kv_plane(pair, shift_by):
    return from_behind((pair[0], pair[1]), "tile", shift_by)


def kv_frame(pair, shift_by):
    return from_behind((pair[0], pair[1]), "frame", shift_by)


def near_tiles(own, pack_first, pack_second, plane_call, frame_call, col_count):
    own_first = pack_first(own)
    own_second = pack_second(own)
    plane = {(0, 0): own_first}
    across = {0: own_second}
    for row_step, col_step in plane_steps:
        if row_step == 0 and col_step == 0:
            continue
        shift_by = -(row_step * col_count + col_step)
        if col_step == 0:
            got = plane_call(own, shift_by)
            plane[row_step, 0] = pack_first(got)
            across[row_step] = pack_second(got)
        else:
            plane[row_step, col_step] = plane_call(own_first, shift_by)
    stacked = (
        jnp.stack([across[-1][0], across[0][0], across[1][0]]),
        jnp.stack([across[-1][1], across[0][1], across[1][1]]),
    )
    frames = {}
    for row_step in (-1, 0, 1):
        frames[0, row_step] = across[row_step]
    for frame_step in (-1, 1):
        got = frame_call(stacked, -frame_step)
        for row_step in (-1, 0, 1):
            frames[frame_step, row_step] = (got[0][row_step + 1], got[1][row_step + 1])
    first = (
        jnp.stack([plane[step][0] for step in plane_steps]),
        jnp.stack([plane[step][1] for step in plane_steps]),
    )
    second = (
        jnp.stack([frames[step][0] for step in frame_steps]),
        jnp.stack([frames[step][1] for step in frame_steps]),
    )
    return (first, second)


def window_grads(query_head, grad_head, key_window, value_window, live_keys, score_scale):
    scores = (
        jnp.einsum("ie,we->iw", query_head, key_window, preferred_element_type=jnp.float32)
        * score_scale
    )
    scores = jnp.where(live_keys[None, :], scores, -jnp.inf)
    row_max = jnp.max(scores, axis=1, keepdims=True)
    log_total = row_max + jnp.log(jnp.sum(jnp.exp(scores - row_max), axis=1, keepdims=True))
    softmax = jnp.exp(scores - log_total)
    grad_softmax = jnp.einsum(
        "ie,we->iw", grad_head, value_window, preferred_element_type=jnp.float32
    )
    row_dot = jnp.sum(softmax * grad_softmax, axis=1, keepdims=True)
    grad_scores = (softmax * (grad_softmax - row_dot)).astype(jnp.bfloat16)
    return (softmax, grad_scores, log_total[:, 0], row_dot[:, 0])


def group_pass(query_part, grad_part, key_stack, value_stack, live_keys, score_scale, head_dim):
    tile_len = query_part.shape[0]
    count_here = query_part.shape[1] // head_dim
    window = key_stack.shape[0]

    def one_head(head_at, buffers):
        query_out, total_all, dot_all, key_parts, value_parts = buffers
        query_head = head_columns(query_part, head_at, head_dim)
        grad_head = head_columns(grad_part, head_at, head_dim)
        key_window = head_columns(key_stack, head_at, head_dim).reshape(window * tile_len, head_dim)
        value_window = head_columns(value_stack, head_at, head_dim).reshape(
            window * tile_len, head_dim
        )
        softmax, grad_scores, log_total, row_dot = window_grads(
            query_head, grad_head, key_window, value_window, live_keys, score_scale
        )
        query_grad = (
            jnp.dot(grad_scores, key_window, preferred_element_type=jnp.float32) * score_scale
        ).astype(jnp.bfloat16)
        query_out = lax.dynamic_update_slice_in_dim(query_out, query_grad, head_at * head_dim, 1)
        total_all = lax.dynamic_update_slice_in_dim(total_all, log_total[None], head_at, 0)
        dot_all = lax.dynamic_update_slice_in_dim(dot_all, row_dot[None], head_at, 0)
        softmax_low = softmax.astype(jnp.bfloat16)
        value_part = jnp.einsum(
            "iw,ie->we", softmax_low, grad_head, preferred_element_type=jnp.float32
        )
        key_part = (
            jnp.einsum("iw,ie->we", grad_scores, query_head, preferred_element_type=jnp.float32)
            * score_scale
        )
        key_parts = lax.dynamic_update_slice_in_dim(
            key_parts, key_part.reshape(window, tile_len, head_dim), head_at * head_dim, 2
        )
        value_parts = lax.dynamic_update_slice_in_dim(
            value_parts, value_part.reshape(window, tile_len, head_dim), head_at * head_dim, 2
        )
        return (query_out, total_all, dot_all, key_parts, value_parts)

    part_shape = (window, tile_len, count_here * head_dim)
    start = (
        jnp.zeros((tile_len, count_here * head_dim), jnp.bfloat16),
        jnp.zeros((count_here, tile_len), jnp.float32),
        jnp.zeros((count_here, tile_len), jnp.float32),
        jnp.zeros(part_shape, jnp.float32),
        jnp.zeros(part_shape, jnp.float32),
    )
    return lax.fori_loop(0, count_here, one_head, start)


def local(queries, key_rows, value_rows, grad_rows, offsets, counts):
    heads_here = offsets.shape[0]
    width_here = queries.shape[3]
    head_dim = width_here // heads_here
    tile_len = queries.shape[2]
    group_heads = heads_here // 2
    score_scale = 1.0 / math.sqrt(head_dim)
    col_count = NCT
    frame_at = lax.axis_index("frame")
    spot_at = lax.axis_index("tile")
    row_at = spot_at // col_count
    col_at = spot_at % col_count
    positions = jnp.arange(tile_len, dtype=jnp.int32)
    grad_local = lax.all_to_all(grad_rows, "section", split_axis=3, concat_axis=2, tiled=True)
    own_count = tile_count(counts, frame_at, row_at, col_at, col_count)
    own_live = positions < own_count
    masked = jnp.where(own_live[:, None], grad_local[0, 0], jnp.zeros((), jnp.bfloat16))
    query_tile = queries[0, 0]
    key_tile = key_rows[0, 0]
    value_tile = value_rows[0, 0]
    temporal = jnp.any(offsets[:, :, 0] != 0, axis=1).astype(jnp.int32)
    order = jnp.argsort(temporal, stable=True)
    heads_first = order[:group_heads]
    heads_second = order[group_heads:]
    restore = jnp.argsort(order)

    def pack_first(pair):
        return (
            pick_heads(pair[0], heads_first, head_dim),
            pick_heads(pair[1], heads_first, head_dim),
        )

    def pack_second(pair):
        return (
            pick_heads(pair[0], heads_second, head_dim),
            pick_heads(pair[1], heads_second, head_dim),
        )

    first_live = jnp.concatenate(
        [
            positions
            < tile_count(counts, frame_at, row_at + row_step, col_at + col_step, col_count)
            for row_step, col_step in plane_steps
        ]
    )
    second_live = jnp.concatenate(
        [
            positions
            < tile_count(counts, frame_at + frame_step, row_at + row_step, col_at, col_count)
            for frame_step, row_step in frame_steps
        ]
    )
    first_kv, second_kv = near_tiles(
        (key_tile, value_tile), pack_first, pack_second, kv_plane, kv_frame, col_count
    )
    first_res = group_pass(
        pick_heads(query_tile, heads_first, head_dim),
        pick_heads(masked, heads_first, head_dim),
        first_kv[0],
        first_kv[1],
        first_live,
        score_scale,
        head_dim,
    )
    second_res = group_pass(
        pick_heads(query_tile, heads_second, head_dim),
        pick_heads(masked, heads_second, head_dim),
        second_kv[0],
        second_kv[1],
        second_live,
        score_scale,
        head_dim,
    )
    first_res, second_res = (first_res, second_res)
    query_out = unpack_heads(first_res[0], second_res[0], restore, head_dim)
    second_key_near = second_res[3][3:6]
    second_value_near = second_res[4][3:6]
    for frame_step in (-1, 1):
        lowest = (frame_step + 1) * 3
        got_key, got_value = (
            from_behind(
                second_res[3][lowest : lowest + 3].astype(jnp.bfloat16), "frame", frame_step
            ).astype(jnp.float32),
            from_behind(
                second_res[4][lowest : lowest + 3].astype(jnp.bfloat16), "frame", frame_step
            ).astype(jnp.float32),
        )
        second_key_near = second_key_near + got_key
        second_value_near = second_value_near + got_value
    first_key_total = first_res[3][4]
    first_value_total = first_res[4][4]
    second_key_total = second_key_near[1]
    second_value_total = second_value_near[1]
    group_width = first_key_total.shape[1]
    for slot_at, (row_step, col_step) in enumerate(plane_steps):
        if row_step == 0 and col_step == 0:
            continue
        shift_by = row_step * col_count + col_step
        if col_step == 0:
            send_key = jnp.concatenate(
                [first_res[3][slot_at], second_key_near[row_step + 1]], axis=1
            )
            send_value = jnp.concatenate(
                [first_res[4][slot_at], second_value_near[row_step + 1]], axis=1
            )
        else:
            send_key = first_res[3][slot_at]
            send_value = first_res[4][slot_at]
        got_key, got_value = (
            from_behind(send_key.astype(jnp.bfloat16), "tile", shift_by).astype(send_key.dtype),
            from_behind(send_value.astype(jnp.bfloat16), "tile", shift_by).astype(send_value.dtype),
        )
        first_key_total = first_key_total + got_key[:, :group_width]
        first_value_total = first_value_total + got_value[:, :group_width]
        if col_step == 0:
            second_key_total = second_key_total + got_key[:, group_width:]
            second_value_total = second_value_total + got_value[:, group_width:]
    grad_key = unpack_heads(first_key_total, second_key_total, restore, head_dim).astype(
        jnp.bfloat16
    )
    grad_value = unpack_heads(first_value_total, second_value_total, restore, head_dim).astype(
        jnp.bfloat16
    )
    return (query_out[None, None], grad_key[None, None], grad_value[None, None])


def solution(mesh):
    return jax.shard_map(
        local,
        mesh=mesh,
        in_specs=(
            P("frame", "tile", None, "section"),
            P("frame", "tile", None, "section"),
            P("frame", "tile", None, "section"),
            P("frame", "tile", "section", None),
            P("section", None, None),
            P(),
        ),
        out_specs=(
            P("frame", "tile", None, "section"),
            P("frame", "tile", None, "section"),
            P("frame", "tile", None, "section"),
        ),
        check_vma=False,
    )
```

profile of v0, /device:TPU:24, one launch (start us, length us, event | category | flops | bytes accessed | tf_op | source)
XLA Modules:
  0.0 454.5 jit_solution(5852380335821789567)
XLA Ops:
  3.2 6.2 %collective-permute-start.6 = (bf16[256,768]{0,1:T(8,128)(2,1)S(1)}, bf16[256,768]{0,1:T(8,128)(2,1)S(1)}, u32[]{:S(2)}, u32[]{:S(2)}) collective-permute-start(bf16[256,768]{0,1:T(8,128)(2,1)S(1)} %bitcast.259), channel_id=1, source_target_pairs={{4,0},{5,1},{6,2},{7,3},{12,8},{13,9},{14,10},{15,11},{20,16},{21,... | collective-permute-start | bytes 1179656 | tf_op jit(solution)/shard_map/ppermute | solution.py:18
  11.9 7.0 %collective-permute-start.14 = (bf16[256,768]{0,1:T(8,128)(2,1)S(1)}, bf16[256,768]{0,1:T(8,128)(2,1)}, u32[]{:S(2)}, u32[]{:S(2)}) collective-permute-start(bf16[256,768]{0,1:T(8,128)(2,1)S(1)} %bitcast.256), channel_id=1, source_target_pairs={{4,0},{5,1},{6,2},{7,3},{12,8},{13,9},{14,10},{15,11},{20,16},{21,... | collective-permute-start | bytes 1179656 | tf_op jit(solution)/shard_map/ppermute | solution.py:18
  19.9 8.8 %reduce.1 = bf16[1536,128]{1,0:T(8,128)(2,1)S(1)} reduce(bf16[1536,1,1,128]{3,2,1,0:T(2,128)(2,1)S(1)} %bitcast.240, bf16[]{:T(256)} %broadcast.420), dimensions={1,2}, to_apply=%bitcast.180.reduce_sub_computation | reduce | bytes 786434
  29.6 3.6 all-to-all-start
  77.3 4.4 collective-permute-start.18
  84.4 6.2 %collective-permute-start.16 = (bf16[3,256,384]{1,2,0:T(8,128)(2,1)}, bf16[3,256,384]{1,2,0:T(8,128)(2,1)}, u32[]{:S(2)}, u32[]{:S(2)}) collective-permute-start(bf16[3,256,384]{1,2,0:T(8,128)(2,1)} %pad_maximum_fusion.2), channel_id=1, source_target_pairs={{0,8},{1,9},{2,10},{3,11},{4,12},{5,13},{6,14},{7,15},{16,24},{17,... | collective-permute-start | bytes 1769480 | tf_op jit(solution)/shard_map/ppermute | solution.py:18
  97.9 8.7 %collective-permute-done = bf16[256,384]{0,1:T(8,128)(2,1)S(1)} collective-permute-done((bf16[256,384]{0,1:T(8,128)(2,1)S(1)}, bf16[256,384]{0,1:T(8,128)(2,1)S(1)}, u32[]{:S(2)}, u32[]{:S(2)}) %collective-permute-start) | collective-permute-done | bytes 196640 | tf_op jit(solution)/shard_map/ppermute | solution.py:18
  108.6 7.3 %collective-permute-done.10 = bf16[256,384]{0,1:T(8,128)(2,1)S(1)} collective-permute-done((bf16[256,384]{0,1:T(8,128)(2,1)S(1)}, bf16[256,384]{0,1:T(8,128)(2,1)S(1)}, u32[]{:S(2)}, u32[]{:S(2)}) %collective-permute-start.10) | collective-permute-done | bytes 196640 | tf_op jit(solution)/shard_map/ppermute | solution.py:18
  115.9 6.8 %collective-permute-start.11 = (bf16[256,384]{0,1:T(8,128)(2,1)S(1)}, bf16[256,384]{0,1:T(8,128)(2,1)S(1)}, u32[]{:S(2)}, u32[]{:S(2)}) collective-permute-start(bf16[256,384]{0,1:T(8,128)(2,1)S(1)} %bitcast.271), channel_id=1, source_target_pairs={{0,1},{1,2},{2,3},{3,4},{4,5},{5,6},{6,7},{8,9},{9,10},{10,11},{11... | collective-permute-start | bytes 589832 | tf_op jit(solution)/shard_map/ppermute | solution.py:18
  123.5 2.8 collective-permute-done.11
  128.3 11.0 %collective-permute-done.2 = bf16[256,384]{0,1:T(8,128)(2,1)S(1)} collective-permute-done((bf16[256,384]{0,1:T(8,128)(2,1)S(1)}, bf16[256,384]{0,1:T(8,128)(2,1)S(1)}, u32[]{:S(2)}, u32[]{:S(2)}) %collective-permute-start.2) | collective-permute-done | bytes 196640 | tf_op jit(solution)/shard_map/ppermute | solution.py:18
  141.2 6.7 %collective-permute-done.3 = bf16[256,384]{0,1:T(8,128)(2,1)S(1)} collective-permute-done((bf16[256,384]{0,1:T(8,128)(2,1)S(1)}, bf16[256,384]{0,1:T(8,128)(2,1)S(1)}, u32[]{:S(2)}, u32[]{:S(2)}) %collective-permute-start.3) | collective-permute-done | bytes 196640 | tf_op jit(solution)/shard_map/ppermute | solution.py:18
  150.5 4.9 %collective-permute-done.12 = bf16[256,384]{0,1:T(8,128)(2,1)S(1)} collective-permute-done((bf16[256,384]{0,1:T(8,128)(2,1)S(1)}, bf16[256,384]{0,1:T(8,128)(2,1)S(1)}, u32[]{:S(2)}, u32[]{:S(2)}) %collective-permute-start.12) | collective-permute-done | bytes 196640 | tf_op jit(solution)/shard_map/ppermute | solution.py:18
  157.6 3.1 collective-permute-done.13
  160.6 2.1 collective-permute-start.4
  163.4 4.8 %collective-permute-done.4 = bf16[256,384]{0,1:T(8,128)(2,1)S(1)} collective-permute-done((bf16[256,384]{0,1:T(8,128)(2,1)S(1)}, bf16[256,384]{0,1:T(8,128)(2,1)S(1)}, u32[]{:S(2)}, u32[]{:S(2)}) %collective-permute-start.4) | collective-permute-done | bytes 196640 | tf_op jit(solution)/shard_map/ppermute | solution.py:18
  168.2 10.9 %collective-permute-start.5 = (bf16[256,384]{0,1:T(8,128)(2,1)S(1)}, bf16[256,384]{0,1:T(8,128)(2,1)S(1)}, u32[]{:S(2)}, u32[]{:S(2)}) collective-permute-start(bf16[256,384]{0,1:T(8,128)(2,1)S(1)} %bitcast.281), channel_id=1, source_target_pairs={{3,0},{4,1},{5,2},{6,3},{7,4},{11,8},{12,9},{13,10},{14,11},{15,12... | collective-permute-start | bytes 589832 | tf_op jit(solution)/shard_map/ppermute | solution.py:18
  179.1 5.1 %collective-permute-done.5 = bf16[256,384]{0,1:T(8,128)(2,1)S(1)} collective-permute-done((bf16[256,384]{0,1:T(8,128)(2,1)S(1)}, bf16[256,384]{0,1:T(8,128)(2,1)S(1)}, u32[]{:S(2)}, u32[]{:S(2)}) %collective-permute-start.5) | collective-permute-done | bytes 196640 | tf_op jit(solution)/shard_map/ppermute | solution.py:18
  184.2 2.2 collective-permute-start.15
  187.1 2.2 collective-permute-done.15
  189.3 7.1 %collective-permute-start.7 = (bf16[256,384]{0,1:T(8,128)(2,1)S(1)}, bf16[256,384]{0,1:T(8,128)(2,1)S(1)}, u32[]{:S(2)}, u32[]{:S(2)}) collective-permute-start(bf16[256,384]{0,1:T(8,128)(2,1)S(1)} %bitcast.282), channel_id=1, source_target_pairs={{5,0},{6,1},{7,2},{13,8},{14,9},{15,10},{21,16},{22,17},{23,18},{2... | collective-permute-start | bytes 589832 | tf_op jit(solution)/shard_map/ppermute | solution.py:18
  197.1 2.5 collective-permute-done.7
  199.6 2.1 broadcast.129.clone2.2
  201.7 2.1 broadcast.129.clone2.3
  204.5 58.4 %while.34 = (s32[]{:T(128)}, bf16[256,384]{0,1:T(8,128)(2,1)}, f32[9,256,384]{1,2,0:T(8,128)}, f32[9,256,384]{1,2,0:T(8,128)}, pred[2304]{0:T(1024)(128)(4,1)S(1...) while((s32[]{:T(128)}, bf16[256,384]{0,1:T(8,128)(2,1)}, ...), condition=%wide.region_7.9_spmd, body=%wide.region_3.8_spmd.sunk | while | flops 763592192 | bytes 62535252 | solution.py:160
  211.4 2.4 convolution_multiply_fusion.8
  213.8 2.7 copy.244
  216.5 2.5 fusion.89
  230.8 2.4 convolution_multiply_fusion.8
  233.2 2.7 copy.244
  236.0 2.5 fusion.89
  250.3 2.4 convolution_multiply_fusion.8
  252.7 2.7 copy.244
  255.4 2.5 fusion.89
  262.8 3.4 convert.52
  271.5 2.2 broadcast.129.clone2
  273.7 2.1 broadcast.129.clone2.1
  276.5 58.1 %while.35 = (s32[]{:T(128)}, bf16[256,384]{0,1:T(8,128)(2,1)}, f32[9,256,384]{1,2,0:T(8,128)}, f32[9,256,384]{1,2,0:T(8,128)}, pred[2304]{0:T(1024)(128)(4,1)S(1...) while((s32[]{:T(128)}, bf16[256,384]{0,1:T(8,128)(2,1)}, ...), condition=%wide.region_12.14_spmd, body=%wide.region_8.13_spmd.sunk | while | flops 763592192 | bytes 62535252 | solution.py:160
  283.3 2.4 convolution_multiply_fusion.9
  285.7 2.7 copy.249
  288.4 2.5 fusion.100
  302.8 2.4 convolution_multiply_fusion.9
  305.2 2.7 copy.249
  307.8 2.5 fusion.100
  322.1 2.4 convolution_multiply_fusion.9
  324.5 2.7 copy.249
  327.2 2.5 fusion.100
  334.6 2.3 convert.53
  338.7 5.2 %collective-permute-start.22 = (bf16[3,256,384]{1,2,0:T(8,128)(2,1)S(1)}, bf16[3,256,384]{1,2,0:T(8,128)(2,1)S(1)}, u32[]{:S(2)}, u32[]{:S(2)}) collective-permute-start(bf16[3,256,384]{1,2,0:T(8,128)(2,1)S(1)} %get-tuple-element.465), channel_id=1, source_target_pairs={{0,8},{1,9},{2,10},{3,11},{4,12},{5,13},{6,14},{7,15},{16,24},{17,... | collective-permute-start | bytes 1769480 | tf_op jit(solution)/shard_map/ppermute | solution.py:18
  344.8 7.1 %collective-permute-start.20 = (bf16[256,384]{0,1:T(8,128)(2,1)S(1)}, bf16[256,384]{0,1:T(8,128)(2,1)S(1)}, u32[]{:S(2)}, u32[]{:S(2)}) collective-permute-start(bf16[256,384]{0,1:T(8,128)(2,1)S(1)} %get-tuple-element.456), channel_id=1, source_target_pairs={{5,0},{6,1},{7,2},{13,8},{14,9},{15,10},{21,16},{22,17},{23,18},{2... | collective-permute-start | bytes 589832 | tf_op jit(solution)/shard_map/ppermute | solution.py:18
  353.1 6.0 %collective-permute-start.25 = (bf16[256,384]{0,1:T(8,128)(2,1)S(1)}, bf16[256,384]{0,1:T(8,128)(2,1)S(1)}, u32[]{:S(2)}, u32[]{:S(2)}) collective-permute-start(bf16[256,384]{0,1:T(8,128)(2,1)S(1)} %get-tuple-element.461), channel_id=1, source_target_pairs={{1,0},{2,1},{3,2},{4,3},{5,4},{6,5},{7,6},{9,8},{10,9},{11,10},{12... | collective-permute-start | bytes 589832 | tf_op jit(solution)/shard_map/ppermute | solution.py:18
  363.2 4.6 %collective-permute-start.32 = (bf16[3,256,384]{1,2,0:T(8,128)(2,1)S(1)}, bf16[3,256,384]{1,2,0:T(8,128)(2,1)S(1)}, u32[]{:S(2)}, u32[]{:S(2)}) collective-permute-start(bf16[3,256,384]{1,2,0:T(8,128)(2,1)S(1)} %get-tuple-element.455), channel_id=1, source_target_pairs={{0,8},{1,9},{2,10},{3,11},{4,12},{5,13},{6,14},{7,15},{16,24},{17,... | collective-permute-start | bytes 1769480 | tf_op jit(solution)/shard_map/ppermute | solution.py:18
  367.8 2.6 fusion.41
  373.7 2.1 collective-permute-start.23
  380.0 3.1 collective-permute-start.26
  383.1 7.0 %collective-permute-start.33 = (bf16[256,768]{0,1:T(8,128)(2,1)}, bf16[256,768]{0,1:T(8,128)(2,1)}, u32[]{:S(2)}, u32[]{:S(2)}) collective-permute-start(bf16[256,768]{0,1:T(8,128)(2,1)} %pad_maximum_fusion.7), channel_id=1, source_target_pairs={{4,0},{5,1},{6,2},{7,3},{12,8},{13,9},{14,10},{15,11},{20,16},{21,... | collective-permute-start | bytes 1179656 | tf_op jit(solution)/shard_map/ppermute | solution.py:18
  392.2 1.9 copy.192
  394.1 2.3 gather_fusion
  396.4 1.9 copy.193
  400.9 4.5 %collective-permute-done.28 = bf16[256,768]{0,1:T(8,128)(2,1)} collective-permute-done((bf16[256,768]{0,1:T(8,128)(2,1)}, bf16[256,768]{0,1:T(8,128)(2,1)}, u32[]{:S(2)}, u32[]{:S(2)}) %collective-permute-start.28) | collective-permute-done | bytes 393248 | tf_op jit(solution)/shard_map/ppermute | solution.py:18
  405.5 17.3 %collective-permute-start.30 = (bf16[256,384]{0,1:T(8,128)(2,1)}, bf16[256,384]{0,1:T(8,128)(2,1)}, u32[]{:S(2)}, u32[]{:S(2)}) collective-permute-start(bf16[256,384]{0,1:T(8,128)(2,1)} %get-tuple-element.446), channel_id=1, source_target_pairs={{5,0},{6,1},{7,2},{13,8},{14,9},{15,10},{21,16},{22,17},{23,18},{2... | collective-permute-start | bytes 589832 | tf_op jit(solution)/shard_map/ppermute | solution.py:18
  428.8 2.0 collective-permute-start.34
  432.7 4.6 %collective-permute-start.36 = (bf16[256,384]{0,1:T(8,128)(2,1)}, bf16[256,384]{0,1:T(8,128)(2,1)}, u32[]{:S(2)}, u32[]{:S(2)}) collective-permute-start(bf16[256,384]{0,1:T(8,128)(2,1)} %get-tuple-element.450), channel_id=1, source_target_pairs={{0,1},{1,2},{2,3},{3,4},{4,5},{5,6},{6,7},{8,9},{9,10},{10,11},{11... | collective-permute-start | bytes 589832 | tf_op jit(solution)/shard_map/ppermute | solution.py:18
  444.3 2.3 gather_fusion.17
  (441 shorter events, 183.2 us)
Async XLA Ops:
  0.6 18.2 %copy-start.37 = (bf16[1,1,128,1536]{3,2,1,0:T(8,128)(2,1)S(1)}, bf16[1,1,128,1536]{3,2,1,0:T(8,128)(2,1)}, u32[]{:S(2)}) copy-start(bf16[1,1,128,1536]{3,2,1,0:T(8,128)(2,1)} %param.17) | copy-start | bytes 1179652
  1.9 59.2 %collective-permute-start.1 = (bf16[256,768]{0,1:T(8,128)(2,1)S(1)}, bf16[256,768]{0,1:T(8,128)(2,1)}, u32[]{:S(2)}, u32[]{:S(2)}) collective-permute-start(bf16[256,768]{0,1:T(8,128)(2,1)S(1)} %bitcast.258), channel_id=1, source_target_pairs={{0,4},{1,5},{2,6},{3,7},{8,12},{9,13},{10,14},{11,15},{16,20},{17,... | collective-permute-start | bytes 1179656 | tf_op jit(solution)/shard_map/ppermute | solution.py:18
  3.2 60.3 %collective-permute-start.6 = (bf16[256,768]{0,1:T(8,128)(2,1)S(1)}, bf16[256,768]{0,1:T(8,128)(2,1)S(1)}, u32[]{:S(2)}, u32[]{:S(2)}) collective-permute-start(bf16[256,768]{0,1:T(8,128)(2,1)S(1)} %bitcast.259), channel_id=1, source_target_pairs={{4,0},{5,1},{6,2},{7,3},{12,8},{13,9},{14,10},{15,11},{20,16},{21,... | collective-permute-start | bytes 1179656 | tf_op jit(solution)/shard_map/ppermute | solution.py:18
  10.6 54.3 %collective-permute-start.9 = (bf16[256,768]{0,1:T(8,128)(2,1)S(1)}, bf16[256,768]{0,1:T(8,128)(2,1)}, u32[]{:S(2)}, u32[]{:S(2)}) collective-permute-start(bf16[256,768]{0,1:T(8,128)(2,1)S(1)} %bitcast.255), channel_id=1, source_target_pairs={{0,4},{1,5},{2,6},{3,7},{8,12},{9,13},{10,14},{11,15},{16,20},{17,... | collective-permute-start | bytes 1179656 | tf_op jit(solution)/shard_map/ppermute | solution.py:18
  11.9 55.4 %collective-permute-start.14 = (bf16[256,768]{0,1:T(8,128)(2,1)S(1)}, bf16[256,768]{0,1:T(8,128)(2,1)}, u32[]{:S(2)}, u32[]{:S(2)}) collective-permute-start(bf16[256,768]{0,1:T(8,128)(2,1)S(1)} %bitcast.256), channel_id=1, source_target_pairs={{4,0},{5,1},{6,2},{7,3},{12,8},{13,9},{14,10},{15,11},{20,16},{21,... | collective-permute-start | bytes 1179656 | tf_op jit(solution)/shard_map/ppermute | solution.py:18
  19.4 14.0 %copy-start.44 = (s32[2,8]{1,0:T(2,128)S(1)}, s32[2,8]{1,0:T(2,128)}, u32[]{:S(2)}) copy-start(s32[2,8]{1,0:T(2,128)} %param.19) | copy-start | bytes 196
  29.6 5.2 %all-to-all-start = ((bf16[2,2,49152]{2,1,0:T(2,128)(2,1)}), bf16[2,2,49152]{2,1,0:T(2,128)(2,1)S(1)}, u32[]{:S(2)}, u32[]{:S(2)}) async-start(bf16[2,2,49152]{2,1,0:T(2,128)(2,1)} %reshape.450), calls=%async_computation | async-start | bytes 786432 | tf_op jit(solution)/shard_map/all_to_all | solution.py:176
  73.0 10.0 %copy-start.33 = (bf16[256,3,128]{2,0,1:T(8,128)(2,1)S(1)}, bf16[256,3,128]{2,0,1:T(8,128)(2,1)}, u32[]{:S(2)}) copy-start(bf16[256,3,128]{2,0,1:T(8,128)(2,1)} %get-tuple-element.502) | copy-start | bytes 589828
  73.9 9.2 %copy-start.32 = (bf16[256,3,128]{2,0,1:T(8,128)(2,1)S(1)}, bf16[256,3,128]{2,0,1:T(8,128)(2,1)}, u32[]{:S(2)}) copy-start(bf16[256,3,128]{2,0,1:T(8,128)(2,1)} %get-tuple-element.503) | copy-start | bytes 589828
  73.9 9.4 %copy-start.31 = (bf16[256,3,128]{2,0,1:T(8,128)(2,1)S(1)}, bf16[256,3,128]{2,0,1:T(8,128)(2,1)}, u32[]{:S(2)}) copy-start(bf16[256,3,128]{2,0,1:T(8,128)(2,1)} %get-tuple-element.504) | copy-start | bytes 589828
  75.1 20.9 %collective-permute-start.8 = (bf16[256,384]{0,1:T(8,128)(2,1)S(1)}, bf16[256,384]{0,1:T(8,128)(2,1)S(1)}, u32[]{:S(2)}, u32[]{:S(2)}) collective-permute-start(bf16[256,384]{0,1:T(8,128)(2,1)S(1)} %bitcast.269), channel_id=1, source_target_pairs={{0,5},{1,6},{2,7},{8,13},{9,14},{10,15},{16,21},{17,22},{18,23},{2... | collective-permute-start | bytes 589832 | tf_op jit(solution)/shard_map/ppermute | solution.py:18
  76.4 15.5 %copy-start.30 = (bf16[256,3,128]{2,0,1:T(8,128)(2,1)S(1)}, bf16[256,3,128]{2,0,1:T(8,128)(2,1)}, u32[]{:S(2)}) copy-start(bf16[256,3,128]{2,0,1:T(8,128)(2,1)} %get-tuple-element.508) | copy-start | bytes 589828
  76.4 16.3 %copy-start.29 = (bf16[256,3,128]{2,0,1:T(8,128)(2,1)S(1)}, bf16[256,3,128]{2,0,1:T(8,128)(2,1)}, u32[]{:S(2)}) copy-start(bf16[256,3,128]{2,0,1:T(8,128)(2,1)} %get-tuple-element.505) | copy-start | bytes 589828
  77.3 16.2 %copy-start.35 = (bf16[256,3,128]{2,0,1:T(8,128)(2,1)S(1)}, bf16[256,3,128]{2,0,1:T(8,128)(2,1)}, u32[]{:S(2)}) copy-start(bf16[256,3,128]{2,0,1:T(8,128)(2,1)} %get-tuple-element.497) | copy-start | bytes 589828
  77.3 189.0 %collective-permute-start.18 = (bf16[3,256,384]{1,2,0:T(8,128)(2,1)}, bf16[3,256,384]{1,2,0:T(8,128)(2,1)}, u32[]{:S(2)}, u32[]{:S(2)}) collective-permute-start(bf16[3,256,384]{1,2,0:T(8,128)(2,1)} %pad_maximum_fusion.3), channel_id=1, source_target_pairs={{0,8},{1,9},{2,10},{3,11},{4,12},{5,13},{6,14},{7,15},{16,24},{17,... | collective-permute-start | bytes 1769480 | tf_op jit(solution)/shard_map/ppermute | solution.py:18
  81.7 187.2 %collective-permute-start.19 = (bf16[3,256,384]{1,2,0:T(8,128)(2,1)}, bf16[3,256,384]{1,2,0:T(8,128)(2,1)}, u32[]{:S(2)}, u32[]{:S(2)}) collective-permute-start(bf16[3,256,384]{1,2,0:T(8,128)(2,1)} %pad_maximum_fusion.3), channel_id=1, source_target_pairs={{8,0},{9,1},{10,2},{11,3},{12,4},{13,5},{14,6},{15,7},{24,16},{25,... | collective-permute-start | bytes 1769480 | tf_op jit(solution)/shard_map/ppermute | solution.py:18
  83.0 10.7 %copy-start.34 = (bf16[256,3,128]{2,0,1:T(8,128)(2,1)S(1)}, bf16[256,3,128]{2,0,1:T(8,128)(2,1)}, u32[]{:S(2)}) copy-start(bf16[256,3,128]{2,0,1:T(8,128)(2,1)} %get-tuple-element.491) | copy-start | bytes 589828
  83.1 10.7 %copy-start.25 = (bf16[256,3,128]{0,2,1:T(8,128)(2,1)}, bf16[256,3,128]{0,2,1:T(8,128)(2,1)S(1)}, u32[]{:S(2)}) copy-start(bf16[256,3,128]{0,2,1:T(8,128)(2,1)S(1)} %copy.174) | copy-start | bytes 589828
  83.3 10.7 %copy-start.23 = (bf16[256,3,128]{0,2,1:T(8,128)(2,1)}, bf16[256,3,128]{0,2,1:T(8,128)(2,1)S(1)}, u32[]{:S(2)}) copy-start(bf16[256,3,128]{0,2,1:T(8,128)(2,1)S(1)} %copy.176) | copy-start | bytes 589828
  83.5 10.7 %copy-start.21 = (bf16[256,3,128]{0,2,1:T(8,128)(2,1)}, bf16[256,3,128]{0,2,1:T(8,128)(2,1)S(1)}, u32[]{:S(2)}) copy-start(bf16[256,3,128]{0,2,1:T(8,128)(2,1)S(1)} %copy.178) | copy-start | bytes 589828
  84.4 183.1 %collective-permute-start.16 = (bf16[3,256,384]{1,2,0:T(8,128)(2,1)}, bf16[3,256,384]{1,2,0:T(8,128)(2,1)}, u32[]{:S(2)}, u32[]{:S(2)}) collective-permute-start(bf16[3,256,384]{1,2,0:T(8,128)(2,1)} %pad_maximum_fusion.2), channel_id=1, source_target_pairs={{0,8},{1,9},{2,10},{3,11},{4,12},{5,13},{6,14},{7,15},{16,24},{17,... | collective-permute-start | bytes 1769480 | tf_op jit(solution)/shard_map/ppermute | solution.py:18
  90.6 179.4 %collective-permute-start.17 = (bf16[3,256,384]{1,2,0:T(8,128)(2,1)}, bf16[3,256,384]{1,2,0:T(8,128)(2,1)}, u32[]{:S(2)}, u32[]{:S(2)}) collective-permute-start(bf16[3,256,384]{1,2,0:T(8,128)(2,1)} %pad_maximum_fusion.2), channel_id=1, source_target_pairs={{8,0},{9,1},{10,2},{11,3},{12,4},{13,5},{14,6},{15,7},{24,16},{25,... | collective-permute-start | bytes 1769480 | tf_op jit(solution)/shard_map/ppermute | solution.py:18
  96.0 10.6 %collective-permute-start = (bf16[256,384]{0,1:T(8,128)(2,1)S(1)}, bf16[256,384]{0,1:T(8,128)(2,1)S(1)}, u32[]{:S(2)}, u32[]{:S(2)}) collective-permute-start(bf16[256,384]{0,1:T(8,128)(2,1)S(1)} %bitcast.276), channel_id=1, source_target_pairs={{0,5},{1,6},{2,7},{8,13},{9,14},{10,15},{16,21},{17,22},{18,23},{2... | collective-permute-start | bytes 589832 | tf_op jit(solution)/shard_map/ppermute | solution.py:18
  106.6 9.3 %collective-permute-start.10 = (bf16[256,384]{0,1:T(8,128)(2,1)S(1)}, bf16[256,384]{0,1:T(8,128)(2,1)S(1)}, u32[]{:S(2)}, u32[]{:S(2)}) collective-permute-start(bf16[256,384]{0,1:T(8,128)(2,1)S(1)} %bitcast.270), channel_id=1, source_target_pairs={{0,3},{1,4},{2,5},{3,6},{4,7},{8,11},{9,12},{10,13},{11,14},{12,15... | collective-permute-start | bytes 589832 | tf_op jit(solution)/shard_map/ppermute | solution.py:18
  115.9 10.3 %collective-permute-start.11 = (bf16[256,384]{0,1:T(8,128)(2,1)S(1)}, bf16[256,384]{0,1:T(8,128)(2,1)S(1)}, u32[]{:S(2)}, u32[]{:S(2)}) collective-permute-start(bf16[256,384]{0,1:T(8,128)(2,1)S(1)} %bitcast.271), channel_id=1, source_target_pairs={{0,1},{1,2},{2,3},{3,4},{4,5},{5,6},{6,7},{8,9},{9,10},{10,11},{11... | collective-permute-start | bytes 589832 | tf_op jit(solution)/shard_map/ppermute | solution.py:18
  126.3 13.0 %collective-permute-start.2 = (bf16[256,384]{0,1:T(8,128)(2,1)S(1)}, bf16[256,384]{0,1:T(8,128)(2,1)S(1)}, u32[]{:S(2)}, u32[]{:S(2)}) collective-permute-start(bf16[256,384]{0,1:T(8,128)(2,1)S(1)} %bitcast.277), channel_id=1, source_target_pairs={{0,3},{1,4},{2,5},{3,6},{4,7},{8,11},{9,12},{10,13},{11,14},{12,15... | collective-permute-start | bytes 589832 | tf_op jit(solution)/shard_map/ppermute | solution.py:18
  139.2 8.6 %collective-permute-start.3 = (bf16[256,384]{0,1:T(8,128)(2,1)S(1)}, bf16[256,384]{0,1:T(8,128)(2,1)S(1)}, u32[]{:S(2)}, u32[]{:S(2)}) collective-permute-start(bf16[256,384]{0,1:T(8,128)(2,1)S(1)} %bitcast.278), channel_id=1, source_target_pairs={{0,1},{1,2},{2,3},{3,4},{4,5},{5,6},{6,7},{8,9},{9,10},{10,11},{11... | collective-permute-start | bytes 589832 | tf_op jit(solution)/shard_map/ppermute | solution.py:18
  147.9 7.6 %collective-permute-start.12 = (bf16[256,384]{0,1:T(8,128)(2,1)S(1)}, bf16[256,384]{0,1:T(8,128)(2,1)S(1)}, u32[]{:S(2)}, u32[]{:S(2)}) collective-permute-start(bf16[256,384]{0,1:T(8,128)(2,1)S(1)} %bitcast.272), channel_id=1, source_target_pairs={{1,0},{2,1},{3,2},{4,3},{5,4},{6,5},{7,6},{9,8},{10,9},{11,10},{12... | collective-permute-start | bytes 589832 | tf_op jit(solution)/shard_map/ppermute | solution.py:18
  155.4 5.2 %collective-permute-start.13 = (bf16[256,384]{0,1:T(8,128)(2,1)S(1)}, bf16[256,384]{0,1:T(8,128)(2,1)S(1)}, u32[]{:S(2)}, u32[]{:S(2)}) collective-permute-start(bf16[256,384]{0,1:T(8,128)(2,1)S(1)} %bitcast.274), channel_id=1, source_target_pairs={{3,0},{4,1},{5,2},{6,3},{7,4},{11,8},{12,9},{13,10},{14,11},{15,12... | collective-permute-start | bytes 589832 | tf_op jit(solution)/shard_map/ppermute | solution.py:18
  160.6 7.6 %collective-permute-start.4 = (bf16[256,384]{0,1:T(8,128)(2,1)S(1)}, bf16[256,384]{0,1:T(8,128)(2,1)S(1)}, u32[]{:S(2)}, u32[]{:S(2)}) collective-permute-start(bf16[256,384]{0,1:T(8,128)(2,1)S(1)} %bitcast.280), channel_id=1, source_target_pairs={{1,0},{2,1},{3,2},{4,3},{5,4},{6,5},{7,6},{9,8},{10,9},{11,10},{12... | collective-permute-start | bytes 589832 | tf_op jit(solution)/shard_map/ppermute | solution.py:18
  168.2 16.0 %collective-permute-start.5 = (bf16[256,384]{0,1:T(8,128)(2,1)S(1)}, bf16[256,384]{0,1:T(8,128)(2,1)S(1)}, u32[]{:S(2)}, u32[]{:S(2)}) collective-permute-start(bf16[256,384]{0,1:T(8,128)(2,1)S(1)} %bitcast.281), channel_id=1, source_target_pairs={{3,0},{4,1},{5,2},{6,3},{7,4},{11,8},{12,9},{13,10},{14,11},{15,12... | collective-permute-start | bytes 589832 | tf_op jit(solution)/shard_map/ppermute | solution.py:18
  184.2 5.2 %collective-permute-start.15 = (bf16[256,384]{0,1:T(8,128)(2,1)S(1)}, bf16[256,384]{0,1:T(8,128)(2,1)S(1)}, u32[]{:S(2)}, u32[]{:S(2)}) collective-permute-start(bf16[256,384]{0,1:T(8,128)(2,1)S(1)} %bitcast.275), channel_id=1, source_target_pairs={{5,0},{6,1},{7,2},{13,8},{14,9},{15,10},{21,16},{22,17},{23,18},{2... | collective-permute-start | bytes 589832 | tf_op jit(solution)/shard_map/ppermute | solution.py:18
  189.3 10.2 %collective-permute-start.7 = (bf16[256,384]{0,1:T(8,128)(2,1)S(1)}, bf16[256,384]{0,1:T(8,128)(2,1)S(1)}, u32[]{:S(2)}, u32[]{:S(2)}) collective-permute-start(bf16[256,384]{0,1:T(8,128)(2,1)S(1)} %bitcast.282), channel_id=1, source_target_pairs={{5,0},{6,1},{7,2},{13,8},{14,9},{15,10},{21,16},{22,17},{23,18},{2... | collective-permute-start | bytes 589832 | tf_op jit(solution)/shard_map/ppermute | solution.py:18
  334.6 9.3 %copy-start.11 = (bf16[9,256,384]{1,2,0:T(8,128)(2,1)S(1)}, bf16[9,256,384]{1,2,0:T(8,128)(2,1)}, u32[]{:S(2)}) copy-start(bf16[9,256,384]{1,2,0:T(8,128)(2,1)} %convert.52) | copy-start | bytes 5308420
  336.9 22.2 %copy-start.7 = (f32[9,256,384]{1,2,0:T(8,128)S(1)}, f32[9,256,384]{1,2,0:T(8,128)}, u32[]{:S(2)}) copy-start(f32[9,256,384]{1,2,0:T(8,128)} %get-tuple-element.325) | copy-start | bytes 10616836
  337.0 24.9 %collective-permute-start.21 = (bf16[3,256,384]{1,2,0:T(8,128)(2,1)S(1)}, bf16[3,256,384]{1,2,0:T(8,128)(2,1)S(1)}, u32[]{:S(2)}, u32[]{:S(2)}) collective-permute-start(bf16[3,256,384]{1,2,0:T(8,128)(2,1)S(1)} %get-tuple-element.464), channel_id=1, source_target_pairs={{8,0},{9,1},{10,2},{11,3},{12,4},{13,5},{14,6},{15,7},{24,16},{25,... | collective-permute-start | bytes 1769480 | tf_op jit(solution)/shard_map/ppermute | solution.py:18
  338.7 24.5 %collective-permute-start.22 = (bf16[3,256,384]{1,2,0:T(8,128)(2,1)S(1)}, bf16[3,256,384]{1,2,0:T(8,128)(2,1)S(1)}, u32[]{:S(2)}, u32[]{:S(2)}) collective-permute-start(bf16[3,256,384]{1,2,0:T(8,128)(2,1)S(1)} %get-tuple-element.465), channel_id=1, source_target_pairs={{0,8},{1,9},{2,10},{3,11},{4,12},{5,13},{6,14},{7,15},{16,24},{17,... | collective-permute-start | bytes 1769480 | tf_op jit(solution)/shard_map/ppermute | solution.py:18
  344.8 35.2 %collective-permute-start.20 = (bf16[256,384]{0,1:T(8,128)(2,1)S(1)}, bf16[256,384]{0,1:T(8,128)(2,1)S(1)}, u32[]{:S(2)}, u32[]{:S(2)}) collective-permute-start(bf16[256,384]{0,1:T(8,128)(2,1)S(1)} %get-tuple-element.456), channel_id=1, source_target_pairs={{5,0},{6,1},{7,2},{13,8},{14,9},{15,10},{21,16},{22,17},{23,18},{2... | collective-permute-start | bytes 589832 | tf_op jit(solution)/shard_map/ppermute | solution.py:18
  351.8 31.2 %collective-permute-start.24 = (bf16[256,384]{0,1:T(8,128)(2,1)S(1)}, bf16[256,384]{0,1:T(8,128)(2,1)S(1)}, u32[]{:S(2)}, u32[]{:S(2)}) collective-permute-start(bf16[256,384]{0,1:T(8,128)(2,1)S(1)} %get-tuple-element.462), channel_id=1, source_target_pairs={{3,0},{4,1},{5,2},{6,3},{7,4},{11,8},{12,9},{13,10},{14,11},{15,12... | collective-permute-start | bytes 589832 | tf_op jit(solution)/shard_map/ppermute | solution.py:18
  353.1 36.9 %collective-permute-start.25 = (bf16[256,384]{0,1:T(8,128)(2,1)S(1)}, bf16[256,384]{0,1:T(8,128)(2,1)S(1)}, u32[]{:S(2)}, u32[]{:S(2)}) collective-permute-start(bf16[256,384]{0,1:T(8,128)(2,1)S(1)} %get-tuple-element.461), channel_id=1, source_target_pairs={{1,0},{2,1},{3,2},{4,3},{5,4},{6,5},{7,6},{9,8},{10,9},{11,10},{12... | collective-permute-start | bytes 589832 | tf_op jit(solution)/shard_map/ppermute | solution.py:18
  361.9 11.8 %collective-permute-start.31 = (bf16[3,256,384]{1,2,0:T(8,128)(2,1)S(1)}, bf16[3,256,384]{1,2,0:T(8,128)(2,1)S(1)}, u32[]{:S(2)}, u32[]{:S(2)}) collective-permute-start(bf16[3,256,384]{1,2,0:T(8,128)(2,1)S(1)} %get-tuple-element.454), channel_id=1, source_target_pairs={{8,0},{9,1},{10,2},{11,3},{12,4},{13,5},{14,6},{15,7},{24,16},{25,... | collective-permute-start | bytes 1769480 | tf_op jit(solution)/shard_map/ppermute | solution.py:18
  363.2 12.5 %collective-permute-start.32 = (bf16[3,256,384]{1,2,0:T(8,128)(2,1)S(1)}, bf16[3,256,384]{1,2,0:T(8,128)(2,1)S(1)}, u32[]{:S(2)}, u32[]{:S(2)}) collective-permute-start(bf16[3,256,384]{1,2,0:T(8,128)(2,1)S(1)} %get-tuple-element.455), channel_id=1, source_target_pairs={{0,8},{1,9},{2,10},{3,11},{4,12},{5,13},{6,14},{7,15},{16,24},{17,... | collective-permute-start | bytes 1769480 | tf_op jit(solution)/shard_map/ppermute | solution.py:18
  373.7 26.0 %collective-permute-start.23 = (bf16[256,768]{0,1:T(8,128)(2,1)}, bf16[256,768]{0,1:T(8,128)(2,1)}, u32[]{:S(2)}, u32[]{:S(2)}) collective-permute-start(bf16[256,768]{0,1:T(8,128)(2,1)} %pad_maximum_fusion.5), channel_id=1, source_target_pairs={{4,0},{5,1},{6,2},{7,3},{12,8},{13,9},{14,10},{15,11},{20,16},{21,... | collective-permute-start | bytes 1179656 | tf_op jit(solution)/shard_map/ppermute | solution.py:18
  375.7 29.8 %collective-permute-start.28 = (bf16[256,768]{0,1:T(8,128)(2,1)}, bf16[256,768]{0,1:T(8,128)(2,1)}, u32[]{:S(2)}, u32[]{:S(2)}) collective-permute-start(bf16[256,768]{0,1:T(8,128)(2,1)} %pad_maximum_fusion.6), channel_id=1, source_target_pairs={{0,4},{1,5},{2,6},{3,7},{8,12},{9,13},{10,14},{11,15},{16,20},{17,... | collective-permute-start | bytes 1179656 | tf_op jit(solution)/shard_map/ppermute | solution.py:18
  378.3 13.0 %copy-start.51 = (s32[6]{0:T(128)S(1)}, s32[6]{0:T(128)}, u32[]{:S(2)}) copy-start(s32[6]{0:T(128)} %compare_select_fusion.2) | copy-start | bytes 76
  378.3 13.0 %copy-start.27 = (bf16[256,384]{0,1:T(8,128)(2,1)S(1)}, bf16[256,384]{0,1:T(8,128)(2,1)}, u32[]{:S(2)}) copy-start(bf16[256,384]{0,1:T(8,128)(2,1)} %get-tuple-element.322) | copy-start | bytes 589828
  378.3 13.1 %copy-start.28 = (bf16[256,384]{0,1:T(8,128)(2,1)S(1)}, bf16[256,384]{0,1:T(8,128)(2,1)}, u32[]{:S(2)}) copy-start(bf16[256,384]{0,1:T(8,128)(2,1)} %get-tuple-element.321) | copy-start | bytes 589828
  380.0 42.8 %copy-start.48 = (pred[768]{0:T(1024)(128)(4,1)S(1)}, pred[768]{0:T(1024)(128)(4,1)}, u32[]{:S(2)}) copy-start(pred[768]{0:T(1024)(128)(4,1)} %broadcast_bitcast_fusion) | copy-start | bytes 2308
  380.0 12.2 %copy-start.38 = (bf16[256,384]{0,1:T(8,128)(2,1)}, bf16[256,384]{0,1:T(8,128)(2,1)S(1)}, u32[]{:S(2)}) copy-start(bf16[256,384]{0,1:T(8,128)(2,1)S(1)} %collective-permute-done.20) | copy-start | bytes 589828
  380.0 18.4 %collective-permute-start.26 = (bf16[256,384]{0,1:T(8,128)(2,1)}, bf16[256,384]{0,1:T(8,128)(2,1)}, u32[]{:S(2)}, u32[]{:S(2)}) collective-permute-start(bf16[256,384]{0,1:T(8,128)(2,1)} %get-tuple-element.460), channel_id=1, source_target_pairs={{0,1},{1,2},{2,3},{3,4},{4,5},{5,6},{6,7},{8,9},{9,10},{10,11},{11... | collective-permute-start | bytes 589832 | tf_op jit(solution)/shard_map/ppermute | solution.py:18
  383.1 9.1 %copy-start.40 = (bf16[256,384]{0,1:T(8,128)(2,1)}, bf16[256,384]{0,1:T(8,128)(2,1)S(1)}, u32[]{:S(2)}) copy-start(bf16[256,384]{0,1:T(8,128)(2,1)S(1)} %collective-permute-done.24) | copy-start | bytes 589828
  383.1 54.2 %collective-permute-start.33 = (bf16[256,768]{0,1:T(8,128)(2,1)}, bf16[256,768]{0,1:T(8,128)(2,1)}, u32[]{:S(2)}, u32[]{:S(2)}) collective-permute-start(bf16[256,768]{0,1:T(8,128)(2,1)} %pad_maximum_fusion.7), channel_id=1, source_target_pairs={{4,0},{5,1},{6,2},{7,3},{12,8},{13,9},{14,10},{15,11},{20,16},{21,... | collective-permute-start | bytes 1179656 | tf_op jit(solution)/shard_map/ppermute | solution.py:18
  390.1 48.6 %collective-permute-start.38 = (bf16[256,768]{0,1:T(8,128)(2,1)}, bf16[256,768]{0,1:T(8,128)(2,1)}, u32[]{:S(2)}, u32[]{:S(2)}) collective-permute-start(bf16[256,768]{0,1:T(8,128)(2,1)} %pad_maximum_fusion.8), channel_id=1, source_target_pairs={{0,4},{1,5},{2,6},{3,7},{8,12},{9,13},{10,14},{11,15},{16,20},{17,... | collective-permute-start | bytes 1179656 | tf_op jit(solution)/shard_map/ppermute | solution.py:18
  398.3 30.5 %collective-permute-start.27 = (bf16[256,384]{0,1:T(8,128)(2,1)}, bf16[256,384]{0,1:T(8,128)(2,1)}, u32[]{:S(2)}, u32[]{:S(2)}) collective-permute-start(bf16[256,384]{0,1:T(8,128)(2,1)} %get-tuple-element.459), channel_id=1, source_target_pairs={{0,3},{1,4},{2,5},{3,6},{4,7},{8,11},{9,12},{10,13},{11,14},{12,15... | collective-permute-start | bytes 589832 | tf_op jit(solution)/shard_map/ppermute | solution.py:18
  399.6 31.1 %collective-permute-start.29 = (bf16[256,384]{0,1:T(8,128)(2,1)}, bf16[256,384]{0,1:T(8,128)(2,1)}, u32[]{:S(2)}, u32[]{:S(2)}) collective-permute-start(bf16[256,384]{0,1:T(8,128)(2,1)} %get-tuple-element.457), channel_id=1, source_target_pairs={{0,5},{1,6},{2,7},{8,13},{9,14},{10,15},{16,21},{17,22},{18,23},{2... | collective-permute-start | bytes 589832 | tf_op jit(solution)/shard_map/ppermute | solution.py:18
  405.5 27.2 %collective-permute-start.30 = (bf16[256,384]{0,1:T(8,128)(2,1)}, bf16[256,384]{0,1:T(8,128)(2,1)}, u32[]{:S(2)}, u32[]{:S(2)}) collective-permute-start(bf16[256,384]{0,1:T(8,128)(2,1)} %get-tuple-element.446), channel_id=1, source_target_pairs={{5,0},{6,1},{7,2},{13,8},{14,9},{15,10},{21,16},{22,17},{23,18},{2... | collective-permute-start | bytes 589832 | tf_op jit(solution)/shard_map/ppermute | solution.py:18
  426.6 13.3 %copy-start.39 = (bf16[256,384]{0,1:T(8,128)(2,1)S(1)}, bf16[256,384]{0,1:T(8,128)(2,1)}, u32[]{:S(2)}) copy-start(bf16[256,384]{0,1:T(8,128)(2,1)} %copy-done.38) | copy-start | bytes 589828
  426.6 13.3 %copy-start.41 = (bf16[256,384]{0,1:T(8,128)(2,1)S(1)}, bf16[256,384]{0,1:T(8,128)(2,1)}, u32[]{:S(2)}) copy-start(bf16[256,384]{0,1:T(8,128)(2,1)} %copy-done.40) | copy-start | bytes 589828
  426.6 13.3 %copy-start.43 = (bf16[256,384]{0,1:T(8,128)(2,1)S(1)}, bf16[256,384]{0,1:T(8,128)(2,1)}, u32[]{:S(2)}) copy-start(bf16[256,384]{0,1:T(8,128)(2,1)} %copy-done.42) | copy-start | bytes 589828
  428.8 19.9 %collective-permute-start.34 = (bf16[256,384]{0,1:T(8,128)(2,1)}, bf16[256,384]{0,1:T(8,128)(2,1)}, u32[]{:S(2)}, u32[]{:S(2)}) collective-permute-start(bf16[256,384]{0,1:T(8,128)(2,1)} %get-tuple-element.452), channel_id=1, source_target_pairs={{3,0},{4,1},{5,2},{6,3},{7,4},{11,8},{12,9},{13,10},{14,11},{15,12... | collective-permute-start | bytes 589832 | tf_op jit(solution)/shard_map/ppermute | solution.py:18
  430.8 18.0 %collective-permute-start.35 = (bf16[256,384]{0,1:T(8,128)(2,1)}, bf16[256,384]{0,1:T(8,128)(2,1)}, u32[]{:S(2)}, u32[]{:S(2)}) collective-permute-start(bf16[256,384]{0,1:T(8,128)(2,1)} %get-tuple-element.451), channel_id=1, source_target_pairs={{1,0},{2,1},{3,2},{4,3},{5,4},{6,5},{7,6},{9,8},{10,9},{11,10},{12... | collective-permute-start | bytes 589832 | tf_op jit(solution)/shard_map/ppermute | solution.py:18
  432.7 16.0 %collective-permute-start.36 = (bf16[256,384]{0,1:T(8,128)(2,1)}, bf16[256,384]{0,1:T(8,128)(2,1)}, u32[]{:S(2)}, u32[]{:S(2)}) collective-permute-start(bf16[256,384]{0,1:T(8,128)(2,1)} %get-tuple-element.450), channel_id=1, source_target_pairs={{0,1},{1,2},{2,3},{3,4},{4,5},{5,6},{6,7},{8,9},{9,10},{10,11},{11... | collective-permute-start | bytes 589832 | tf_op jit(solution)/shard_map/ppermute | solution.py:18
  437.3 11.5 %collective-permute-start.37 = (bf16[256,384]{0,1:T(8,128)(2,1)}, bf16[256,384]{0,1:T(8,128)(2,1)}, u32[]{:S(2)}, u32[]{:S(2)}) collective-permute-start(bf16[256,384]{0,1:T(8,128)(2,1)} %get-tuple-element.449), channel_id=1, source_target_pairs={{0,3},{1,4},{2,5},{3,6},{4,7},{8,11},{9,12},{10,13},{11,14},{12,15... | collective-permute-start | bytes 589832 | tf_op jit(solution)/shard_map/ppermute | solution.py:18
  438.6 10.6 %collective-permute-start.39 = (bf16[256,384]{0,1:T(8,128)(2,1)}, bf16[256,384]{0,1:T(8,128)(2,1)}, u32[]{:S(2)}, u32[]{:S(2)}) collective-permute-start(bf16[256,384]{0,1:T(8,128)(2,1)} %get-tuple-element.447), channel_id=1, source_target_pairs={{0,5},{1,6},{2,7},{8,13},{9,14},{10,15},{16,21},{17,22},{18,23},{2... | collective-permute-start | bytes 589832 | tf_op jit(solution)/shard_map/ppermute | solution.py:18
  (49 other events, 101.2 us)
where the time goes:
time: 463 us; the launch traced here: 454 us
  starting transfers between devices  145 us (31%)
  local copies, waits for them, and re-layouts  131 us (28%)
  waiting for transfers between devices  65.7 us (14%)
  matrix products  50.7 us (11%)
  other arithmetic  49.5 us (11%)
  between operations  12 us (3%)
    ppermute x40, starting transfers between devices, from_behind(): return lax.ppermute(block, axis, route)  141 us
    ppermute x40, waiting for transfers between devices, from_behind(): return lax.ppermute(block, axis, route)  65.7 us
    unnamed x135, local copies, waits for them, and re-layouts  22.6 us
    dynamic_update_slice x12, local copies, waits for them, and re-layouts, one_head(): lax.dynamic_update_slice_in_dim(value_parts, value_part.reshape(window, t...  20.4 us
    dynamic_update_slice x6, local copies, waits for them, and re-layouts, one_head(): lax.dynamic_update_slice_in_dim(key_parts, key_part.reshape(window, tile_...  16.1 us
    dot_general x6, matrix products, one_head(): jnp.einsum('iw,ie->we', softmax_low, grad_head, preferred_element_type=jn...  15.2 us
    dot_general x6, matrix products, one_head(): jnp.einsum('iw,ie->we', grad_scores, query_head, preferred_element_type=j...  14.5 us
    dynamic_slice x24, local copies, waits for them, and re-layouts, head_columns(): lax.dynamic_slice_in_dim(values, head_at * head_dim, head_dim, values.ndi...  10.5 us
  transfers between devices with their start and end apart: 41, of which 14 were waited for; matrix products, arithmetic and copies ran while one was open for 32% of the time, Pallas kernels for 0%

commit v1 on v0

v1 whole, which is shorter than its diff:
```python
import functools
import math

import jax
import jax.numpy as jnp
from jax import lax
from jax.experimental import pallas as pl
from jax.experimental.pallas import tpu as pltpu
from jax.sharding import PartitionSpec as P

NCT = 4
LOG2E = 1.4426950408889634
DEAD = -1e30
VMEM_LIMIT = 48 * 1024 * 1024

SMEM = pl.BlockSpec(memory_space=pltpu.SMEM)
NT = (((1,), (1,)), ((), ()))
NN = (((1,), (0,)), ((), ()))
TN = (((0,), (0,)), ((), ()))


def dot(a, b, dims):
    return lax.dot_general(a, b, dims, preferred_element_type=jnp.float32)


def steps_along(size):
    if size == 1:
        return []
    if size == 2:
        return [[1, 0]]
    return [
        [p - 1 if p > 0 else None for p in range(size)],
        [p + 1 if p + 1 < size else None for p in range(size)],
    ]


def row_route(step, col_count):
    return [
        (source * col_count + col, row * col_count + col)
        for row, source in enumerate(step)
        if source is not None
        for col in range(col_count)
    ]


def col_route(step, row_count):
    col_count = len(step)
    return [
        (row * col_count + source, row * col_count + col)
        for col, source in enumerate(step)
        if source is not None
        for row in range(row_count)
    ]


def frame_route(step):
    return [(source, frame) for frame, source in enumerate(step) if source is not None]


def reverse(route):
    return [(b, a) for a, b in route]


def source_of(step, place):
    if len(step) == 2:
        return 1 - place, True
    if step[0] is None:
        return jnp.maximum(place - 1, 0), place > 0
    return jnp.minimum(place + 1, len(step) - 1), place + 1 < len(step)


def slot_counts(counts_ref, frame_steps, col_steps, col_count):
    frame = lax.axis_index("frame")
    spot = lax.axis_index("tile")
    row = lax.div(spot, col_count)
    col = lax.rem(spot, col_count)
    own = counts_ref[frame, spot]
    plane, across = [own], [own]
    for step in col_steps:
        source, there = source_of(step, col)
        plane.append(jnp.where(there, counts_ref[frame, row * col_count + source], 0))
    for step in frame_steps:
        source, there = source_of(step, frame)
        across.append(jnp.where(there, counts_ref[source, spot], 0))
    return plane, across


def pair_flip(offsets_ref, pair):
    hits = jnp.int32(0)
    for slot in range(offsets_ref.shape[1]):
        hits = hits | jnp.abs(offsets_ref[2 * pair, slot, 0])
    return jnp.where(hits != 0, 1, 0).astype(jnp.int32)


def pack_kernel(pairs, hd, offsets_ref, k_ref, v_ref, plane_ref, across_ref):
    for pair in range(pairs):
        flip = pair_flip(offsets_ref, pair)
        first = pl.ds(pl.multiple_of(2 * pair * hd + flip * hd, hd), hd)
        second = pl.ds(pl.multiple_of(2 * pair * hd + (1 - flip) * hd, hd), hd)
        at = pl.ds(pair * hd, hd)
        for i, ref in enumerate((k_ref, v_ref)):
            plane_ref[i, :, at] = ref[:, first]
            across_ref[i, :, at] = ref[:, second]


def gather_kernel(sections, pairs, counts_ref, grad_ref, *refs):
    got_refs, out_refs = refs[: sections - 1], refs[sections - 1 :]
    section = lax.axis_index("section")
    count = counts_ref[lax.axis_index("frame"), lax.axis_index("tile")]
    rows, width = got_refs[0].shape if got_refs else grad_ref.shape
    pair_width = width // pairs
    at_rows = lax.broadcasted_iota(jnp.int32, (rows, 1), 0)
    for k in range(sections):
        holder = lax.rem(section + sections - k, sections)
        live = at_rows + holder * rows < count
        start = pl.multiple_of(holder * rows, rows)
        for pair in range(pairs):
            if k == 0:
                at = pl.multiple_of(section * width + pair * pair_width, pair_width)
                part = grad_ref[:, pl.ds(at, pair_width)]
            else:
                part = got_refs[k - 1][:, pl.ds(pair * pair_width, pair_width)]
            part = jnp.where(live, part.astype(jnp.float32), 0.0).astype(part.dtype)
            out_refs[pair][pl.ds(start, rows), :] = part


class Window:
    def __init__(self, plan, refs):
        refs = list(refs)
        self.plan = plan
        take = lambda n: [refs.pop(0) for _ in range(n)]
        self.offsets, self.counts = take(2)
        self.q = take(1 + plan.nr)
        self.grad = take(1 + plan.nr)
        self.k, self.v = take(2)
        self.near_plane = take(plan.nc)
        self.near_across = take(plan.nf)
        self.rest = refs

    def heads(self):
        plan = self.plan
        hd = plan.hd
        flip = pair_flip(self.offsets, plan.pair)
        plane_counts, across_counts = slot_counts(
            self.counts, plan.frame_steps, plan.col_steps, plan.col_count
        )
        for kind, near, live in (
            (0, self.near_plane, plane_counts),
            (1, self.near_across, across_counts),
        ):
            at = flip if kind == 0 else 1 - flip
            cols = pl.ds(pl.multiple_of(at * hd, hd), hd)
            q = jnp.concatenate([ref[:, cols] for ref in self.q], axis=0)
            grad = jnp.concatenate([ref[:, cols] for ref in self.grad], axis=0)
            slots = [(self.k[:, cols], self.v[:, cols])]
            slots += [(ref[0], ref[1]) for ref in near]
            yield kind, cols, q, grad, list(zip(slots, live))


def masked_scores(key, q, count, factor):
    scores = dot(key, q, NT) * factor
    live = lax.broadcasted_iota(jnp.int32, (key.shape[0], 1), 0) < count
    return jnp.where(live, scores, DEAD)


def merge(parts):
    top = functools.reduce(jnp.maximum, [m for m, _, _ in parts])
    weights = [jnp.exp2(m - top) for m, _, _ in parts]
    total = sum(w * l for w, (_, l, _) in zip(weights, parts))
    cross = sum(w * t for w, (_, _, t) in zip(weights, parts))
    return top, total, cross


def stats_kernel(plan, *refs):
    window = Window(plan, refs)
    (out_ref,) = window.rest
    rows = []
    for kind, cols, q, grad, slots in window.heads():
        parts = []
        for (key, value), count in slots:
            scores = masked_scores(key, q, count, plan.factor)
            top = jnp.max(scores, axis=0, keepdims=True)
            weight = jnp.exp2(scores - top)
            total = jnp.sum(weight, axis=0, keepdims=True)
            cross = jnp.sum(weight * dot(value, grad, NT), axis=0, keepdims=True)
            parts.append((top, total, cross))
        rows += list(merge(parts))
        rows.append(jnp.zeros_like(rows[0]))
    out_ref[...] = jnp.concatenate(rows, axis=0)


def grads_kernel(plan, *refs):
    window = Window(plan, refs)
    rest = list(window.rest)
    stats = [rest.pop(0)[...] for _ in range(plan.n_stats)]
    if plan.n_stats == 2:
        half = plan.tile
        stats[1] = jnp.concatenate([stats[1][:, half:], stats[1][:, :half]], axis=1)
    dq_refs = [rest.pop(0) for _ in range(1 + plan.nr)]
    dk_ref, dv_ref = rest.pop(0), rest.pop(0)
    near_refs = ([rest.pop(0) for _ in range(plan.nc)], [rest.pop(0) for _ in range(plan.nf)])
    tile, hd = plan.tile, plan.hd
    for kind, cols, q, grad, slots in window.heads():
        base = 4 * kind
        parts = [tuple(s[base + i : base + i + 1, :] for i in range(3)) for s in stats]
        top, total, cross = merge(parts)
        log_total = top + jnp.log(total) * LOG2E
        row_dot = cross / total
        query_grad = None
        for at, ((key, value), count) in enumerate(slots):
            scores = masked_scores(key, q, count, plan.factor)
            softmax = jnp.exp2(scores - log_total)
            grad_softmax = dot(value, grad, NT)
            grad_scores = (softmax * (grad_softmax - row_dot)).astype(jnp.bfloat16)
            dv = dot(softmax.astype(jnp.bfloat16), grad, NN)
            dk = dot(grad_scores, q, NN) * plan.scale
            term = dot(key, grad_scores, TN)
            query_grad = term if query_grad is None else query_grad + term
            if at == 0:
                dk_ref[:, cols] = dk
                dv_ref[:, cols] = dv
            else:
                near_refs[kind][at - 1][0] = dk.astype(jnp.bfloat16)
                near_refs[kind][at - 1][1] = dv.astype(jnp.bfloat16)
        query_grad = jnp.transpose(query_grad * plan.scale)
        for at, ref in enumerate(dq_refs):
            ref[:, cols] = query_grad[at * tile : (at + 1) * tile].astype(ref.dtype)


def finish_kernel(plan, pairs, offsets_ref, *refs):
    refs = list(refs)
    take = lambda n: [refs.pop(0) for _ in range(n)]
    tile, hd = plan.tile, plan.hd
    per_pair = [(take(1 + plan.nr), take(2), take(plan.nc), take(plan.nf)) for _ in range(pairs)]
    dq_ref, dk_ref, dv_ref = refs
    for pair, (dq, own, near_plane, near_across) in enumerate(per_pair):
        at = pl.ds(pair * 2 * hd, 2 * hd)
        total = dq[0][...]
        for ref in dq[1:]:
            total = total + ref[...].astype(jnp.float32)
        dq_ref[:, at] = total.astype(dq_ref.dtype)
        flip = pair_flip(offsets_ref, pair)
        for kind, near in ((0, near_plane), (1, near_across)):
            place = flip if kind == 0 else 1 - flip
            cols = pl.ds(pl.multiple_of(place * hd, hd), hd)
            out_cols = pl.ds(pl.multiple_of((2 * pair + place) * hd, hd), hd)
            for i, out in enumerate((dk_ref, dv_ref)):
                total = own[i][:, cols]
                for ref in near:
                    total = total + ref[i].astype(jnp.float32)
                out[:, out_cols] = total.astype(out.dtype)


class Plan:
    pass


def params():
    return pltpu.CompilerParams(vmem_limit_bytes=VMEM_LIMIT)


def local(queries, key_rows, value_rows, grad_rows, offsets, counts):
    q, k, v, grad = queries[0, 0], key_rows[0, 0], value_rows[0, 0], grad_rows[0, 0]
    tile, width = q.shape
    heads = offsets.shape[0]
    pairs = heads // 2
    hd = width // heads
    sections = lax.axis_size("section")
    frame_count = lax.axis_size("frame")
    col_count = NCT
    row_count = lax.axis_size("tile") // col_count

    plan = Plan()
    plan.tile, plan.hd, plan.col_count = tile, hd, col_count
    plan.scale = 1.0 / math.sqrt(hd)
    plan.factor = plan.scale * LOG2E
    row_steps = steps_along(row_count)
    plan.col_steps = steps_along(col_count)
    plan.frame_steps = steps_along(frame_count)
    plan.nr, plan.nc, plan.nf = len(row_steps), len(plan.col_steps), len(plan.frame_steps)
    row_routes = [row_route(step, col_count) for step in row_steps]
    col_routes = [col_route(step, row_count) for step in plan.col_steps]
    frame_routes = [frame_route(step) for step in plan.frame_steps]

    def from_rows(x):
        return [lax.ppermute(x, "tile", route) for route in row_routes]

    far_q = from_rows(q)

    section = lax.axis_index("section")
    got = []
    for shift in range(1, sections):
        target = lax.rem(section + shift, sections)
        part = lax.dynamic_slice_in_dim(grad, target * width, width, 1)
        route = [(i, (i + shift) % sections) for i in range(sections)]
        got.append(lax.ppermute(part, "section", route))
    pair_shape = jax.ShapeDtypeStruct((tile, 2 * hd), jnp.bfloat16)
    vm = pl.BlockSpec(memory_space=pltpu.VMEM)
    grads = pl.pallas_call(
        functools.partial(gather_kernel, sections, pairs),
        out_shape=[pair_shape] * pairs,
        in_specs=[SMEM] + [vm] * sections,
        out_specs=[vm] * pairs,
        compiler_params=params(),
        name="gather_grad",
    )(counts, grad, *got)

    packed = jax.ShapeDtypeStruct((2, tile, pairs * hd), jnp.bfloat16)
    plane_kv, across_kv = pl.pallas_call(
        functools.partial(pack_kernel, pairs, hd),
        out_shape=[packed, packed],
        in_specs=[SMEM, vm, vm],
        out_specs=[vm, vm],
        compiler_params=params(),
        name="pack_kv",
    )(offsets, k, v)
    near_plane = [lax.ppermute(plane_kv, "tile", route) for route in col_routes]
    near_across = [lax.ppermute(across_kv, "frame", route) for route in frame_routes]
    far_grads = [from_rows(g) for g in grads]

    nq = 1 + plan.nr
    blocks = 2 * nq + plan.nc + plan.nf
    half_cost = 2 * 2 * nq * (2 + plan.nc + plan.nf) * tile * tile * hd
    done = []
    for pair in range(pairs):
        plan_m = Plan()
        plan_m.__dict__.update(plan.__dict__)
        plan_m.pair = pair
        wide = pl.BlockSpec((tile, 2 * hd), lambda i, pair=pair: (0, pair))
        whole = pl.BlockSpec((tile, 2 * hd), lambda i: (0, 0))
        kv = pl.BlockSpec((2, tile, hd), lambda i, pair=pair: (0, 0, pair))
        kv_out = pl.BlockSpec((2, tile, hd), lambda i: (0, 0, 0))
        stat = pl.BlockSpec((8, nq * tile), lambda i: (0, 0))
        operands = [offsets, counts, q, *far_q, grads[pair], *far_grads[pair], k, v]
        operands += near_plane + near_across
        specs = [SMEM, SMEM] + [wide] * nq + [whole] * nq + [wide] * 2 + [kv] * (plan.nc + plan.nf)
        stats = pl.pallas_call(
            functools.partial(stats_kernel, plan_m),
            grid=(1,),
            out_shape=jax.ShapeDtypeStruct((8, nq * tile), jnp.float32),
            in_specs=specs,
            out_specs=stat,
            compiler_params=params(),
            cost_estimate=pl.CostEstimate(flops=half_cost, bytes_accessed=2 << 20, transcendentals=0),
            name="row_totals",
        )(*operands)
        all_stats = share_stats(stats, row_routes, tile)
        plan_m.n_stats = len(all_stats)
        f32_pair = jax.ShapeDtypeStruct((tile, 2 * hd), jnp.float32)
        near_out = jax.ShapeDtypeStruct((2, tile, hd), jnp.bfloat16)
        outs = pl.pallas_call(
            functools.partial(grads_kernel, plan_m),
            grid=(1,),
            out_shape=[f32_pair] + [pair_shape] * plan.nr + [f32_pair] * 2 + [near_out] * (plan.nc + plan.nf),
            in_specs=specs + [stat] * len(all_stats),
            out_specs=[whole] * (nq + 2) + [kv_out] * (plan.nc + plan.nf),
            compiler_params=params(),
            cost_estimate=pl.CostEstimate(flops=half_cost * 5 // 2, bytes_accessed=4 << 20, transcendentals=0),
            name="pair_grads",
        )(*operands, *all_stats)
        own_q, far_out = outs[0], outs[1:nq]
        own_kv = outs[nq : nq + 2]
        plane_out = outs[nq + 2 : nq + 2 + plan.nc]
        across_out = outs[nq + 2 + plan.nc :]
        back_q = [lax.ppermute(x, "tile", reverse(r)) for x, r in zip(far_out, row_routes)]
        back_plane = [lax.ppermute(x, "tile", reverse(r)) for x, r in zip(plane_out, col_routes)]
        back_across = [lax.ppermute(x, "frame", reverse(r)) for x, r in zip(across_out, frame_routes)]
        done += [own_q, *back_q, *own_kv, *back_plane, *back_across]

    out = jax.ShapeDtypeStruct((tile, width), jnp.bfloat16)
    dq, dk, dv = pl.pallas_call(
        functools.partial(finish_kernel, plan, pairs),
        out_shape=[out] * 3,
        in_specs=[SMEM] + [vm] * len(done),
        out_specs=[vm] * 3,
        compiler_params=params(),
        name="add_terms",
    )(offsets, *done)
    return dq[None, None], dk[None, None], dv[None, None]


def share_stats(stats, row_routes, tile):
    if len(row_routes) == 0:
        return [stats]
    if len(row_routes) == 1:
        return [stats, lax.ppermute(stats, "tile", row_routes[0])]
    terms = [stats[:, :tile]]
    for at, route in enumerate(row_routes):
        part = stats[:, (at + 1) * tile : (at + 2) * tile]
        terms.append(lax.ppermute(part, "tile", reverse(route)))
    merged = []
    for base in (0, 4):
        parts = [(t[base], t[base + 1], t[base + 2]) for t in terms]
        parts = [(jnp.where(l > 0, m, DEAD), l, t) for m, l, t in parts]
        merged += list(merge(parts))
        merged.append(jnp.ones_like(merged[0]))
    totals = jnp.stack(merged)
    shared = [totals] + [lax.ppermute(totals, "tile", route) for route in row_routes]
    return [jnp.concatenate(shared, axis=1)]


def solution(mesh):
    return jax.shard_map(
        local,
        mesh=mesh,
        in_specs=(
            P("frame", "tile", None, "section"),
            P("frame", "tile", None, "section"),
            P("frame", "tile", None, "section"),
            P("frame", "tile", "section", None),
            P("section", None, None),
            P(),
        ),
        out_specs=(
            P("frame", "tile", None, "section"),
            P("frame", "tile", None, "section"),
            P("frame", "tile", None, "section"),
        ),
        check_vma=False,
    )
```

time: 463 us -> 104 us (0.22); the launches traced: 454 us -> 103 us
  local copies, waits for them, and re-layouts: 131 us -> 2.85 us
  starting transfers between devices: 145 us -> 42.3 us
  matrix products: 50.7 us -> 0 us
  other arithmetic: 49.5 us -> 0 us
  waiting for transfers between devices: 65.7 us -> 34.8 us
  Pallas kernels: 0 us -> 22.1 us
  between operations: 12 us -> 0.89 us
    ppermute x40 -> x23, starting transfers between devices: 141 us -> 42.3 us  [the longest x9 22.3 us: local(): lax.ppermute(x, 'tile', reverse(r))]
    dot_general x30 -> x0, matrix products: 50.7 us -> none  [the longest x6 15.2 us: one_head(): jnp.einsum('iw,ie->we', softmax_low, grad_head, preferred_element_type=jn...]
    dynamic_update_slice x30 -> x0, local copies, waits for them, and re-layouts: 41 us -> none  [the longest x12 20.4 us: one_head(): lax.dynamic_update_slice_in_dim(value_parts, value_part.reshape(window, t...]
    ppermute x40 -> x23, waiting for transfers between devices: 65.7 us -> 34.8 us  [the longest x4 20.9 us: from_rows(): return [lax.ppermute(x, 'tile', route) for route in row_routes]]
    pallas_call x0 -> x9, Pallas kernels: none -> 22.1 us  [the longest x3 9.82 us: local(): pl.pallas_call(functools.partial(grads_kernel, plan_m), grid=(1,), out_sh...]
    unnamed x135 -> x15, local copies, waits for them, and re-layouts: 22.6 us -> 2.84 us
    gather x20 -> x0, local copies, waits for them, and re-layouts: 16.6 us -> none  [the longest x16 9.36 us: pick_heads(): jnp.take(split, chosen, axis=1)]
    another operation x13 -> x0, local copies, waits for them, and re-layouts: 13.9 us -> none
  transfers between devices with their start and end apart: 41 -> 23, of which waited for: 14 -> 5; matrix products, arithmetic and copies ran while one was open for 32% -> 0% of each run, Pallas kernels for 0% -> 17%
where the time goes in v1:
time: 104 us; the launch traced here: 103 us
  starting transfers between devices  42.3 us (41%)
  waiting for transfers between devices  34.8 us (33%)
  Pallas kernels  22.1 us (21%)
  local copies, waits for them, and re-layouts  2.85 us (3%)
    ppermute x9, starting transfers between devices, local(): lax.ppermute(x, 'tile', reverse(r))  22.3 us
    ppermute x4, waiting for transfers between devices, from_rows(): return [lax.ppermute(x, 'tile', route) for route in row_routes]  20.9 us
    pallas_call x3, Pallas kernels, local(): pl.pallas_call(functools.partial(grads_kernel, plan_m), grid=(1,), out_sh...  9.82 us
    pallas_call x3, Pallas kernels, local(): pl.pallas_call(functools.partial(stats_kernel, plan_m), grid=(1,), out_sh...  7.54 us
    ppermute x2, starting transfers between devices, local(): near_plane = [lax.ppermute(plane_kv, 'tile', route) for route in col_routes]  6.74 us
    ppermute x3, waiting for transfers between devices, share_stats(): return [stats, lax.ppermute(stats, 'tile', row_routes[0])]  6.68 us
    ppermute x4, starting transfers between devices, from_rows(): return [lax.ppermute(x, 'tile', route) for route in row_routes]  5.92 us
    ppermute x9, waiting for transfers between devices, local(): lax.ppermute(x, 'tile', reverse(r))  5.82 us
  transfers between devices with their start and end apart: 23, of which 5 were waited for; matrix products, arithmetic and copies ran while one was open for 0% of the time, Pallas kernels for 17%

profile of v1, /device:TPU:24, one launch (start us, length us, event | category | flops | bytes accessed | tf_op | source)
XLA Modules:
  0.0 103.0 jit_solution(1479437534230121126)
XLA Ops:
  0.6 0.8 copy.16.offsets_ref.refs_0_
  1.5 1.0 copy-done
  2.5 1.0 copy-done.2
  3.5 1.5 %pack_kv.1 = (bf16[2,256,384]{2,1,0:T(8,128)(2,1)S(1)}, bf16[2,256,384]{2,1,0:T(8,128)(2,1)S(1)}) custom-call(s32[6,9,3]{2,1,0:T(8,128)S(1)} %copy.16.offsets_ref.refs_0_, bf16[256,768]{1,0:T(8,128)(2,1)S(1)} %bitcast.9, bf16[256,768]{1,0:T(8,128)(2,1)S(1)} %bitcast.16), custom_call_target="tpu_custom_call" | custom-call | tf_op jit(solution)/shard_map/pack_kv/pallas_call | solution.py:309
  5.0 3.4 %collective-permute-start.3 = (bf16[2,256,384]{2,1,0:T(8,128)(2,1)S(1)}, bf16[2,256,384]{2,1,0:T(8,128)(2,1)S(1)}, u32[]{:S(2)}, u32[]{:S(2)}) collective-permute-start(bf16[2,256,384]{2,1,0:T(8,128)(2,1)S(1)} %get-tuple-element.33), channel_id=1, source_target_pairs={{0,1},{4,5},{1,2},{5,6},{2,3},{6,7},{8,9},{12,13},{9,10},{13,14},{... | collective-permute-start | bytes 1179656 | tf_op jit(solution)/shard_map/ppermute | solution.py:317
  8.4 3.3 %collective-permute-start.4 = (bf16[2,256,384]{2,1,0:T(8,128)(2,1)S(1)}, bf16[2,256,384]{2,1,0:T(8,128)(2,1)S(1)}, u32[]{:S(2)}, u32[]{:S(2)}) collective-permute-start(bf16[2,256,384]{2,1,0:T(8,128)(2,1)S(1)} %get-tuple-element.33), channel_id=1, source_target_pairs={{1,0},{5,4},{2,1},{6,5},{3,2},{7,6},{9,8},{13,12},{10,9},{14,13},{... | collective-permute-start | bytes 1179656 | tf_op jit(solution)/shard_map/ppermute | solution.py:317
  11.7 1.6 %collective-permute-start.5 = (bf16[2,256,384]{2,1,0:T(8,128)(2,1)S(1)}, bf16[2,256,384]{2,1,0:T(8,128)(2,1)S(1)}, u32[]{:S(2)}, u32[]{:S(2)}) collective-permute-start(bf16[2,256,384]{2,1,0:T(8,128)(2,1)S(1)} %get-tuple-element.34), channel_id=1, source_target_pairs={{8,0},{0,8},{9,1},{1,9},{10,2},{2,10},{11,3},{3,11},{12,4},{4,12},... | collective-permute-start | bytes 1179656 | tf_op jit(solution)/shard_map/ppermute | solution.py:318
  13.3 0.0 copy-done.4
  13.3 0.3 collective-permute-start
  13.7 0.0 copy-done.5
  13.7 0.0 copy-start.1
  13.7 0.1 collective-permute-start.1
  13.8 1.4 %collective-permute-done.1.refs_0_ = bf16[128,768]{1,0:T(8,128)(2,1)S(1)} collective-permute-done((bf16[128,768]{1,0:T(8,128)(2,1)S(1)}, bf16[128,768]{1,0:T(8,128)(2,1)S(1)}, u32[]{:S(2)}, u32[]{:S(2)}) %collective-permute-start.1) | collective-permute-done | bytes 196640 | tf_op jit(solution)/shard_map/ppermute | solution.py:296
  15.2 0.0 copy-done.6
  15.2 0.6 gather_grad.1
  15.9 2.7 %collective-permute-start.17 = (bf16[256,256]{1,0:T(8,128)(2,1)S(1)}, bf16[256,256]{1,0:T(8,128)(2,1)S(1)}, u32[]{:S(2)}, u32[]{:S(2)}) collective-permute-start(bf16[256,256]{1,0:T(8,128)(2,1)S(1)} %get-tuple-element.50.refs_4_), channel_id=1, source_target_pairs={{4,0},{5,1},{6,2},{7,3},{0,4},{1,5},{2,6},{3,7},{12,8},{13,9},{14,... | collective-permute-start | bytes 393224 | tf_op jit(solution)/shard_map/ppermute | solution.py:286
  18.5 20.9 %collective-permute-done.17.refs_5_ = bf16[256,256]{1,0:T(8,128)(2,1)S(1)} collective-permute-done((bf16[256,256]{1,0:T(8,128)(2,1)S(1)}, bf16[256,256]{1,0:T(8,128)(2,1)S(1)}, u32[]{:S(2)}, u32[]{:S(2)}) %collective-permute-start.17) | collective-permute-done | bytes 131104 | tf_op jit(solution)/shard_map/ppermute | solution.py:286
  39.4 0.0 collective-permute-start.11
  39.4 0.0 collective-permute-done.3.refs_8_
  39.4 2.9 %collective-permute-start.2 = (bf16[256,256]{1,0:T(8,128)(2,1)S(1)}, bf16[256,256]{1,0:T(8,128)(2,1)S(1)}, u32[]{:S(2)}, u32[]{:S(2)}) collective-permute-start(bf16[256,256]{1,0:T(8,128)(2,1)S(1)} %get-tuple-element.32.refs_4_), channel_id=1, source_target_pairs={{4,0},{5,1},{6,2},{7,3},{0,4},{1,5},{2,6},{3,7},{12,8},{13,9},{14,... | collective-permute-start | bytes 393224 | tf_op jit(solution)/shard_map/ppermute | solution.py:286
  42.3 0.0 collective-permute-done.4.refs_9_
  42.3 0.0 collective-permute-done.5.refs_10_
  42.3 0.0 collective-permute-done.refs_3_
  42.3 0.0 copy-done.3
  42.4 0.0 copy-done.1
  42.4 2.5 %row_totals.5.refs_11_ = f32[8,512]{1,0:T(8,128)S(1)} custom-call(s32[6,9,3]{2,1,0:T(8,128)S(1)} %copy.16.offsets_ref.refs_0_, s32[2,8]{1,0:T(2,128)S(1)} %copy-done.6, bf16[256,768]{1,0:T(8,128)(2,1)S(1)} %bitcast.24, bf16[256,768]{1,0:T(8,128)(2,1)S(1)} %collective-permute-done.refs_3_, bf16[256,256]{1,0:T(8,128)(2,1)S(1)} %get-tuple-element.50.refs_4_, ...), custom_call_target="tpu_custom_call" | custom-call | flops 335544320 | bytes 2097152 | tf_op jit(solution)/shard_map/row_totals/pallas_call | solution.py:337
  44.9 0.1 collective-permute-start.18
  45.0 6.7 %collective-permute-done.18.refs_12_ = f32[8,512]{1,0:T(8,128)S(1)} collective-permute-done((f32[8,512]{1,0:T(8,128)S(1)}, f32[8,512]{1,0:T(8,128)S(1)}, u32[]{:S(2)}, u32[]{:S(2)}) %collective-permute-start.18) | collective-permute-done | bytes 16416 | tf_op jit(solution)/shard_map/ppermute | solution.py:386
  51.7 3.3 %pair_grads.5 = (f32[256,256]{1,0:T(8,128)S(1)}, bf16[256,256]{1,0:T(8,128)(2,1)S(1)}, f32[256,256]{1,0:T(8,128)S(1)}, f32[256,256]{1,0:T(8,128)S(1)}, bf16[2,25...) custom-call(s32[6,9,3]{2,1,0:T(8,128)S(1)} %copy.16.offsets_ref.refs_0_, ...), custom_call_target="tpu_custom_call" | custom-call | flops 838860800 | bytes 4194304 | tf_op jit(solution)/shard_map/pair_grads/pallas_call | solution.py:351
  54.9 0.1 collective-permute-start.19
  55.0 3.7 %collective-permute-start.20 = (bf16[2,256,128]{2,1,0:T(8,128)(2,1)S(1)}, bf16[2,256,128]{2,1,0:T(8,128)(2,1)S(1)}, u32[]{:S(2)}, u32[]{:S(2)}) collective-permute-start(bf16[2,256,128]{2,1,0:T(8,128)(2,1)S(1)} %get-tuple-element.55), channel_id=1, source_target_pairs={{1,0},{5,4},{2,1},{6,5},{3,2},{7,6},{9,8},{13,12},{10,9},{14,13},{... | collective-permute-start | bytes 393224 | tf_op jit(solution)/shard_map/ppermute | solution.py:366
  58.7 0.0 collective-permute-done.11.refs_5_
  58.7 2.5 %row_totals.4.refs_11_ = f32[8,512]{1,0:T(8,128)S(1)} custom-call(s32[6,9,3]{2,1,0:T(8,128)S(1)} %copy.16.offsets_ref.refs_0_, s32[2,8]{1,0:T(2,128)S(1)} %copy-done.6, bf16[256,768]{1,0:T(8,128)(2,1)S(1)} %bitcast.26, bf16[256,768]{1,0:T(8,128)(2,1)S(1)} %collective-permute-done.refs_3_, bf16[256,256]{1,0:T(8,128)(2,1)S(1)} %get-tuple-element.42.refs_4_, ...), custom_call_target="tpu_custom_call" | custom-call | flops 335544320 | bytes 2097152 | tf_op jit(solution)/shard_map/row_totals/pallas_call | solution.py:337
  61.3 1.2 %collective-permute-start.12 = (f32[8,512]{1,0:T(8,128)S(1)}, f32[8,512]{1,0:T(8,128)S(1)}, u32[]{:S(2)}, u32[]{:S(2)}) collective-permute-start(f32[8,512]{1,0:T(8,128)S(1)} %row_totals.4.refs_11_), channel_id=1, source_target_pairs={{4,0},{5,1},{6,2},{7,3},{0,4},{1,5},{2,6},{3,7},{12,8},{13,9},{14,... | collective-permute-start | bytes 49160 | tf_op jit(solution)/shard_map/ppermute | solution.py:386
  62.4 0.0 collective-permute-done.2.refs_5_
  62.4 2.5 %row_totals.3.refs_11_ = f32[8,512]{1,0:T(8,128)S(1)} custom-call(s32[6,9,3]{2,1,0:T(8,128)S(1)} %copy.16.offsets_ref.refs_0_, s32[2,8]{1,0:T(2,128)S(1)} %copy-done.6, bf16[256,768]{1,0:T(8,128)(2,1)S(1)} %bitcast.27, bf16[256,768]{1,0:T(8,128)(2,1)S(1)} %collective-permute-done.refs_3_, bf16[256,256]{1,0:T(8,128)(2,1)S(1)} %get-tuple-element.32.refs_4_, ...), custom_call_target="tpu_custom_call" | custom-call | flops 335544320 | bytes 2097152 | tf_op jit(solution)/shard_map/row_totals/pallas_call | solution.py:337
  65.0 1.9 %collective-permute-start.6 = (f32[8,512]{1,0:T(8,128)S(1)}, f32[8,512]{1,0:T(8,128)S(1)}, u32[]{:S(2)}, u32[]{:S(2)}) collective-permute-start(f32[8,512]{1,0:T(8,128)S(1)} %row_totals.3.refs_11_), channel_id=1, source_target_pairs={{4,0},{5,1},{6,2},{7,3},{0,4},{1,5},{2,6},{3,7},{12,8},{13,9},{14,... | collective-permute-start | bytes 49160 | tf_op jit(solution)/shard_map/ppermute | solution.py:386
  66.8 2.1 %collective-permute-start.21 = (bf16[2,256,128]{2,1,0:T(8,128)(2,1)S(1)}, bf16[2,256,128]{2,1,0:T(8,128)(2,1)S(1)}, u32[]{:S(2)}, u32[]{:S(2)}) collective-permute-start(bf16[2,256,128]{2,1,0:T(8,128)(2,1)S(1)} %get-tuple-element.56), channel_id=1, source_target_pairs={{0,1},{4,5},{1,2},{5,6},{2,3},{6,7},{8,9},{12,13},{9,10},{13,14},{... | collective-permute-start | bytes 393224 | tf_op jit(solution)/shard_map/ppermute | solution.py:366
  69.0 0.0 collective-permute-done.12.refs_12_
  69.0 0.4 collective-permute-start.22
  69.4 3.3 %pair_grads.4 = (f32[256,256]{1,0:T(8,128)S(1)}, bf16[256,256]{1,0:T(8,128)(2,1)S(1)}, f32[256,256]{1,0:T(8,128)S(1)}, f32[256,256]{1,0:T(8,128)S(1)}, bf16[2,25...) custom-call(s32[6,9,3]{2,1,0:T(8,128)S(1)} %copy.16.offsets_ref.refs_0_, ...), custom_call_target="tpu_custom_call" | custom-call | flops 838860800 | bytes 4194304 | tf_op jit(solution)/shard_map/pair_grads/pallas_call | solution.py:351
  72.7 0.0 collective-permute-done.6.refs_12_
  72.7 2.9 %collective-permute-start.13 = (bf16[256,256]{1,0:T(8,128)(2,1)S(1)}, bf16[256,256]{1,0:T(8,128)(2,1)S(1)}, u32[]{:S(2)}, u32[]{:S(2)}) collective-permute-start(bf16[256,256]{1,0:T(8,128)(2,1)S(1)} %get-tuple-element.44), channel_id=1, source_target_pairs={{0,4},{1,5},{2,6},{3,7},{4,0},{5,1},{6,2},{7,3},{8,12},{9,13},{10,... | collective-permute-start | bytes 393224 | tf_op jit(solution)/shard_map/ppermute | solution.py:365
  75.7 0.0 collective-permute-done.19.refs_15_
  75.7 2.8 %collective-permute-start.14 = (bf16[2,256,128]{2,1,0:T(8,128)(2,1)S(1)}, bf16[2,256,128]{2,1,0:T(8,128)(2,1)S(1)}, u32[]{:S(2)}, u32[]{:S(2)}) collective-permute-start(bf16[2,256,128]{2,1,0:T(8,128)(2,1)S(1)} %get-tuple-element.47), channel_id=1, source_target_pairs={{1,0},{5,4},{2,1},{6,5},{3,2},{7,6},{9,8},{13,12},{10,9},{14,13},{... | collective-permute-start | bytes 393224 | tf_op jit(solution)/shard_map/ppermute | solution.py:366
  78.5 0.0 collective-permute-done.20.refs_18_
  78.5 3.0 %collective-permute-start.15 = (bf16[2,256,128]{2,1,0:T(8,128)(2,1)S(1)}, bf16[2,256,128]{2,1,0:T(8,128)(2,1)S(1)}, u32[]{:S(2)}, u32[]{:S(2)}) collective-permute-start(bf16[2,256,128]{2,1,0:T(8,128)(2,1)S(1)} %get-tuple-element.48), channel_id=1, source_target_pairs={{0,1},{4,5},{1,2},{5,6},{2,3},{6,7},{8,9},{12,13},{9,10},{13,14},{... | collective-permute-start | bytes 393224 | tf_op jit(solution)/shard_map/ppermute | solution.py:366
  81.5 3.3 %pair_grads.3 = (f32[256,256]{1,0:T(8,128)S(1)}, bf16[256,256]{1,0:T(8,128)(2,1)S(1)}, f32[256,256]{1,0:T(8,128)S(1)}, f32[256,256]{1,0:T(8,128)S(1)}, bf16[2,25...) custom-call(s32[6,9,3]{2,1,0:T(8,128)S(1)} %copy.16.offsets_ref.refs_0_, ...), custom_call_target="tpu_custom_call" | custom-call | flops 838860800 | bytes 4194304 | tf_op jit(solution)/shard_map/pair_grads/pallas_call | solution.py:351
  84.8 0.0 collective-permute-done.21.refs_19_
  84.8 1.7 %collective-permute-start.16 = (bf16[2,256,128]{2,1,0:T(8,128)(2,1)S(1)}, bf16[2,256,128]{2,1,0:T(8,128)(2,1)S(1)}, u32[]{:S(2)}, u32[]{:S(2)}) collective-permute-start(bf16[2,256,128]{2,1,0:T(8,128)(2,1)S(1)} %get-tuple-element.49), channel_id=1, source_target_pairs={{0,8},{8,0},{1,9},{9,1},{2,10},{10,2},{3,11},{11,3},{4,12},{12,4},... | collective-permute-start | bytes 393224 | tf_op jit(solution)/shard_map/ppermute | solution.py:367
  86.6 0.0 collective-permute-done.22.refs_20_
  86.6 0.4 collective-permute-start.10
  86.9 0.0 collective-permute-done.13.refs_8_
  86.9 0.8 collective-permute-start.7
  87.8 0.0 collective-permute-done.14.refs_11_
  87.8 4.8 %collective-permute-start.8 = (bf16[2,256,128]{2,1,0:T(8,128)(2,1)S(1)}, bf16[2,256,128]{2,1,0:T(8,128)(2,1)S(1)}, u32[]{:S(2)}, u32[]{:S(2)}) collective-permute-start(bf16[2,256,128]{2,1,0:T(8,128)(2,1)S(1)} %get-tuple-element.39), channel_id=1, source_target_pairs={{1,0},{5,4},{2,1},{6,5},{3,2},{7,6},{9,8},{13,12},{10,9},{14,13},{... | collective-permute-start | bytes 393224 | tf_op jit(solution)/shard_map/ppermute | solution.py:366
  92.6 0.0 collective-permute-done.15.refs_12_
  92.6 1.9 %collective-permute-start.9 = (bf16[2,256,128]{2,1,0:T(8,128)(2,1)S(1)}, bf16[2,256,128]{2,1,0:T(8,128)(2,1)S(1)}, u32[]{:S(2)}, u32[]{:S(2)}) collective-permute-start(bf16[2,256,128]{2,1,0:T(8,128)(2,1)S(1)} %get-tuple-element.40), channel_id=1, source_target_pairs={{0,1},{4,5},{1,2},{5,6},{2,3},{6,7},{8,9},{12,13},{9,10},{13,14},{... | collective-permute-start | bytes 393224 | tf_op jit(solution)/shard_map/ppermute | solution.py:366
  94.5 0.0 collective-permute-done.16.refs_13_
  94.6 0.0 collective-permute-done.10.refs_6_
  94.6 0.0 collective-permute-done.7.refs_1_
  94.6 1.5 %collective-permute-done.8.refs_4_ = bf16[2,256,128]{2,1,0:T(8,128)(2,1)S(1)} collective-permute-done((bf16[2,256,128]{2,1,0:T(8,128)(2,1)S(1)}, bf16[2,256,128]{2,1,0:T(8,128)(2,1)S(1)}, u32[]{:S(2)}, u32[]{:S(2)}) %collective-permute-start.8) | collective-permute-done | bytes 131104 | tf_op jit(solution)/shard_map/ppermute | solution.py:366
  96.0 4.3 %collective-permute-done.9.refs_5_ = bf16[2,256,128]{2,1,0:T(8,128)(2,1)S(1)} collective-permute-done((bf16[2,256,128]{2,1,0:T(8,128)(2,1)S(1)}, bf16[2,256,128]{2,1,0:T(8,128)(2,1)S(1)}, u32[]{:S(2)}, u32[]{:S(2)}) %collective-permute-start.9) | collective-permute-done | bytes 131104 | tf_op jit(solution)/shard_map/ppermute | solution.py:366
  100.4 2.6 %add_terms.1 = (bf16[256,768]{1,0:T(8,128)(2,1)}, bf16[256,768]{1,0:T(8,128)(2,1)}, bf16[256,768]{1,0:T(8,128)(2,1)}) custom-call(s32[6,9,3]{2,1,0:T(8,128)S(1)} %copy.16.offsets_ref.refs_0_, f32[256,256]{1,0:T(8,128)S(1)} %get-tuple-element.35.refs_0_, bf16[256,256]{1,0:T(8,128)(2,1)S(1)} %collective-permute-done.7.refs_1_, ...), custom_call_target="tpu_custom_call" | custom-call | tf_op jit(solution)/shard_map/add_terms/pallas_call | solution.py:371
  (7 shorter events, 0.0 us)
Async XLA Ops:
  1.5 1.0 copy-start
  2.5 1.0 copy-start.2
  3.4 9.9 %copy-start.4 = (bf16[1,1,256,768]{3,2,1,0:T(8,128)(2,1)S(1)}, bf16[1,1,256,768]{3,2,1,0:T(8,128)(2,1)}, u32[]{:S(2)}) copy-start(bf16[1,1,256,768]{3,2,1,0:T(8,128)(2,1)} %param.6) | copy-start | bytes 1179652
  3.5 10.2 %copy-start.5 = (bf16[1,1,128,1536]{3,2,1,0:T(8,128)(2,1)S(1)}, bf16[1,1,128,1536]{3,2,1,0:T(8,128)(2,1)}, u32[]{:S(2)}) copy-start(bf16[1,1,128,1536]{3,2,1,0:T(8,128)(2,1)} %param.9) | copy-start | bytes 1179652
  5.0 34.4 %collective-permute-start.3 = (bf16[2,256,384]{2,1,0:T(8,128)(2,1)S(1)}, bf16[2,256,384]{2,1,0:T(8,128)(2,1)S(1)}, u32[]{:S(2)}, u32[]{:S(2)}) collective-permute-start(bf16[2,256,384]{2,1,0:T(8,128)(2,1)S(1)} %get-tuple-element.33), channel_id=1, source_target_pairs={{0,1},{4,5},{1,2},{5,6},{2,3},{6,7},{8,9},{12,13},{9,10},{13,14},{... | collective-permute-start | bytes 1179656 | tf_op jit(solution)/shard_map/ppermute | solution.py:317
  8.4 33.9 %collective-permute-start.4 = (bf16[2,256,384]{2,1,0:T(8,128)(2,1)S(1)}, bf16[2,256,384]{2,1,0:T(8,128)(2,1)S(1)}, u32[]{:S(2)}, u32[]{:S(2)}) collective-permute-start(bf16[2,256,384]{2,1,0:T(8,128)(2,1)S(1)} %get-tuple-element.33), channel_id=1, source_target_pairs={{1,0},{5,4},{2,1},{6,5},{3,2},{7,6},{9,8},{13,12},{10,9},{14,13},{... | collective-permute-start | bytes 1179656 | tf_op jit(solution)/shard_map/ppermute | solution.py:317
  11.7 30.6 %collective-permute-start.5 = (bf16[2,256,384]{2,1,0:T(8,128)(2,1)S(1)}, bf16[2,256,384]{2,1,0:T(8,128)(2,1)S(1)}, u32[]{:S(2)}, u32[]{:S(2)}) collective-permute-start(bf16[2,256,384]{2,1,0:T(8,128)(2,1)S(1)} %get-tuple-element.34), channel_id=1, source_target_pairs={{8,0},{0,8},{9,1},{1,9},{10,2},{2,10},{11,3},{3,11},{12,4},{4,12},... | collective-permute-start | bytes 1179656 | tf_op jit(solution)/shard_map/ppermute | solution.py:318
  13.3 29.0 %collective-permute-start = (bf16[256,768]{1,0:T(8,128)(2,1)S(1)}, bf16[256,768]{1,0:T(8,128)(2,1)S(1)}, u32[]{:S(2)}, u32[]{:S(2)}) collective-permute-start(bf16[256,768]{1,0:T(8,128)(2,1)S(1)} %bitcast.23), channel_id=1, source_target_pairs={{4,0},{5,1},{6,2},{7,3},{0,4},{1,5},{2,6},{3,7},{12,8},{13,9},{14,... | collective-permute-start | bytes 1179656 | tf_op jit(solution)/shard_map/ppermute | solution.py:286
  13.7 1.5 %copy-start.6 = (s32[2,8]{1,0:T(2,128)S(1)}, s32[2,8]{1,0:T(2,128)}, u32[]{:S(2)}) copy-start(s32[2,8]{1,0:T(2,128)} %refs_1_.11) | copy-start | bytes 196
  13.7 28.7 %copy-start.3 = (bf16[1,1,256,768]{3,2,1,0:T(8,128)(2,1)S(1)}, bf16[1,1,256,768]{3,2,1,0:T(8,128)(2,1)}, u32[]{:S(2)}) copy-start(bf16[1,1,256,768]{3,2,1,0:T(8,128)(2,1)} %param.8) | copy-start | bytes 1179652
  13.7 28.7 %copy-start.1 = (bf16[1,1,256,768]{3,2,1,0:T(8,128)(2,1)S(1)}, bf16[1,1,256,768]{3,2,1,0:T(8,128)(2,1)}, u32[]{:S(2)}) copy-start(bf16[1,1,256,768]{3,2,1,0:T(8,128)(2,1)} %param.7) | copy-start | bytes 1179652
  13.7 1.5 %collective-permute-start.1 = (bf16[128,768]{1,0:T(8,128)(2,1)S(1)}, bf16[128,768]{1,0:T(8,128)(2,1)S(1)}, u32[]{:S(2)}, u32[]{:S(2)}) collective-permute-start(bf16[128,768]{1,0:T(8,128)(2,1)S(1)} %dynamic-slice_bitcast_fusion), channel_id=1, source_target_pairs={{0,16},{16,0},{1,17},{17,1},{2,18},{18,2},{3,19},{19,3},{4,20},{20... | collective-permute-start | bytes 589832 | tf_op jit(solution)/shard_map/ppermute | solution.py:296
  15.9 23.5 %collective-permute-start.17 = (bf16[256,256]{1,0:T(8,128)(2,1)S(1)}, bf16[256,256]{1,0:T(8,128)(2,1)S(1)}, u32[]{:S(2)}, u32[]{:S(2)}) collective-permute-start(bf16[256,256]{1,0:T(8,128)(2,1)S(1)} %get-tuple-element.50.refs_4_), channel_id=1, source_target_pairs={{4,0},{5,1},{6,2},{7,3},{0,4},{1,5},{2,6},{3,7},{12,8},{13,9},{14,... | collective-permute-start | bytes 393224 | tf_op jit(solution)/shard_map/ppermute | solution.py:286
  39.4 19.3 %collective-permute-start.11 = (bf16[256,256]{1,0:T(8,128)(2,1)S(1)}, bf16[256,256]{1,0:T(8,128)(2,1)S(1)}, u32[]{:S(2)}, u32[]{:S(2)}) collective-permute-start(bf16[256,256]{1,0:T(8,128)(2,1)S(1)} %get-tuple-element.42.refs_4_), channel_id=1, source_target_pairs={{4,0},{5,1},{6,2},{7,3},{0,4},{1,5},{2,6},{3,7},{12,8},{13,9},{14,... | collective-permute-start | bytes 393224 | tf_op jit(solution)/shard_map/ppermute | solution.py:286
  39.4 23.0 %collective-permute-start.2 = (bf16[256,256]{1,0:T(8,128)(2,1)S(1)}, bf16[256,256]{1,0:T(8,128)(2,1)S(1)}, u32[]{:S(2)}, u32[]{:S(2)}) collective-permute-start(bf16[256,256]{1,0:T(8,128)(2,1)S(1)} %get-tuple-element.32.refs_4_), channel_id=1, source_target_pairs={{4,0},{5,1},{6,2},{7,3},{0,4},{1,5},{2,6},{3,7},{12,8},{13,9},{14,... | collective-permute-start | bytes 393224 | tf_op jit(solution)/shard_map/ppermute | solution.py:286
  44.9 6.8 %collective-permute-start.18 = (f32[8,512]{1,0:T(8,128)S(1)}, f32[8,512]{1,0:T(8,128)S(1)}, u32[]{:S(2)}, u32[]{:S(2)}) collective-permute-start(f32[8,512]{1,0:T(8,128)S(1)} %row_totals.5.refs_11_), channel_id=1, source_target_pairs={{4,0},{5,1},{6,2},{7,3},{0,4},{1,5},{2,6},{3,7},{12,8},{13,9},{14,... | collective-permute-start | bytes 49160 | tf_op jit(solution)/shard_map/ppermute | solution.py:386
  54.9 20.7 %collective-permute-start.19 = (bf16[256,256]{1,0:T(8,128)(2,1)S(1)}, bf16[256,256]{1,0:T(8,128)(2,1)S(1)}, u32[]{:S(2)}, u32[]{:S(2)}) collective-permute-start(bf16[256,256]{1,0:T(8,128)(2,1)S(1)} %get-tuple-element.52), channel_id=1, source_target_pairs={{0,4},{1,5},{2,6},{3,7},{4,0},{5,1},{6,2},{7,3},{8,12},{9,13},{10,... | collective-permute-start | bytes 393224 | tf_op jit(solution)/shard_map/ppermute | solution.py:365
  55.0 23.5 %collective-permute-start.20 = (bf16[2,256,128]{2,1,0:T(8,128)(2,1)S(1)}, bf16[2,256,128]{2,1,0:T(8,128)(2,1)S(1)}, u32[]{:S(2)}, u32[]{:S(2)}) collective-permute-start(bf16[2,256,128]{2,1,0:T(8,128)(2,1)S(1)} %get-tuple-element.55), channel_id=1, source_target_pairs={{1,0},{5,4},{2,1},{6,5},{3,2},{7,6},{9,8},{13,12},{10,9},{14,13},{... | collective-permute-start | bytes 393224 | tf_op jit(solution)/shard_map/ppermute | solution.py:366
  61.3 7.7 %collective-permute-start.12 = (f32[8,512]{1,0:T(8,128)S(1)}, f32[8,512]{1,0:T(8,128)S(1)}, u32[]{:S(2)}, u32[]{:S(2)}) collective-permute-start(f32[8,512]{1,0:T(8,128)S(1)} %row_totals.4.refs_11_), channel_id=1, source_target_pairs={{4,0},{5,1},{6,2},{7,3},{0,4},{1,5},{2,6},{3,7},{12,8},{13,9},{14,... | collective-permute-start | bytes 49160 | tf_op jit(solution)/shard_map/ppermute | solution.py:386
  65.0 7.7 %collective-permute-start.6 = (f32[8,512]{1,0:T(8,128)S(1)}, f32[8,512]{1,0:T(8,128)S(1)}, u32[]{:S(2)}, u32[]{:S(2)}) collective-permute-start(f32[8,512]{1,0:T(8,128)S(1)} %row_totals.3.refs_11_), channel_id=1, source_target_pairs={{4,0},{5,1},{6,2},{7,3},{0,4},{1,5},{2,6},{3,7},{12,8},{13,9},{14,... | collective-permute-start | bytes 49160 | tf_op jit(solution)/shard_map/ppermute | solution.py:386
  66.8 18.0 %collective-permute-start.21 = (bf16[2,256,128]{2,1,0:T(8,128)(2,1)S(1)}, bf16[2,256,128]{2,1,0:T(8,128)(2,1)S(1)}, u32[]{:S(2)}, u32[]{:S(2)}) collective-permute-start(bf16[2,256,128]{2,1,0:T(8,128)(2,1)S(1)} %get-tuple-element.56), channel_id=1, source_target_pairs={{0,1},{4,5},{1,2},{5,6},{2,3},{6,7},{8,9},{12,13},{9,10},{13,14},{... | collective-permute-start | bytes 393224 | tf_op jit(solution)/shard_map/ppermute | solution.py:366
  69.0 17.6 %collective-permute-start.22 = (bf16[2,256,128]{2,1,0:T(8,128)(2,1)S(1)}, bf16[2,256,128]{2,1,0:T(8,128)(2,1)S(1)}, u32[]{:S(2)}, u32[]{:S(2)}) collective-permute-start(bf16[2,256,128]{2,1,0:T(8,128)(2,1)S(1)} %get-tuple-element.57), channel_id=1, source_target_pairs={{0,8},{8,0},{1,9},{9,1},{2,10},{10,2},{3,11},{11,3},{4,12},{12,4},... | collective-permute-start | bytes 393224 | tf_op jit(solution)/shard_map/ppermute | solution.py:367
  72.7 14.2 %collective-permute-start.13 = (bf16[256,256]{1,0:T(8,128)(2,1)S(1)}, bf16[256,256]{1,0:T(8,128)(2,1)S(1)}, u32[]{:S(2)}, u32[]{:S(2)}) collective-permute-start(bf16[256,256]{1,0:T(8,128)(2,1)S(1)} %get-tuple-element.44), channel_id=1, source_target_pairs={{0,4},{1,5},{2,6},{3,7},{4,0},{5,1},{6,2},{7,3},{8,12},{9,13},{10,... | collective-permute-start | bytes 393224 | tf_op jit(solution)/shard_map/ppermute | solution.py:365
  75.7 12.1 %collective-permute-start.14 = (bf16[2,256,128]{2,1,0:T(8,128)(2,1)S(1)}, bf16[2,256,128]{2,1,0:T(8,128)(2,1)S(1)}, u32[]{:S(2)}, u32[]{:S(2)}) collective-permute-start(bf16[2,256,128]{2,1,0:T(8,128)(2,1)S(1)} %get-tuple-element.47), channel_id=1, source_target_pairs={{1,0},{5,4},{2,1},{6,5},{3,2},{7,6},{9,8},{13,12},{10,9},{14,13},{... | collective-permute-start | bytes 393224 | tf_op jit(solution)/shard_map/ppermute | solution.py:366
  78.5 14.1 %collective-permute-start.15 = (bf16[2,256,128]{2,1,0:T(8,128)(2,1)S(1)}, bf16[2,256,128]{2,1,0:T(8,128)(2,1)S(1)}, u32[]{:S(2)}, u32[]{:S(2)}) collective-permute-start(bf16[2,256,128]{2,1,0:T(8,128)(2,1)S(1)} %get-tuple-element.48), channel_id=1, source_target_pairs={{0,1},{4,5},{1,2},{5,6},{2,3},{6,7},{8,9},{12,13},{9,10},{13,14},{... | collective-permute-start | bytes 393224 | tf_op jit(solution)/shard_map/ppermute | solution.py:366
  84.8 9.7 %collective-permute-start.16 = (bf16[2,256,128]{2,1,0:T(8,128)(2,1)S(1)}, bf16[2,256,128]{2,1,0:T(8,128)(2,1)S(1)}, u32[]{:S(2)}, u32[]{:S(2)}) collective-permute-start(bf16[2,256,128]{2,1,0:T(8,128)(2,1)S(1)} %get-tuple-element.49), channel_id=1, source_target_pairs={{0,8},{8,0},{1,9},{9,1},{2,10},{10,2},{3,11},{11,3},{4,12},{12,4},... | collective-permute-start | bytes 393224 | tf_op jit(solution)/shard_map/ppermute | solution.py:367
  86.6 8.0 %collective-permute-start.10 = (bf16[2,256,128]{2,1,0:T(8,128)(2,1)S(1)}, bf16[2,256,128]{2,1,0:T(8,128)(2,1)S(1)}, u32[]{:S(2)}, u32[]{:S(2)}) collective-permute-start(bf16[2,256,128]{2,1,0:T(8,128)(2,1)S(1)} %get-tuple-element.41), channel_id=1, source_target_pairs={{0,8},{8,0},{1,9},{9,1},{2,10},{10,2},{3,11},{11,3},{4,12},{12,4},... | collective-permute-start | bytes 393224 | tf_op jit(solution)/shard_map/ppermute | solution.py:367
  86.9 7.6 %collective-permute-start.7 = (bf16[256,256]{1,0:T(8,128)(2,1)S(1)}, bf16[256,256]{1,0:T(8,128)(2,1)S(1)}, u32[]{:S(2)}, u32[]{:S(2)}) collective-permute-start(bf16[256,256]{1,0:T(8,128)(2,1)S(1)} %get-tuple-element.36), channel_id=1, source_target_pairs={{0,4},{1,5},{2,6},{3,7},{4,0},{5,1},{6,2},{7,3},{8,12},{9,13},{10,... | collective-permute-start | bytes 393224 | tf_op jit(solution)/shard_map/ppermute | solution.py:365
  87.8 8.3 %collective-permute-start.8 = (bf16[2,256,128]{2,1,0:T(8,128)(2,1)S(1)}, bf16[2,256,128]{2,1,0:T(8,128)(2,1)S(1)}, u32[]{:S(2)}, u32[]{:S(2)}) collective-permute-start(bf16[2,256,128]{2,1,0:T(8,128)(2,1)S(1)} %get-tuple-element.39), channel_id=1, source_target_pairs={{1,0},{5,4},{2,1},{6,5},{3,2},{7,6},{9,8},{13,12},{10,9},{14,13},{... | collective-permute-start | bytes 393224 | tf_op jit(solution)/shard_map/ppermute | solution.py:366
  92.6 7.8 %collective-permute-start.9 = (bf16[2,256,128]{2,1,0:T(8,128)(2,1)S(1)}, bf16[2,256,128]{2,1,0:T(8,128)(2,1)S(1)}, u32[]{:S(2)}, u32[]{:S(2)}) collective-permute-start(bf16[2,256,128]{2,1,0:T(8,128)(2,1)S(1)} %get-tuple-element.40), channel_id=1, source_target_pairs={{0,1},{4,5},{1,2},{5,6},{2,3},{6,7},{8,9},{12,13},{9,10},{13,14},{... | collective-permute-start | bytes 393224 | tf_op jit(solution)/shard_map/ppermute | solution.py:366

commit v2 on v1

v2 whole, which is shorter than its diff:
```python
import functools
import math

import jax
import jax.numpy as jnp
from jax import lax
from jax.experimental import pallas as pl
from jax.experimental.pallas import tpu as pltpu
from jax.sharding import PartitionSpec as P

NCT = 4
LOG2E = 1.4426950408889634
DEAD = -1e30
VMEM_LIMIT = 24 * 1024 * 1024

SMEM = pl.BlockSpec(memory_space=pltpu.SMEM)
NT = (((1,), (1,)), ((), ()))
NN = (((1,), (0,)), ((), ()))
TN = (((0,), (0,)), ((), ()))


def dot(a, b, dims):
    return lax.dot_general(a, b, dims, preferred_element_type=jnp.float32)


def swaps_along(size):
    return [
        [(p, p + 1) for p in range(first, size - 1, 2)] for first in (0, 1) if first + 1 < size
    ]


def both_ways(pairs):
    return [(a, b) for a, b in pairs] + [(b, a) for a, b in pairs]


def row_route(swap, col_count):
    return [
        (a * col_count + col, b * col_count + col)
        for a, b in both_ways(swap)
        for col in range(col_count)
    ]


def col_route(swap, row_count, col_count):
    return [
        (row * col_count + a, row * col_count + b)
        for a, b in both_ways(swap)
        for row in range(row_count)
    ]


def partner(at, place, size):
    other = jnp.where(lax.rem(place, 2) == at, place + 1, place - 1)
    return jnp.clip(other, 0, size - 1), (other >= 0) & (other < size)


def table_rows(plan):
    cols = 1
    frames = cols + plan.nc
    rows = frames + plan.nf
    flips = rows + plan.nr
    return cols, frames, rows, flips


def table_shape(plan):
    rows = table_rows(plan)[-1] + plan.pairs
    return jax.ShapeDtypeStruct((-(-rows // 8) * 8, plan.hd), jnp.int32)


def prepare_kernel(plan, offsets_ref, counts_ref, q_ref, k_ref, v_ref, *refs):
    table_ref, plane_ref, across_ref, q_out_ref = refs
    hd = plan.hd
    frame, spot = lax.axis_index("frame"), lax.axis_index("tile")
    row, col = lax.div(spot, plan.col_count), lax.rem(spot, plan.col_count)
    entries = [counts_ref[frame, spot]]
    for at in range(plan.nc):
        other, there = partner(at, col, plan.col_count)
        entries.append(jnp.where(there, counts_ref[frame, row * plan.col_count + other], 0))
    for at in range(plan.nf):
        other, there = partner(at, frame, plan.frame_count)
        entries.append(jnp.where(there, counts_ref[other, spot], 0))
    for at in range(plan.nr):
        other, there = partner(at, row, plan.row_count)
        entries.append(jnp.where(there, counts_ref[frame, other * plan.col_count + col], 0))
    for pair in range(plan.pairs):
        hits = jnp.int32(0)
        for slot in range(offsets_ref.shape[1]):
            hits = hits | jnp.abs(offsets_ref[2 * pair, slot, 0])
        flip = jnp.where(hits != 0, 1, 0).astype(jnp.int32)
        entries.append(flip)
        first = pl.ds(pl.multiple_of(2 * pair * hd + flip * hd, hd), hd)
        second = pl.ds(pl.multiple_of(2 * pair * hd + (1 - flip) * hd, hd), hd)
        at = pl.ds(pair * hd, hd)
        for i, ref in enumerate((k_ref, v_ref)):
            plane_ref[i, :, at] = ref[:, first]
            across_ref[i, :, at] = ref[:, second]
        q_out_ref[:, pl.ds(2 * pair * hd, hd)] = q_ref[:, first]
        q_out_ref[:, pl.ds((2 * pair + 1) * hd, hd)] = q_ref[:, second]
    entries += [jnp.int32(0)] * (table_ref.shape[0] - len(entries))
    for at, entry in enumerate(entries):
        table_ref[at : at + 1, :] = jnp.full((1, hd), entry, jnp.int32)


def gather_kernel(plan, swap, table_ref, grad_ref, *refs):
    refs = list(refs)
    if swap is not None:
        q_ref, q_out_ref = refs.pop(0), refs.pop()
    got_refs, out_ref = refs[:-1], refs[-1]
    section = lax.axis_index("section")
    sections = len(refs)
    _, _, row_rows, flip_rows = table_rows(plan)
    at = 0 if swap is None else row_rows + swap
    count = table_ref[at : at + 1, :]
    rows, width, hd = grad_ref.shape[0], out_ref.shape[1], plan.hd
    at_rows = lax.broadcasted_iota(jnp.int32, (rows, hd), 0)
    for k in range(sections):
        holder = lax.rem(section + sections - k, sections)
        live = at_rows + holder * rows < count
        start = pl.multiple_of(holder * rows, rows)
        for pair in range(plan.pairs):
            heads = []
            for head in (2 * pair, 2 * pair + 1):
                if k == 0:
                    at = pl.multiple_of(section * width + head * hd, hd)
                    part = grad_ref[:, pl.ds(at, hd)]
                else:
                    part = got_refs[k - 1][:, pl.ds(head * hd, hd)]
                heads.append(jnp.where(live, part.astype(jnp.float32), 0.0))
            for i, part in enumerate(in_order(table_ref, flip_rows + pair, *heads)):
                part = part.astype(out_ref.dtype)
                out_ref[pl.ds(start, rows), pl.ds((2 * pair + i) * hd, hd)] = part


    if swap is not None:
        for pair in range(plan.pairs):
            cols = [pl.ds((2 * pair + i) * hd, hd) for i in (0, 1)]
            heads = [q_ref[:, at].astype(jnp.float32) for at in cols]
            for at, part in zip(cols, in_order(table_ref, flip_rows + pair, *heads)):
                q_out_ref[:, at] = part.astype(q_out_ref.dtype)


def in_order(table_ref, row, a, b):
    flip = jnp.broadcast_to(table_ref[row : row + 1, :], a.shape) != 0
    return jnp.where(flip, b, a), jnp.where(flip, a, b)


class Window:
    def __init__(self, plan, refs, own=True, far=True):
        refs = list(refs)
        self.plan = plan
        take = lambda n: [refs.pop(0) for _ in range(n)]
        (self.table,) = take(1)
        self.q = take((1 if own else 0) + (plan.nr if far else 0))
        self.grad = take((1 if own else 0) + (plan.nr if far else 0))
        self.kv = [take(1 + plan.nc), take(1 + plan.nf)]
        self.rest = refs

    def heads(self, pair):
        plan = self.plan
        hd, tile = plan.hd, plan.tile
        cols, frames, _, _ = table_rows(plan)
        at_rows = lax.broadcasted_iota(jnp.int32, (tile, hd), 0)
        near_at = pl.ds(pair * hd, hd)
        for kind, first in ((0, cols), (1, frames)):
            q = [ref[:, pl.ds((2 * pair + kind) * hd, hd)] for ref in self.q]
            grad = [ref[:, pl.ds((2 * pair + kind) * hd, hd)] for ref in self.grad]
            slots = []
            for at, ref in enumerate(self.kv[kind]):
                row = 0 if at == 0 else first + at - 1
                bias = jnp.where(at_rows < self.table[row : row + 1, :], 0.0, DEAD)
                bias = jnp.concatenate([bias] * (len(q) * tile // hd), axis=1)
                slots.append((ref[0, :, near_at], ref[1, :, near_at], bias))
            yield kind, jnp.concatenate(q, axis=0), jnp.concatenate(grad, axis=0), slots


def merge(parts):
    top = functools.reduce(jnp.maximum, [m for m, _, _ in parts])
    weights = [jnp.exp2(m - top) for m, _, _ in parts]
    total = sum(w * l for w, (_, l, _) in zip(weights, parts))
    cross = sum(w * t for w, (_, _, t) in zip(weights, parts))
    return top, total, cross


def row_stats(window, pair):
    rows = []
    for kind, q, grad, slots in window.heads(pair):
        parts = []
        for key, value, bias in slots:
            scores = dot(key, q, NT) * window.plan.factor + bias
            top = jnp.max(scores, axis=0, keepdims=True)
            weight = jnp.exp2(scores - top)
            total = jnp.sum(weight, axis=0, keepdims=True)
            cross = jnp.sum(weight * dot(value, grad, NT), axis=0, keepdims=True)
            parts.append((top, total, cross))
        rows += list(merge(parts))
        rows.append(jnp.zeros_like(rows[0]))
    return jnp.concatenate(rows, axis=0)


def own_stats_kernel(plan, *refs):
    pairs = range(plan.pairs)
    window = Window(plan, refs, far=False)
    (out_ref,) = window.rest
    for pair in pairs:
        out_ref[pair] = row_stats(window, pair)


def far_stats_kernel(plan, *refs):
    window = Window(plan, refs, own=False)
    own_ref, out_ref = window.rest
    for at, pair in enumerate(plan.group):
        out_ref[at, :, : plan.tile] = own_ref[pair]
        out_ref[at, :, plan.tile :] = row_stats(window, pair)


def grads_kernel(plan, *refs):
    window = Window(plan, refs)
    rest = list(window.rest)
    take = lambda n: [rest.pop(0) for _ in range(n)]
    stats_refs = take(plan.n_stats)
    dq_refs = take(1 + plan.nr)
    own_refs = take(2)
    near_refs = [take(plan.nc), take(plan.nf)]
    tile, hd = plan.tile, plan.hd
    for behind, pair in enumerate(plan.part):
        stats = [ref[plan.group.index(pair)] for ref in stats_refs]
        if plan.n_stats == 2:
            stats[1] = jnp.concatenate([stats[1][:, tile:], stats[1][:, :tile]], axis=1)
        near_at = pl.ds(behind * hd, hd)
        for kind, q, grad, slots in window.heads(pair):
            base = 4 * kind
            cols = pl.ds((2 * behind + kind) * hd, hd)
            parts = [tuple(s[base + i : base + i + 1, :] for i in range(3)) for s in stats]
            top, total, cross = merge(parts)
            log_total = top + jnp.log(total) * LOG2E
            row_dot = cross / total
            query_grad = None
            for at, (key, value, bias) in enumerate(slots):
                scores = dot(key, q, NT) * plan.factor + bias
                softmax = jnp.exp2(scores - log_total)
                grad_softmax = dot(value, grad, NT)
                grad_scores = (softmax * (grad_softmax - row_dot)).astype(jnp.bfloat16)
                dk = dot(grad_scores, q, NN) * plan.scale
                dv = dot(softmax.astype(jnp.bfloat16), grad, NN)
                term = dot(key, grad_scores, TN)
                query_grad = term if query_grad is None else query_grad + term
                for i, out in enumerate((dk, dv)):
                    if at == 0:
                        own_refs[i][:, cols] = out
                    else:
                        near_refs[kind][at - 1][i, :, near_at] = out.astype(jnp.bfloat16)
            query_grad = jnp.transpose(query_grad * plan.scale)
            for at, ref in enumerate(dq_refs):
                ref[:, cols] = query_grad[at * tile : (at + 1) * tile].astype(ref.dtype)


def finish_kernel(plan, parts, table_ref, *refs):
    refs = list(refs)
    take = lambda n: [refs.pop(0) for _ in range(n)]
    hd = plan.hd
    flip_rows = table_rows(plan)[-1]
    per_part = [(part, take(1 + plan.nr), take(2), take(plan.nc), take(plan.nf)) for part in parts]
    dq_ref, dk_ref, dv_ref = refs

    def put(out_ref, pair, kinds):
        for i, part in enumerate(in_order(table_ref, flip_rows + pair, *kinds)):
            out_ref[:, pl.ds((2 * pair + i) * hd, hd)] = part.astype(out_ref.dtype)

    for part, dq, own, *near in per_part:
        for behind, pair in enumerate(part):
            near_at = pl.ds(behind * hd, hd)
            cols = [pl.ds((2 * behind + kind) * hd, hd) for kind in (0, 1)]
            put(dq_ref, pair, [sum(ref[:, at].astype(jnp.float32) for ref in dq) for at in cols])
            for i, out in enumerate((dk_ref, dv_ref)):
                kinds = []
                for kind in (0, 1):
                    total = own[i][:, cols[kind]]
                    for ref in near[kind]:
                        total = total + ref[i, :, near_at].astype(jnp.float32)
                    kinds.append(total)
                put(out, pair, kinds)


class Plan:
    pass


def split_pairs(pairs):
    return [list(range(pairs))]


def params():
    return pltpu.CompilerParams(vmem_limit_bytes=VMEM_LIMIT)


def local(queries, key_rows, value_rows, grad_rows, offsets, counts):
    q, k, v, grad = queries[0, 0], key_rows[0, 0], value_rows[0, 0], grad_rows[0, 0]
    tile, width = q.shape
    heads = offsets.shape[0]
    pairs = heads // 2
    hd = width // heads
    sections = lax.axis_size("section")
    frame_count = lax.axis_size("frame")
    col_count = NCT
    row_count = lax.axis_size("tile") // col_count

    plan = Plan()
    plan.tile, plan.hd, plan.col_count = tile, hd, col_count
    plan.scale = 1.0 / math.sqrt(hd)
    plan.factor = plan.scale * LOG2E
    row_swaps = swaps_along(row_count)
    col_swaps = swaps_along(col_count)
    frame_swaps = swaps_along(frame_count)
    plan.nr, plan.nc, plan.nf = len(row_swaps), len(col_swaps), len(frame_swaps)
    plan.frame_count = frame_count
    row_routes = [row_route(swap, col_count) for swap in row_swaps]
    col_routes = [col_route(swap, row_count, col_count) for swap in col_swaps]
    frame_routes = [both_ways(swap) for swap in frame_swaps]

    def from_rows(x):
        return [lax.ppermute(x, "tile", route) for route in row_routes]

    vm = pl.BlockSpec(memory_space=pltpu.VMEM)
    plan.row_count = row_count

    plan.pairs = pairs

    def call(kernel, name, out_shape, flops, *operands, scalars=()):
        many = isinstance(out_shape, list)
        return pl.pallas_call(
            kernel,
            out_shape=out_shape,
            in_specs=[SMEM] * len(scalars) + [vm] * len(operands),
            out_specs=[vm] * len(out_shape) if many else vm,
            compiler_params=params(),
            cost_estimate=pl.CostEstimate(
                flops=flops, bytes_accessed=1 << 20, transcendentals=0
            ),
            name=name,
        )(*scalars, *operands)

    low = jax.ShapeDtypeStruct((tile, width), jnp.bfloat16)

    far_raw = from_rows(grad)
    far_q_raw = from_rows(q)
    packed = jax.ShapeDtypeStruct((2, tile, pairs * hd), jnp.bfloat16)
    table, plane_kv, across_kv, own_q = call(
        functools.partial(prepare_kernel, plan),
        "prepare",
        [table_shape(plan), packed, packed, low],
        0,
        *(q, k, v),
        scalars=(offsets, counts),
    )
    section = lax.axis_index("section")

    def all_slots(raw, swap, *queries):
        got = []
        for shift in range(1, sections):
            target = lax.rem(section + shift, sections)
            part = lax.dynamic_slice_in_dim(raw, target * width, width, 1)
            route = [(i, (i + shift) % sections) for i in range(sections)]
            got.append(lax.ppermute(part, "section", route))
        return call(
            functools.partial(gather_kernel, plan, swap),
            "gather_grad",
            [low] * (1 + len(queries)),
            0,
            *(table, raw, *queries, *got),
        )

    (own_grad,) = all_slots(grad, None)
    near_plane = [lax.ppermute(plane_kv, "tile", route) for route in col_routes]
    near_across = [lax.ppermute(across_kv, "frame", route) for route in frame_routes]
    kv = [plane_kv, *near_plane, across_kv, *near_across]
    n_near = plan.nc + plan.nf
    far = [all_slots(raw, swap, far_q_raw[swap]) for swap, raw in enumerate(far_raw)]
    far_grad, far_q = [pair[0] for pair in far], [pair[1] for pair in far]

    nq = 1 + plan.nr
    quarter = 2 * 2 * (2 + n_near) * tile * tile * hd

    own_stats = call(
        functools.partial(own_stats_kernel, plan),
        "own_totals",
        jax.ShapeDtypeStruct((pairs, 8, tile), jnp.float32),
        quarter * pairs,
        *(table, own_q, own_grad, *kv),
    )
    parts = split_pairs(pairs)
    plan.group = list(range(pairs))
    stats = call(
        functools.partial(far_stats_kernel, plan),
        "far_totals",
        jax.ShapeDtypeStruct((pairs, 8, nq * tile), jnp.float32),
        quarter * plan.nr * pairs,
        *(table, *far_q, *far_grad, *kv, own_stats),
    )
    all_stats = share_stats(stats, row_routes, tile)
    plan.n_stats = len(all_stats)
    done = []
    for part in parts:
        plan_m = Plan()
        plan_m.__dict__.update(plan.__dict__)
        plan_m.part = part
        part_low = jax.ShapeDtypeStruct((tile, len(part) * 2 * hd), jnp.bfloat16)
        part_f32 = jax.ShapeDtypeStruct((tile, len(part) * 2 * hd), jnp.float32)
        near_out = jax.ShapeDtypeStruct((2, tile, len(part) * hd), jnp.bfloat16)
        outs = call(
            functools.partial(grads_kernel, plan_m),
            "pair_grads",
            [part_f32] + [part_low] * plan.nr + [part_f32] * 2 + [near_out] * n_near,
            quarter * nq * 5 // 2 * len(part),
            *(table, own_q, *far_q, own_grad, *far_grad, *kv, *all_stats),
        )
        plane_out, across_out = outs[nq + 2 : nq + 2 + plan.nc], outs[nq + 2 + plan.nc :]
        done += [outs[0]]
        done += [lax.ppermute(x, "tile", r) for x, r in zip(outs[1:nq], row_routes)]
        done += outs[nq : nq + 2]
        done += [lax.ppermute(x, "tile", r) for x, r in zip(plane_out, col_routes)]
        done += [lax.ppermute(x, "frame", r) for x, r in zip(across_out, frame_routes)]

    dq, dk, dv = call(
        functools.partial(finish_kernel, plan, parts), "add_terms", [low] * 3, 0, table, *done
    )
    return dq[None, None], dk[None, None], dv[None, None]


def share_stats(stats, row_routes, tile):
    if len(row_routes) == 0:
        return [stats]
    if len(row_routes) == 1:
        return [stats, lax.ppermute(stats, "tile", row_routes[0])]
    terms = [stats[:, :, :tile]]
    for at, route in enumerate(row_routes):
        part = stats[:, :, (at + 1) * tile : (at + 2) * tile]
        terms.append(lax.ppermute(part, "tile", route))
    merged = []
    for base in (0, 4):
        parts = [(t[:, base], t[:, base + 1], t[:, base + 2]) for t in terms]
        parts = [(jnp.where(l > 0, m, DEAD), l, t) for m, l, t in parts]
        merged += list(merge(parts))
        merged.append(jnp.ones_like(merged[0]))
    totals = jnp.stack(merged, axis=1)
    shared = [totals] + [lax.ppermute(totals, "tile", route) for route in row_routes]
    return [jnp.concatenate(shared, axis=2)]


def solution(mesh):
    return jax.shard_map(
        local,
        mesh=mesh,
        in_specs=(
            P("frame", "tile", None, "section"),
            P("frame", "tile", None, "section"),
            P("frame", "tile", None, "section"),
            P("frame", "tile", "section", None),
            P("section", None, None),
            P(),
        ),
        out_specs=(
            P("frame", "tile", None, "section"),
            P("frame", "tile", None, "section"),
            P("frame", "tile", None, "section"),
        ),
        check_vma=False,
    )
```

time: 104 us -> 74.6 us (0.72)
  starting transfers between devices: 42.3 us -> 12.4 us
  Pallas kernels: 22.1 us -> 13 us
  waiting for transfers between devices: 34.8 us -> 42.8 us
  local copies, waits for them, and re-layouts: 2.85 us -> 4.52 us
    ppermute x13 -> x6, starting transfers between devices: 24.9 us -> 4.39 us  [the longest x2 2.54 us: local(): done += [lax.ppermute(x, 'tile', r) for x, r in zip(plane_out, col_routes)]]
    pallas_call x9 -> x7, Pallas kernels: 22.1 us -> 13 us  [call(): pl.pallas_call(kernel, out_shape=out_shape, in_specs=[SMEM] * len(scalars...]
    ppermute x2, waiting for transfers between devices: 0.01 us -> 8.43 us  [local(): near_plane = [lax.ppermute(plane_kv, 'tile', route) for route in col_routes]]
    ppermute x13 -> x6, waiting for transfers between devices: 7.25 us -> 14.6 us  [the longest x1 8.35 us: local(): done += [lax.ppermute(x, 'tile', r) for x, r in zip(outs[1:nq], row_routes)]]
    ppermute x4 -> x2, waiting for transfers between devices: 20.9 us -> 14.8 us  [from_rows(): return [lax.ppermute(x, 'tile', route) for route in row_routes]]
    ppermute x2, starting transfers between devices: 6.74 us -> 3.36 us  [local(): near_plane = [lax.ppermute(plane_kv, 'tile', route) for route in col_routes]]
    ppermute x3 -> x1, starting transfers between devices: 3.15 us -> 0.07 us  [share_stats(): return [stats, lax.ppermute(stats, 'tile', row_routes[0])]]
    ppermute x4 -> x2, starting transfers between devices: 5.92 us -> 2.99 us  [from_rows(): return [lax.ppermute(x, 'tile', route) for route in row_routes]]
  transfers between devices with their start and end apart: 23 -> 12, of which waited for: 5 -> 6; matrix products, arithmetic and copies ran while one was open for 0% -> 1% of each run, Pallas kernels for 17% -> 5%
where the time goes in v2:
time: 74.6 us; the launch traced here: 73.5 us
  waiting for transfers between devices  42.8 us (57%)
  Pallas kernels  13 us (17%)
  starting transfers between devices  12.4 us (17%)
  local copies, waits for them, and re-layouts  4.52 us (6%)
  between operations  0.76 us (1%)
    ppermute x2, waiting for transfers between devices, from_rows(): return [lax.ppermute(x, 'tile', route) for route in row_routes]  14.8 us
    pallas_call x7, Pallas kernels, call(): pl.pallas_call(kernel, out_shape=out_shape, in_specs=[SMEM] * len(scalars...  13 us
    ppermute x2, waiting for transfers between devices, local(): near_plane = [lax.ppermute(plane_kv, 'tile', route) for route in col_routes]  8.43 us
    ppermute x1, waiting for transfers between devices, local(): done += [lax.ppermute(x, 'tile', r) for x, r in zip(outs[1:nq], row_routes)]  8.35 us
    ppermute x1, waiting for transfers between devices, share_stats(): return [stats, lax.ppermute(stats, 'tile', row_routes[0])]  4.98 us
    ppermute x2, waiting for transfers between devices, local(): done += [lax.ppermute(x, 'tile', r) for x, r in zip(plane_out, col_routes)]  4.84 us
    unnamed x11, local copies, waits for them, and re-layouts  4.49 us
    ppermute x2, starting transfers between devices, local(): near_plane = [lax.ppermute(plane_kv, 'tile', route) for route in col_routes]  3.36 us
  transfers between devices with their start and end apart: 12, of which 6 were waited for; matrix products, arithmetic and copies ran while one was open for 1% of the time, Pallas kernels for 5%

profile of v2, /device:TPU:24, one launch (start us, length us, event | category | flops | bytes accessed | tf_op | source)
XLA Modules:
  0.0 73.5 jit_solution(12376438891666198992)
XLA Ops:
  0.6 0.4 collective-permute-start
  1.0 2.6 %collective-permute-start.1 = (bf16[256,768]{1,0:T(8,128)(2,1)}, bf16[256,768]{1,0:T(8,128)(2,1)S(1)}, u32[]{:S(2)}, u32[]{:S(2)}) collective-permute-start(bf16[256,768]{1,0:T(8,128)(2,1)} %bitcast.13), channel_id=1, source_target_pairs={{0,4},{1,5},{2,6},{3,7},{4,0},{5,1},{6,2},{7,3},{8,12},{9,13},{10,... | collective-permute-start | bytes 1179656 | tf_op jit(solution)/shard_map/ppermute | solution.py:321
  3.6 0.8 %copy.9.offsets_ref = s32[6,9,3]{2,1,0:T(8,128)S(1)} copy(s32[6,9,3]{1,2,0:T(4,128)} %param.10) | data formatting | bytes 1296 | tf_op args[4]
  4.4 0.0 copy-start.4
  4.4 0.7 copy-done.4
  5.1 0.0 copy-start.1
  5.1 1.0 %copy-done.1 = bf16[1,1,256,768]{3,2,1,0:T(8,128)(2,1)S(1)} copy-done((bf16[1,1,256,768]{3,2,1,0:T(8,128)(2,1)S(1)}, bf16[1,1,256,768]{3,2,1,0:T(8,128)(2,1)}, u32[]{:S(2)}) %copy-start.1) | copy-done | bytes 393240
  6.1 0.0 copy-start.2
  6.1 1.0 %copy-done.2 = bf16[1,1,256,768]{3,2,1,0:T(8,128)(2,1)S(1)} copy-done((bf16[1,1,256,768]{3,2,1,0:T(8,128)(2,1)S(1)}, bf16[1,1,256,768]{3,2,1,0:T(8,128)(2,1)}, u32[]{:S(2)}) %copy-start.2) | copy-done | bytes 393240
  7.1 0.0 copy-start.3
  7.1 1.0 %copy-done.3 = bf16[1,1,256,768]{3,2,1,0:T(8,128)(2,1)S(1)} copy-done((bf16[1,1,256,768]{3,2,1,0:T(8,128)(2,1)S(1)}, bf16[1,1,256,768]{3,2,1,0:T(8,128)(2,1)}, u32[]{:S(2)}) %copy-start.3) | copy-done | bytes 393240
  8.1 0.0 copy-start
  8.1 1.6 %prepare.1 = (s32[8,128]{1,0:T(8,128)S(1)}, bf16[2,256,384]{2,1,0:T(8,128)(2,1)S(1)}, bf16[2,256,384]{2,1,0:T(8,128)(2,1)S(1)}, bf16[256,768]{1,0:T(8,128)(2,1)S(1)}) custom-call(s32[6,9,3]{2,1,0:T(8,128)S(1)} %copy.9.offsets_ref, s32[2,8]{1,0:T(2,128)S(1)} %copy-done.4, bf16[256,768]{1,0:T(8,128)(2,1)S(1)} %bitcast.14, bf16[256,768]{1,0:T(8,128)(2,1)S(1)} %bitcast.11, ...), custom_call_target="tpu_custom_call" | custom-call | bytes 1048576 | tf_op jit(solution)/shard_map/prepare/pallas_call | solution.py:330
  9.8 3.3 %collective-permute-start.5 = (bf16[2,256,384]{2,1,0:T(8,128)(2,1)S(1)}, bf16[2,256,384]{2,1,0:T(8,128)(2,1)S(1)}, u32[]{:S(2)}, u32[]{:S(2)}) collective-permute-start(bf16[2,256,384]{2,1,0:T(8,128)(2,1)S(1)} %get-tuple-element.23.refs_3_.refs_5_), channel_id=1, source_target_pairs={{1,2},{5,6},{2,1},{6,5},{9,10},{13,14},{10,9},{14,13},{17,18},{21,... | collective-permute-start | bytes 1179656 | tf_op jit(solution)/shard_map/ppermute | solution.py:373
  13.1 0.1 collective-permute-start.4
  13.1 1.6 %collective-permute-start.6 = (bf16[2,256,384]{2,1,0:T(8,128)(2,1)S(1)}, bf16[2,256,384]{2,1,0:T(8,128)(2,1)S(1)}, u32[]{:S(2)}, u32[]{:S(2)}) collective-permute-start(bf16[2,256,384]{2,1,0:T(8,128)(2,1)S(1)} %get-tuple-element.24.refs_6_.refs_8_), channel_id=1, source_target_pairs={{0,8},{8,0},{1,9},{9,1},{2,10},{10,2},{3,11},{11,3},{4,12},{12,4},... | collective-permute-start | bytes 1179656 | tf_op jit(solution)/shard_map/ppermute | solution.py:374
  14.7 0.0 copy-done
  14.7 14.8 %collective-permute-done.grad_ref = bf16[128,1536]{1,0:T(8,128)(2,1)S(1)} collective-permute-done((bf16[128,1536]{1,0:T(8,128)(2,1)}, bf16[128,1536]{1,0:T(8,128)(2,1)S(1)}, u32[]{:S(2)}, u32[]{:S(2)}) %collective-permute-start) | collective-permute-done | bytes 393248 | tf_op jit(solution)/shard_map/ppermute | solution.py:321
  29.5 0.0 collective-permute-start.3
  29.5 1.4 %collective-permute-done.3.refs_0_ = bf16[128,768]{1,0:T(8,128)(2,1)S(1)} collective-permute-done((bf16[128,768]{1,0:T(8,128)(2,1)S(1)}, bf16[128,768]{1,0:T(8,128)(2,1)S(1)}, u32[]{:S(2)}, u32[]{:S(2)}) %collective-permute-start.3) | collective-permute-done | bytes 196640 | tf_op jit(solution)/shard_map/ppermute | solution.py:363
  30.9 0.1 collective-permute-start.2
  31.1 0.1 gather_grad.3.refs_2_.refs_3_
  31.2 0.0 collective-permute-done.6.refs_7_.refs_9_
  31.2 8.4 %collective-permute-done.5.refs_5_.refs_7_ = bf16[2,256,384]{2,1,0:T(8,128)(2,1)S(1)} collective-permute-done((bf16[2,256,384]{2,1,0:T(8,128)(2,1)S(1)}, bf16[2,256,384]{2,1,0:T(8,128)(2,1)S(1)}, u32[]{:S(2)}, u32[]{:S(2)}) %collective-permute-start.5) | collective-permute-done | bytes 393248 | tf_op jit(solution)/shard_map/ppermute | solution.py:373
  39.6 0.0 collective-permute-done.4.refs_4_.refs_6_
  39.6 1.8 %own_totals.1.refs_8_ = f32[3,8,256]{2,1,0:T(8,128)S(1)} custom-call(s32[8,128]{1,0:T(8,128)S(1)} %get-tuple-element.19.table_ref.refs_0_, bf16[256,768]{1,0:T(8,128)(2,1)S(1)} %get-tuple-element.20.refs_1_, bf16[256,768]{1,0:T(8,128)(2,1)S(1)} %gather_grad.3.refs_2_.refs_3_, bf16[2,256,384]{2,1,0:T(8,128)(2,1)S(1)} %get-tuple-element.23.refs_3_.refs_5_, ...), custom_call_target="tpu_custom_call" | custom-call | flops 503316480 | bytes 1048576 | tf_op jit(solution)/shard_map/own_totals/pallas_call | solution.py:330
  41.4 0.0 collective-permute-done.1.refs_0_
  41.4 0.0 collective-permute-done.2.refs_1_
  41.5 0.2 gather_grad.2
  41.7 1.8 %far_totals.1.refs_10_ = f32[3,8,512]{2,1,0:T(8,128)S(1)} custom-call(s32[8,128]{1,0:T(8,128)S(1)} %get-tuple-element.19.table_ref.refs_0_, bf16[256,768]{1,0:T(8,128)(2,1)S(1)} %get-tuple-element.21.refs_1_.refs_2_, bf16[256,768]{1,0:T(8,128)(2,1)S(1)} %get-tuple-element.22.refs_2_.refs_4_, bf16[2,256,384]{2,1,0:T(8,128)(2,1)S(1)} %get-tuple-element.23.refs_3_.refs_5_, ...), custom_call_target="tpu_custom_call" | custom-call | flops 503316480 | bytes 1048576 | tf_op jit(solution)/shard_map/far_totals/pallas_call | solution.py:330
  43.5 0.1 collective-permute-start.7
  43.6 5.0 %collective-permute-done.7.refs_11_ = f32[3,8,512]{2,1,0:T(8,128)S(1)} collective-permute-done((f32[3,8,512]{2,1,0:T(8,128)S(1)}, f32[3,8,512]{2,1,0:T(8,128)S(1)}, u32[]{:S(2)}, u32[]{:S(2)}) %collective-permute-start.7) | collective-permute-done | bytes 49184 | tf_op jit(solution)/shard_map/ppermute | solution.py:433
  48.5 6.3 %pair_grads.1 = (f32[256,768]{1,0:T(8,128)S(1)}, bf16[256,768]{1,0:T(8,128)(2,1)S(1)}, f32[256,768]{1,0:T(8,128)S(1)}, f32[256,768]{1,0:T(8,128)S(1)}, bf16[2,25...) custom-call(s32[8,128]{1,0:T(8,128)S(1)} %get-tuple-element.19.table_ref.refs_0_, ...), custom_call_target="tpu_custom_call" | custom-call | flops 2516582400 | bytes 1048576 | tf_op jit(solution)/shard_map/pair_grads/pallas_call | solution.py:330
  54.8 0.1 collective-permute-start.8
  54.9 0.1 collective-permute-start.9
  55.0 2.5 %collective-permute-start.10 = (bf16[2,256,384]{2,1,0:T(8,128)(2,1)S(1)}, bf16[2,256,384]{2,1,0:T(8,128)(2,1)S(1)}, u32[]{:S(2)}, u32[]{:S(2)}) collective-permute-start(bf16[2,256,384]{2,1,0:T(8,128)(2,1)S(1)} %get-tuple-element.30), channel_id=1, source_target_pairs={{1,2},{5,6},{2,1},{6,5},{9,10},{13,14},{10,9},{14,13},{17,18},{21,... | collective-permute-start | bytes 1179656 | tf_op jit(solution)/shard_map/ppermute | solution.py:420
  57.5 1.6 %collective-permute-start.11 = (bf16[2,256,384]{2,1,0:T(8,128)(2,1)S(1)}, bf16[2,256,384]{2,1,0:T(8,128)(2,1)S(1)}, u32[]{:S(2)}, u32[]{:S(2)}) collective-permute-start(bf16[2,256,384]{2,1,0:T(8,128)(2,1)S(1)} %get-tuple-element.31), channel_id=1, source_target_pairs={{0,8},{8,0},{1,9},{9,1},{2,10},{10,2},{3,11},{11,3},{4,12},{12,4},... | collective-permute-start | bytes 1179656 | tf_op jit(solution)/shard_map/ppermute | solution.py:421
  59.1 8.3 %collective-permute-done.8.refs_1_ = bf16[256,768]{1,0:T(8,128)(2,1)S(1)} collective-permute-done((bf16[256,768]{1,0:T(8,128)(2,1)S(1)}, bf16[256,768]{1,0:T(8,128)(2,1)S(1)}, u32[]{:S(2)}, u32[]{:S(2)}) %collective-permute-start.8) | collective-permute-done | bytes 393248 | tf_op jit(solution)/shard_map/ppermute | solution.py:418
  67.4 0.0 collective-permute-done.9.refs_4_
  67.4 4.8 %collective-permute-done.10.refs_5_ = bf16[2,256,384]{2,1,0:T(8,128)(2,1)S(1)} collective-permute-done((bf16[2,256,384]{2,1,0:T(8,128)(2,1)S(1)}, bf16[2,256,384]{2,1,0:T(8,128)(2,1)S(1)}, u32[]{:S(2)}, u32[]{:S(2)}) %collective-permute-start.10) | collective-permute-done | bytes 393248 | tf_op jit(solution)/shard_map/ppermute | solution.py:420
  72.3 0.0 collective-permute-done.11.refs_6_
  72.3 1.2 %add_terms.1 = (bf16[256,768]{1,0:T(8,128)(2,1)}, bf16[256,768]{1,0:T(8,128)(2,1)}, bf16[256,768]{1,0:T(8,128)(2,1)}) custom-call(s32[8,128]{1,0:T(8,128)S(1)} %get-tuple-element.19.table_ref.refs_0_, f32[256,768]{1,0:T(8,128)S(1)} %get-tuple-element.25.refs_0_, bf16[256,768]{1,0:T(8,128)(2,1)S(1)} %collective-permute-done.8.refs_1_, ...), custom_call_target="tpu_custom_call" | custom-call | bytes 1048576 | tf_op jit(solution)/shard_map/add_terms/pallas_call | solution.py:330
  (2 shorter events, 0.0 us)
Async XLA Ops:
  0.6 28.9 %collective-permute-start = (bf16[128,1536]{1,0:T(8,128)(2,1)}, bf16[128,1536]{1,0:T(8,128)(2,1)S(1)}, u32[]{:S(2)}, u32[]{:S(2)}) collective-permute-start(bf16[128,1536]{1,0:T(8,128)(2,1)} %bitcast.9), channel_id=1, source_target_pairs={{0,4},{1,5},{2,6},{3,7},{4,0},{5,1},{6,2},{7,3},{8,12},{9,13},{10,... | collective-permute-start | bytes 1179656 | tf_op jit(solution)/shard_map/ppermute | solution.py:321
  1.0 40.4 %collective-permute-start.1 = (bf16[256,768]{1,0:T(8,128)(2,1)}, bf16[256,768]{1,0:T(8,128)(2,1)S(1)}, u32[]{:S(2)}, u32[]{:S(2)}) collective-permute-start(bf16[256,768]{1,0:T(8,128)(2,1)} %bitcast.13), channel_id=1, source_target_pairs={{0,4},{1,5},{2,6},{3,7},{4,0},{5,1},{6,2},{7,3},{8,12},{9,13},{10,... | collective-permute-start | bytes 1179656 | tf_op jit(solution)/shard_map/ppermute | solution.py:321
  4.4 0.7 copy-start.4
  5.1 1.0 %copy-start.1 = (bf16[1,1,256,768]{3,2,1,0:T(8,128)(2,1)S(1)}, bf16[1,1,256,768]{3,2,1,0:T(8,128)(2,1)}, u32[]{:S(2)}) copy-start(bf16[1,1,256,768]{3,2,1,0:T(8,128)(2,1)} %param.7) | copy-start | bytes 1179652
  6.1 1.0 %copy-start.2 = (bf16[1,1,256,768]{3,2,1,0:T(8,128)(2,1)S(1)}, bf16[1,1,256,768]{3,2,1,0:T(8,128)(2,1)}, u32[]{:S(2)}) copy-start(bf16[1,1,256,768]{3,2,1,0:T(8,128)(2,1)} %param.8) | copy-start | bytes 1179652
  7.1 1.0 %copy-start.3 = (bf16[1,1,256,768]{3,2,1,0:T(8,128)(2,1)S(1)}, bf16[1,1,256,768]{3,2,1,0:T(8,128)(2,1)}, u32[]{:S(2)}) copy-start(bf16[1,1,256,768]{3,2,1,0:T(8,128)(2,1)} %param.6) | copy-start | bytes 1179652
  8.1 6.6 %copy-start = (bf16[1,1,128,1536]{3,2,1,0:T(8,128)(2,1)S(1)}, bf16[1,1,128,1536]{3,2,1,0:T(8,128)(2,1)}, u32[]{:S(2)}) copy-start(bf16[1,1,128,1536]{3,2,1,0:T(8,128)(2,1)} %param.9) | copy-start | bytes 1179652
  9.8 29.9 %collective-permute-start.5 = (bf16[2,256,384]{2,1,0:T(8,128)(2,1)S(1)}, bf16[2,256,384]{2,1,0:T(8,128)(2,1)S(1)}, u32[]{:S(2)}, u32[]{:S(2)}) collective-permute-start(bf16[2,256,384]{2,1,0:T(8,128)(2,1)S(1)} %get-tuple-element.23.refs_3_.refs_5_), channel_id=1, source_target_pairs={{1,2},{5,6},{2,1},{6,5},{9,10},{13,14},{10,9},{14,13},{17,18},{21,... | collective-permute-start | bytes 1179656 | tf_op jit(solution)/shard_map/ppermute | solution.py:373
  13.1 26.6 %collective-permute-start.4 = (bf16[2,256,384]{2,1,0:T(8,128)(2,1)S(1)}, bf16[2,256,384]{2,1,0:T(8,128)(2,1)S(1)}, u32[]{:S(2)}, u32[]{:S(2)}) collective-permute-start(bf16[2,256,384]{2,1,0:T(8,128)(2,1)S(1)} %get-tuple-element.23.refs_3_.refs_5_), channel_id=1, source_target_pairs={{0,1},{4,5},{2,3},{6,7},{1,0},{5,4},{3,2},{7,6},{8,9},{12,13},{10,... | collective-permute-start | bytes 1179656 | tf_op jit(solution)/shard_map/ppermute | solution.py:373
  13.1 18.1 %collective-permute-start.6 = (bf16[2,256,384]{2,1,0:T(8,128)(2,1)S(1)}, bf16[2,256,384]{2,1,0:T(8,128)(2,1)S(1)}, u32[]{:S(2)}, u32[]{:S(2)}) collective-permute-start(bf16[2,256,384]{2,1,0:T(8,128)(2,1)S(1)} %get-tuple-element.24.refs_6_.refs_8_), channel_id=1, source_target_pairs={{0,8},{8,0},{1,9},{9,1},{2,10},{10,2},{3,11},{11,3},{4,12},{12,4},... | collective-permute-start | bytes 1179656 | tf_op jit(solution)/shard_map/ppermute | solution.py:374
  29.5 1.4 %collective-permute-start.3 = (bf16[128,768]{1,0:T(8,128)(2,1)S(1)}, bf16[128,768]{1,0:T(8,128)(2,1)S(1)}, u32[]{:S(2)}, u32[]{:S(2)}) collective-permute-start(bf16[128,768]{1,0:T(8,128)(2,1)S(1)} %dynamic-slice_bitcast_fusion), channel_id=1, source_target_pairs={{0,16},{16,0},{1,17},{17,1},{2,18},{18,2},{3,19},{19,3},{4,20},{20... | collective-permute-start | bytes 589832 | tf_op jit(solution)/shard_map/ppermute | solution.py:363
  30.9 10.5 %collective-permute-start.2 = (bf16[128,768]{1,0:T(8,128)(2,1)S(1)}, bf16[128,768]{1,0:T(8,128)(2,1)S(1)}, u32[]{:S(2)}, u32[]{:S(2)}) collective-permute-start(bf16[128,768]{1,0:T(8,128)(2,1)S(1)} %constant_dynamic-slice_fusion), channel_id=1, source_target_pairs={{0,16},{16,0},{1,17},{17,1},{2,18},{18,2},{3,19},{19,3},{4,20},{20... | collective-permute-start | bytes 589832 | tf_op jit(solution)/shard_map/ppermute | solution.py:363
  43.5 5.1 %collective-permute-start.7 = (f32[3,8,512]{2,1,0:T(8,128)S(1)}, f32[3,8,512]{2,1,0:T(8,128)S(1)}, u32[]{:S(2)}, u32[]{:S(2)}) collective-permute-start(f32[3,8,512]{2,1,0:T(8,128)S(1)} %far_totals.1.refs_10_), channel_id=1, source_target_pairs={{0,4},{1,5},{2,6},{3,7},{4,0},{5,1},{6,2},{7,3},{8,12},{9,13},{10,... | collective-permute-start | bytes 147464 | tf_op jit(solution)/shard_map/ppermute | solution.py:433
  54.8 12.6 %collective-permute-start.8 = (bf16[256,768]{1,0:T(8,128)(2,1)S(1)}, bf16[256,768]{1,0:T(8,128)(2,1)S(1)}, u32[]{:S(2)}, u32[]{:S(2)}) collective-permute-start(bf16[256,768]{1,0:T(8,128)(2,1)S(1)} %get-tuple-element.26), channel_id=1, source_target_pairs={{0,4},{1,5},{2,6},{3,7},{4,0},{5,1},{6,2},{7,3},{8,12},{9,13},{10,... | collective-permute-start | bytes 1179656 | tf_op jit(solution)/shard_map/ppermute | solution.py:418
  54.9 12.5 %collective-permute-start.9 = (bf16[2,256,384]{2,1,0:T(8,128)(2,1)S(1)}, bf16[2,256,384]{2,1,0:T(8,128)(2,1)S(1)}, u32[]{:S(2)}, u32[]{:S(2)}) collective-permute-start(bf16[2,256,384]{2,1,0:T(8,128)(2,1)S(1)} %get-tuple-element.29), channel_id=1, source_target_pairs={{0,1},{4,5},{2,3},{6,7},{1,0},{5,4},{3,2},{7,6},{8,9},{12,13},{10,... | collective-permute-start | bytes 1179656 | tf_op jit(solution)/shard_map/ppermute | solution.py:420
  55.0 17.3 %collective-permute-start.10 = (bf16[2,256,384]{2,1,0:T(8,128)(2,1)S(1)}, bf16[2,256,384]{2,1,0:T(8,128)(2,1)S(1)}, u32[]{:S(2)}, u32[]{:S(2)}) collective-permute-start(bf16[2,256,384]{2,1,0:T(8,128)(2,1)S(1)} %get-tuple-element.30), channel_id=1, source_target_pairs={{1,2},{5,6},{2,1},{6,5},{9,10},{13,14},{10,9},{14,13},{17,18},{21,... | collective-permute-start | bytes 1179656 | tf_op jit(solution)/shard_map/ppermute | solution.py:420
  57.5 14.8 %collective-permute-start.11 = (bf16[2,256,384]{2,1,0:T(8,128)(2,1)S(1)}, bf16[2,256,384]{2,1,0:T(8,128)(2,1)S(1)}, u32[]{:S(2)}, u32[]{:S(2)}) collective-permute-start(bf16[2,256,384]{2,1,0:T(8,128)(2,1)S(1)} %get-tuple-element.31), channel_id=1, source_target_pairs={{0,8},{8,0},{1,9},{9,1},{2,10},{10,2},{3,11},{11,3},{4,12},{12,4},... | collective-permute-start | bytes 1179656 | tf_op jit(solution)/shard_map/ppermute | solution.py:421

commit v3 on v2

v3 whole, which is shorter than its diff:
```python
import functools
import math

import jax
import jax.numpy as jnp
from jax import lax
from jax.experimental import pallas as pl
from jax.experimental.pallas import tpu as pltpu
from jax.sharding import PartitionSpec as P

NCT = 4
LOG2E = 1.4426950408889634
DEAD = -1e30
BYTES = 1 << 20
VMEM_LIMIT = 24 << 20
PREPARE_VMEM_LIMIT = 56 << 20

SMEM = pl.BlockSpec(memory_space=pltpu.SMEM)
NT = (((1,), (1,)), ((), ()))
NN = (((1,), (0,)), ((), ()))
TN = (((0,), (0,)), ((), ()))


def dot(a, b, dims):
    return lax.dot_general(a, b, dims, preferred_element_type=jnp.float32)


def swaps_along(size):
    return [
        [(p, p + 1) for p in range(first, size - 1, 2)] for first in (0, 1) if first + 1 < size
    ]


def both_ways(pairs):
    return [(a, b) for a, b in pairs] + [(b, a) for a, b in pairs]


def row_route(swap, col_count):
    return [
        (a * col_count + col, b * col_count + col)
        for a, b in both_ways(swap)
        for col in range(col_count)
    ]


def col_route(swap, row_count, col_count):
    return [
        (row * col_count + a, row * col_count + b)
        for a, b in both_ways(swap)
        for row in range(row_count)
    ]


def partner(at, place, size):
    other = jnp.where(lax.rem(place, 2) == at, place + 1, place - 1)
    return jnp.clip(other, 0, size - 1), (other >= 0) & (other < size)


def table_rows(plan):
    cols = 1
    frames = cols + plan.nc
    flips = frames + plan.nf
    return cols, frames, flips


def table_shape(plan):
    rows = table_rows(plan)[-1] + plan.pairs
    return jax.ShapeDtypeStruct((-(-rows // 8) * 8, plan.hd), jnp.int32)


def prepare_kernel(plan, offsets_ref, counts_ref, q_ref, k_ref, v_ref, *refs):
    table_ref, plane_ref, across_ref, q_out_ref, sems = refs
    hd = plan.hd
    flips, copies = [], []
    for pair in range(plan.pairs):
        hits = jnp.int32(0)
        for slot in range(offsets_ref.shape[2]):
            hits = hits | jnp.abs(offsets_ref[2 * pair, 0, slot])
        flip = jnp.where(hits != 0, 1, 0).astype(jnp.int32)
        flips.append(flip)
        at = pl.ds(pair * hd, hd)
        for kind, near_ref in enumerate((plane_ref, across_ref)):
            head = 2 * pair + (flip if kind == 0 else 1 - flip)
            cols = pl.ds(pl.multiple_of(head * hd, hd), hd)
            targets = [
                (k_ref, near_ref.at[0, :, at]),
                (v_ref, near_ref.at[1, :, at]),
                (q_ref, q_out_ref.at[:, pl.ds((2 * pair + kind) * hd, hd)]),
            ]
            for source, target in targets:
                sem = sems.at[len(copies)]
                copies.append(pltpu.make_async_copy(source.at[:, cols], target, sem))
                copies[-1].start()
    frame, spot = lax.axis_index("frame"), lax.axis_index("tile")
    row, col = lax.div(spot, plan.col_count), lax.rem(spot, plan.col_count)
    entries = [counts_ref[frame, spot]]
    for at in range(plan.nc):
        other, there = partner(at, col, plan.col_count)
        entries.append(jnp.where(there, counts_ref[frame, row * plan.col_count + other], 0))
    for at in range(plan.nf):
        other, there = partner(at, frame, plan.frame_count)
        entries.append(jnp.where(there, counts_ref[other, spot], 0))
    entries += flips
    entries += [jnp.int32(0)] * (table_ref.shape[0] - len(entries))
    for at, entry in enumerate(entries):
        table_ref[at : at + 1, :] = jnp.full((1, hd), entry, jnp.int32)
    for copy in copies:
        copy.wait()


def gather_kernel(plan, table_ref, grad_ref, *refs):
    got_refs, out_ref = refs[:-1], refs[-1]
    section = lax.axis_index("section")
    sections = len(refs)
    flips = table_rows(plan)[-1]
    count = table_ref[0:1, :]
    rows, width, hd = grad_ref.shape[0], out_ref.shape[1], plan.hd
    at_rows = lax.broadcasted_iota(jnp.int32, (rows, hd), 0)
    for k in range(sections):
        holder = lax.rem(section + sections - k, sections)
        live = at_rows + holder * rows < count
        start = pl.multiple_of(holder * rows, rows)
        for pair in range(plan.pairs):
            heads = []
            for head in (2 * pair, 2 * pair + 1):
                at = pl.multiple_of(section * width + head * hd, hd)
                if k == 0:
                    part = grad_ref[:, pl.ds(at, hd)]
                else:
                    part = got_refs[k - 1][:, pl.ds(at, hd)]
                heads.append(jnp.where(live, part.astype(jnp.float32), 0.0))
            for i, part in enumerate(in_order(table_ref, flips + pair, *heads)):
                part = part.astype(out_ref.dtype)
                out_ref[pl.ds(start, rows), pl.ds((2 * pair + i) * hd, hd)] = part


def in_order(table_ref, row, a, b):
    flip = jnp.broadcast_to(table_ref[row : row + 1, :], a.shape) != 0
    return jnp.where(flip, b, a), jnp.where(flip, a, b)


def windows(plan, kv_refs):
    cols, frames, _ = table_rows(plan)
    per_kind = (kv_refs[: 1 + plan.nc], kv_refs[1 + plan.nc :])
    block = 0
    for pair in range(plan.pairs):
        for kind, first in ((0, cols), (1, frames)):
            slots = []
            for at, ref in enumerate(per_kind[kind]):
                row = 0 if at == 0 else first + at - 1
                slots.append((block, ref, pl.ds(pair * plan.hd, plan.hd), row))
                block += 1
            yield pair, kind, pl.ds((2 * pair + kind) * plan.hd, plan.hd), slots


def block_count(plan):
    return plan.pairs * (2 + plan.nc + plan.nf)


def block_weights(plan, table_ref, ref, at, row, q):
    at_rows = lax.broadcasted_iota(jnp.int32, (plan.tile, plan.hd), 0)
    bias = jnp.where(at_rows < table_ref[row : row + 1, :], 0.0, DEAD)
    bias = jnp.concatenate([bias] * (plan.tile // plan.hd), axis=1)
    scores = dot(ref[0, :, at], q, NT) * plan.factor + bias
    top = jnp.max(scores, axis=0, keepdims=True)
    weight = jnp.exp2(scores - top)
    return weight, top, jnp.sum(weight, axis=0, keepdims=True)


def merge(parts):
    top = functools.reduce(jnp.maximum, [log_total for log_total, _ in parts])
    weights = [jnp.exp2(log_total - top) for log_total, _ in parts]
    total = sum(weights)
    mean = sum(w * mean for w, (_, mean) in zip(weights, parts)) / total
    return top + jnp.log(total) * LOG2E, mean


def totals_at(plan, at, pair, kind):
    return pl.ds(4 * at + 2 * kind, 2), pl.ds(pair * plan.tile, plan.tile)


def totals_shape(plan, sets):
    return jax.ShapeDtypeStruct((4 * sets, plan.pairs * plan.tile), jnp.float32)


def totals(parts):
    top = functools.reduce(jnp.maximum, [top for top, _, _ in parts])
    weights = [jnp.exp2(part_top - top) for part_top, _, _ in parts]
    total = sum(w * total for w, (_, total, _) in zip(weights, parts))
    cross = sum(w * cross for w, (_, _, cross) in zip(weights, parts))
    return jnp.concatenate([top + jnp.log(total) * LOG2E, cross / total], axis=0)


def own_kernel(plan, table_ref, q_ref, grad_ref, *refs):
    *kv_refs, weight_ref, top_ref, slope_ref, total_ref = refs
    for pair, kind, cols, slots in windows(plan, kv_refs):
        parts = []
        for block, ref, at, row in slots:
            weight, top, total = block_weights(plan, table_ref, ref, at, row, q_ref[:, cols])
            slope = dot(ref[1, :, at], grad_ref[:, cols], NT)
            weight_ref[block] = weight
            slope_ref[block] = slope
            top_ref[block : block + 1, :] = top
            parts.append((top, total, jnp.sum(weight * slope, axis=0, keepdims=True)))
        total_ref[totals_at(plan, 0, pair, kind)] = totals(parts)


def order_kernel(plan, table_ref, q_ref, out_ref):
    hd = plan.hd
    flips = table_rows(plan)[-1]
    for pair in range(plan.pairs):
        cols = [pl.ds((2 * pair + i) * hd, hd) for i in (0, 1)]
        heads = [q_ref[:, at].astype(jnp.float32) for at in cols]
        for at, part in zip(cols, in_order(table_ref, flips + pair, *heads)):
            out_ref[:, at] = part.astype(out_ref.dtype)


def far_weights_kernel(plan, table_ref, q_ref, *refs):
    *kv_refs, weight_ref, top_ref, sum_ref = refs
    for pair, kind, cols, slots in windows(plan, kv_refs):
        for block, ref, at, row in slots:
            weight, top, total = block_weights(plan, table_ref, ref, at, row, q_ref[:, cols])
            weight_ref[block] = weight
            top_ref[block : block + 1, :] = top
            sum_ref[block : block + 1, :] = total


def far_totals_kernel(plan, weight_ref, top_ref, sum_ref, own_ref, grad_ref, *refs):
    *kv_refs, slope_ref, total_ref = refs
    total_ref[0:4, :] = own_ref[...]
    for pair, kind, cols, slots in windows(plan, kv_refs):
        parts = []
        for block, ref, at, _ in slots:
            slope = dot(ref[1, :, at], grad_ref[:, cols], NT)
            slope_ref[block] = slope
            cross = jnp.sum(weight_ref[block] * slope, axis=0, keepdims=True)
            parts.append((top_ref[block : block + 1, :], sum_ref[block : block + 1, :], cross))
        total_ref[totals_at(plan, 1, pair, kind)] = totals(parts)


def head_grads(plan, sets, total_refs, kv_refs):
    for pair, kind, cols, slots in windows(plan, kv_refs):
        log_totals, row_dots = [], []
        for places in plan.totals_of:
            parts = []
            for ref, place in places:
                part = total_refs[ref][totals_at(plan, place, pair, kind)]
                parts.append((part[0:1], part[1:2]))
            log_total, row_dot = merge(parts)
            log_totals.append(log_total)
            row_dots.append(row_dot)

        def tile_grads(block, log_totals=log_totals, row_dots=row_dots):
            softmax, grad_scores = [], []
            for (weight_ref, top_ref, slope_ref, _, _), log_total, row_dot in zip(
                sets, log_totals, row_dots
            ):
                scale = jnp.exp2(top_ref[block : block + 1, :] - log_total)
                part = weight_ref[block] * scale
                softmax.append(part.astype(jnp.bfloat16))
                grad_scores.append((part * (slope_ref[block] - row_dot)).astype(jnp.bfloat16))
            return jnp.concatenate(softmax, axis=1), jnp.concatenate(grad_scores, axis=1)

        q = jnp.concatenate([q_ref[:, cols] for _, _, _, q_ref, _ in sets], axis=0)
        grad = jnp.concatenate([grad_ref[:, cols] for _, _, _, _, grad_ref in sets], axis=0)
        yield kind, cols, q, grad, slots, tile_grads


def first_grads_kernel(plan, *refs):
    refs = list(refs)
    take = lambda n: [refs.pop(0) for _ in range(n)]
    sets = [take(5) for _ in range(1 + plan.nr)]
    kv_refs, total_refs = take(2 + plan.nc + plan.nf), take(plan.n_totals)
    dq_refs = take(1 + plan.nr)
    for kind, cols, q, grad, slots, tile_grads in head_grads(plan, sets, total_refs, kv_refs):
        query_grad = None
        for slot, (block, ref, at, _) in enumerate(slots):
            softmax, grad_scores = tile_grads(block)
            term = dot(ref[0, :, at], grad_scores, TN)
            query_grad = term if query_grad is None else query_grad + term
            if kind == 0 and slot > 0:
                dk = dot(grad_scores, q, NN) * plan.scale
                refs[slot - 1][0, :, at] = dk.astype(jnp.bfloat16)
                refs[slot - 1][1, :, at] = dot(softmax, grad, NN).astype(jnp.bfloat16)
        query_grad = jnp.transpose(query_grad * plan.scale)
        for at, ref in enumerate(dq_refs):
            rows = query_grad[at * plan.tile : (at + 1) * plan.tile]
            ref[:, cols] = rows.astype(ref.dtype)


def last_grads_kernel(plan, *refs):
    refs = list(refs)
    take = lambda n: [refs.pop(0) for _ in range(n)]
    sets = [take(5) for _ in range(1 + plan.nr)]
    kv_refs, total_refs = take(2 + plan.nc + plan.nf), take(plan.n_totals)
    own_refs = take(2)
    for kind, cols, q, grad, slots, tile_grads in head_grads(plan, sets, total_refs, kv_refs):
        for slot, (block, ref, at, _) in enumerate(slots if kind else slots[:1]):
            softmax, grad_scores = tile_grads(block)
            dk = dot(grad_scores, q, NN) * plan.scale
            dv = dot(softmax, grad, NN)
            for i, out in enumerate((dk, dv)):
                if slot == 0:
                    own_refs[i][:, cols] = out
                else:
                    refs[slot - 1][i, :, at] = out.astype(jnp.bfloat16)


def add_query_kernel(plan, table_ref, *refs):
    *refs, out_ref = refs
    flips, hd = table_rows(plan)[-1], plan.hd
    for pair in range(plan.pairs):
        cols = [pl.ds((2 * pair + kind) * hd, hd) for kind in (0, 1)]
        parts = [sum(ref[:, at].astype(jnp.float32) for ref in refs) for at in cols]
        for at, head in zip(cols, in_order(table_ref, flips + pair, *parts)):
            out_ref[:, at] = head.astype(out_ref.dtype)


def add_key_kernel(plan, table_ref, *refs):
    refs = list(refs)
    take = lambda n: [refs.pop(0) for _ in range(n)]
    flips, hd = table_rows(plan)[-1], plan.hd
    own, near = take(2), (take(plan.nc), take(plan.nf))
    for pair in range(plan.pairs):
        cols = [pl.ds((2 * pair + kind) * hd, hd) for kind in (0, 1)]
        near_at = pl.ds(pair * hd, hd)
        for i, out_ref in enumerate(refs):
            parts = []
            for kind in (0, 1):
                total = own[i][:, cols[kind]]
                for ref in near[kind]:
                    total = total + ref[i, :, near_at].astype(jnp.float32)
                parts.append(total)
            for at, head in zip(cols, in_order(table_ref, flips + pair, *parts)):
                out_ref[:, at] = head.astype(out_ref.dtype)


class Plan:
    pass


def params():
    return pltpu.CompilerParams(vmem_limit_bytes=VMEM_LIMIT)


def local(queries, key_rows, value_rows, grad_rows, offsets, counts):
    q, k, v, grad = queries[0, 0], key_rows[0, 0], value_rows[0, 0], grad_rows[0, 0]
    tile, width = q.shape
    heads = offsets.shape[0]
    pairs = heads // 2
    hd = width // heads
    sections = lax.axis_size("section")
    frame_count = lax.axis_size("frame")
    col_count = NCT
    row_count = lax.axis_size("tile") // col_count

    plan = Plan()
    plan.tile, plan.hd, plan.col_count = tile, hd, col_count
    plan.scale = 1.0 / math.sqrt(hd)
    plan.factor = plan.scale * LOG2E
    row_swaps = swaps_along(row_count)
    col_swaps = swaps_along(col_count)
    frame_swaps = swaps_along(frame_count)
    plan.nr, plan.nc, plan.nf = len(row_swaps), len(col_swaps), len(frame_swaps)
    plan.frame_count = frame_count
    row_routes = [row_route(swap, col_count) for swap in row_swaps]
    col_routes = [col_route(swap, row_count, col_count) for swap in col_swaps]
    frame_routes = [both_ways(swap) for swap in frame_swaps]

    def from_rows(x):
        return [lax.ppermute(x, "tile", route) for route in row_routes]

    vm = pl.BlockSpec(memory_space=pltpu.VMEM)
    plan.row_count = row_count

    plan.pairs = pairs

    def call(kernel, name, out_shape, flops, *operands, nbytes=BYTES):
        return pl.pallas_call(
            functools.partial(kernel, plan),
            out_shape=out_shape,
            in_specs=[vm] * len(operands),
            out_specs=[vm] * len(out_shape),
            compiler_params=params(),
            cost_estimate=pl.CostEstimate(
                flops=flops, bytes_accessed=nbytes, transcendentals=0
            ),
            name=name,
        )(*operands)

    low = jax.ShapeDtypeStruct((tile, width), jnp.bfloat16)
    wide = jax.ShapeDtypeStruct((tile, width), jnp.float32)
    packed = jax.ShapeDtypeStruct((2, tile, pairs * hd), jnp.bfloat16)
    blocks = block_count(plan)
    block_shape = jax.ShapeDtypeStruct((blocks, tile, tile), jnp.float32)
    rows_shape = jax.ShapeDtypeStruct((-(-blocks // 8) * 8, tile), jnp.float32)

    got = []
    for shift in range(1, sections):
        route = [(i, (i + shift) % sections) for i in range(sections)]
        got.append(lax.ppermute(grad, "section", route))
    far_q_raw = from_rows(q)

    hbm = pl.BlockSpec(memory_space=pl.ANY)
    table, plane_kv, across_kv, own_q = pl.pallas_call(
        functools.partial(prepare_kernel, plan),
        out_shape=[table_shape(plan), packed, packed, low],
        in_specs=[SMEM] * 2 + [hbm] * 3,
        out_specs=[vm] * 4,
        scratch_shapes=[pltpu.SemaphoreType.DMA((6 * pairs,))],
        compiler_params=pltpu.CompilerParams(vmem_limit_bytes=PREPARE_VMEM_LIMIT),
        cost_estimate=pl.CostEstimate(flops=0, bytes_accessed=0, transcendentals=0),
        name="prepare",
    )(jnp.transpose(offsets, (0, 2, 1)), counts, q, k, v)

    (own_grad,) = call(gather_kernel, "gather_grad", [low], 0, table, grad, *got)

    near_plane = [lax.ppermute(plane_kv, "tile", route) for route in col_routes]
    near_across = [lax.ppermute(across_kv, "frame", route) for route in frame_routes]
    kv = [plane_kv, *near_plane, across_kv, *near_across]
    far_grad = from_rows(own_grad)

    matmul = 2 * blocks * tile * tile * hd
    far_q = [call(order_kernel, "order_queries", [low], 0, table, raw)[0] for raw in far_q_raw]
    table, *far_q = lax.optimization_barrier((table, *far_q))
    own_weight, own_top, own_slope, own_total = call(
        own_kernel,
        "own_rows",
        [block_shape, rows_shape, block_shape, totals_shape(plan, 1)],
        2 * matmul,
        *(table, own_q, own_grad, *kv),
    )
    sets = [(own_weight, own_top, own_slope, own_q, own_grad)]
    far_totals = []
    for queries, far in zip(far_q, far_grad):
        weight, top, total = call(
            far_weights_kernel,
            "far_weights",
            [block_shape, rows_shape, rows_shape],
            matmul,
            *(table, queries, *kv),
        )
        slope, total = call(
            far_totals_kernel,
            "far_totals",
            [block_shape, totals_shape(plan, 2)],
            matmul,
            *(weight, top, total, own_total, far, *kv),
        )
        sets.append((weight, top, slope, queries, far))
        far_totals.append(total)
    shared, plan.totals_of = share_totals(own_total, far_totals, row_routes)
    plan.n_totals = len(shared)

    nq = 1 + plan.nr
    operands = [ref for refs in sets for ref in refs] + kv + shared
    outs = call(
        first_grads_kernel,
        "first_grads",
        [wide] + [low] * plan.nr + [packed] * plan.nc,
        2 * nq * matmul,
        *operands,
    )
    own_dq, far_dq, plane_out = outs[0], outs[1:nq], outs[nq:]
    back = [lax.ppermute(x, "tile", r) for x, r in zip(far_dq, row_routes)]
    back_plane = [lax.ppermute(x, "tile", r) for x, r in zip(plane_out, col_routes)]
    operands[-1], _ = lax.optimization_barrier((operands[-1], own_dq))
    own_dk, own_dv, *across_out = call(
        last_grads_kernel,
        "last_grads",
        [wide] * 2 + [packed] * plan.nf,
        nq * matmul,
        *operands,
    )
    back_across = [lax.ppermute(x, "frame", r) for x, r in zip(across_out, frame_routes)]
    (dq,) = call(add_query_kernel, "add_query", [low], 0, table, own_dq, *back)
    dk, dv = call(
        add_key_kernel,
        "add_key",
        [low] * 2,
        0,
        *(table, own_dk, own_dv, *back_plane, *back_across),
    )
    return dq[None, None], dk[None, None], dv[None, None]


def share_totals(own, far, row_routes):
    if len(far) == 0:
        return [own], [[(0, 0)]]
    if len(far) == 1:
        back = lax.ppermute(far[0], "tile", row_routes[0])
        return [far[0], back], [[(0, 0), (1, 1)], [(0, 1), (1, 0)]]
    terms = [own]
    for part, route in zip(far, row_routes):
        term = lax.ppermute(part[4:], "tile", route)
        there = lax.ppermute(jnp.ones((8, 128), jnp.float32), "tile", route)[0, 0] > 0
        logs = jnp.array([1, 0, 1, 0], jnp.float32)[:, None]
        terms.append(jnp.where(there, term, DEAD * logs))
    merged = []
    for kind in (0, 1):
        merged += merge([(t[2 * kind], t[2 * kind + 1]) for t in terms])
    total = jnp.stack(merged)
    shared = [total] + [lax.ppermute(total, "tile", route) for route in row_routes]
    return shared, [[(at, 0)] for at in range(len(shared))]


def solution(mesh):
    return jax.shard_map(
        local,
        mesh=mesh,
        in_specs=(
            P("frame", "tile", None, "section"),
            P("frame", "tile", None, "section"),
            P("frame", "tile", None, "section"),
            P("frame", "tile", "section", None),
            P("section", None, None),
            P(),
        ),
        out_specs=(
            P("frame", "tile", None, "section"),
            P("frame", "tile", None, "section"),
            P("frame", "tile", None, "section"),
        ),
        check_vma=False,
    )
```

time: 74.6 us -> 70.5 us (0.945)
  waiting for transfers between devices: 42.8 us -> 37.3 us
  starting transfers between devices: 12.4 us -> 14.8 us
  local copies, waits for them, and re-layouts: 4.52 us -> 3.67 us
    ppermute x2, waiting for transfers between devices: 8.43 us -> 0.01 us  [local(): near_plane = [lax.ppermute(plane_kv, 'tile', route) for route in col_routes]]
    ppermute x2, waiting for transfers between devices: 14.8 us -> 18.6 us  [from_rows(): return [lax.ppermute(x, 'tile', route) for route in row_routes]]
    ppermute x6 -> x5, starting transfers between devices: 2.83 us -> 4.67 us  [the longest x2 4.46 us: local(): lax.ppermute(x, 'tile', r)]
    ppermute x6 -> x5, waiting for transfers between devices: 19.6 us -> 18.7 us  [the longest x1 9.12 us: local(): back = [lax.ppermute(x, 'tile', r) for x, r in zip(far_dq, row_routes)]]
    unnamed x11 -> x14, local copies, waits for them, and re-layouts: 4.49 us -> 3.67 us
    pallas_call x7 -> x10, Pallas kernels: 13 us -> 13.6 us  [the longest x9 10.2 us: call(): pl.pallas_call(functools.partial(kernel, plan), out_shape=out_shape, in_s...]
  transfers between devices with their start and end apart: 12 -> 11, of which waited for: 6 -> 5; matrix products, arithmetic and copies ran while one was open for 1% -> 0% of each run, Pallas kernels for 5% -> 13%
where the time goes in v3:
time: 70.5 us; the launch traced here: 70.1 us
  waiting for transfers between devices  37.3 us (53%)
  starting transfers between devices  14.8 us (21%)
  Pallas kernels  13.6 us (19%)
  local copies, waits for them, and re-layouts  3.67 us (5%)
  between operations  0.78 us (1%)
    ppermute x2, waiting for transfers between devices, from_rows(): return [lax.ppermute(x, 'tile', route) for route in row_routes]  18.6 us
    pallas_call x9, Pallas kernels, call(): pl.pallas_call(functools.partial(kernel, plan), out_shape=out_shape, in_s...  10.2 us
    ppermute x1, waiting for transfers between devices, local(): back = [lax.ppermute(x, 'tile', r) for x, r in zip(far_dq, row_routes)]  9.12 us
    ppermute x2, waiting for transfers between devices, local(): lax.ppermute(x, 'tile', r)  4.85 us
    ppermute x1, waiting for transfers between devices, share_totals(): back = lax.ppermute(far[0], 'tile', row_routes[0])  4.71 us
    ppermute x2, starting transfers between devices, local(): lax.ppermute(x, 'tile', r)  4.46 us
    ppermute x2, starting transfers between devices, local(): near_plane = [lax.ppermute(plane_kv, 'tile', route) for route in col_routes]  3.69 us
    unnamed x14, local copies, waits for them, and re-layouts  3.67 us
  transfers between devices with their start and end apart: 11, of which 5 were waited for; matrix products, arithmetic and copies ran while one was open for 0% of the time, Pallas kernels for 13%

profile of v3, /device:TPU:24, one launch (start us, length us, event | category | flops | bytes accessed | tf_op | source)
XLA Modules:
  0.0 70.1 jit_solution(13074391342308922754)
XLA Ops:
  0.6 0.1 collective-permute-start.1
  0.7 0.4 collective-permute-start
  1.1 3.4 %prepare.1 = (s32[8,128]{1,0:T(8,128)}, bf16[2,256,384]{2,1,0:T(8,128)(2,1)}, bf16[2,256,384]{2,1,0:T(8,128)(2,1)}, bf16[256,768]{1,0:T(8,128)(2,1)}) custom-call(s32[6,3,9]{2,1,0:T(4,128)} %bitcast.15, s32[2,8]{1,0:T(2,128)} %counts_ref.1, bf16[256,768]{1,0:T(8,128)(2,1)} %bitcast.13, bf16[256,768]{1,0:T(8,128)(2,1)} %bitcast.10, bf16[256,768]{1,0:T(8,128)(2,1)} %bitcast.11), custom_call_target="tpu_custom_call" | custom-call | tf_op jit(solution)/shard_map/prepare/pallas_call | solution.py:405
  4.5 0.0 copy-start.4
  4.5 0.0 copy-start.1
  4.5 0.0 copy-start.3
  4.5 1.6 %collective-permute-start.2 = (bf16[2,256,384]{2,1,0:T(8,128)(2,1)}, bf16[2,256,384]{2,1,0:T(8,128)(2,1)S(1)}, u32[]{:S(2)}, u32[]{:S(2)}) collective-permute-start(bf16[2,256,384]{2,1,0:T(8,128)(2,1)} %get-tuple-element.31.refs_0_.refs_10_), channel_id=1, source_target_pairs={{0,1},{4,5},{2,3},{6,7},{1,0},{5,4},{3,2},{7,6},{8,9},{12,13},{10,... | collective-permute-start | bytes 1179656 | tf_op jit(solution)/shard_map/ppermute | solution.py:418
  6.1 2.1 %collective-permute-start.3 = (bf16[2,256,384]{2,1,0:T(8,128)(2,1)}, bf16[2,256,384]{2,1,0:T(8,128)(2,1)S(1)}, u32[]{:S(2)}, u32[]{:S(2)}) collective-permute-start(bf16[2,256,384]{2,1,0:T(8,128)(2,1)} %get-tuple-element.31.refs_0_.refs_10_), channel_id=1, source_target_pairs={{1,2},{5,6},{2,1},{6,5},{9,10},{13,14},{10,9},{14,13},{17,18},{21,... | collective-permute-start | bytes 1179656 | tf_op jit(solution)/shard_map/ppermute | solution.py:418
  8.2 1.8 %collective-permute-start.4 = (bf16[2,256,384]{2,1,0:T(8,128)(2,1)}, bf16[2,256,384]{2,1,0:T(8,128)(2,1)S(1)}, u32[]{:S(2)}, u32[]{:S(2)}) collective-permute-start(bf16[2,256,384]{2,1,0:T(8,128)(2,1)} %get-tuple-element.32.refs_3_.refs_13_), channel_id=1, source_target_pairs={{0,8},{8,0},{1,9},{9,1},{2,10},{10,2},{3,11},{11,3},{4,12},{12,4},... | collective-permute-start | bytes 1179656 | tf_op jit(solution)/shard_map/ppermute | solution.py:419
  10.0 0.0 collective-permute-done.1.refs_0_
  10.0 0.0 copy-start.5
  10.0 1.0 %copy-done.5 = bf16[1,1,128,1536]{3,2,1,0:T(8,128)(2,1)S(1)} copy-done((bf16[1,1,128,1536]{3,2,1,0:T(8,128)(2,1)S(1)}, bf16[1,1,128,1536]{3,2,1,0:T(8,128)(2,1)}, u32[]{:S(2)}) %copy-start.5) | copy-done | bytes 393240
  11.0 0.0 copy-start.6
  11.0 0.7 copy-done.6
  11.7 0.1 gather_grad.1.grad_ref.refs_4_
  11.8 2.7 %collective-permute-start.5 = (bf16[256,768]{1,0:T(8,128)(2,1)S(1)}, bf16[256,768]{1,0:T(8,128)(2,1)S(1)}, u32[]{:S(2)}, u32[]{:S(2)}) collective-permute-start(bf16[256,768]{1,0:T(8,128)(2,1)S(1)} %gather_grad.1.grad_ref.refs_4_), channel_id=1, source_target_pairs={{0,4},{1,5},{2,6},{3,7},{4,0},{5,1},{6,2},{7,3},{8,12},{9,13},{10,... | collective-permute-start | bytes 1179656 | tf_op jit(solution)/shard_map/ppermute | solution.py:371
  14.5 15.7 %collective-permute-done.q_ref = bf16[256,768]{1,0:T(8,128)(2,1)S(1)} collective-permute-done((bf16[256,768]{1,0:T(8,128)(2,1)}, bf16[256,768]{1,0:T(8,128)(2,1)S(1)}, u32[]{:S(2)}, u32[]{:S(2)}) %collective-permute-start) | collective-permute-done | bytes 393248 | tf_op jit(solution)/shard_map/ppermute | solution.py:371
  30.1 0.1 order_queries.1.q_ref.refs_8_
  30.2 0.0 collective-permute-done.2.refs_1_.refs_11_
  30.2 0.0 collective-permute-done.3.refs_2_.refs_12_
  30.3 0.0 collective-permute-done.4.refs_4_.refs_14_
  30.3 0.0 copy-start
  30.3 1.0 %copy-done = bf16[2,256,384]{2,1,0:T(8,128)(2,1)S(1)} copy-done((bf16[2,256,384]{2,1,0:T(8,128)(2,1)S(1)}, bf16[2,256,384]{2,1,0:T(8,128)(2,1)}, u32[]{:S(2)}) %copy-start) | copy-done | bytes 393240
  31.3 0.0 copy-start.2
  31.3 1.0 %copy-done.2 = bf16[2,256,384]{2,1,0:T(8,128)(2,1)S(1)} copy-done((bf16[2,256,384]{2,1,0:T(8,128)(2,1)S(1)}, bf16[2,256,384]{2,1,0:T(8,128)(2,1)}, u32[]{:S(2)}) %copy-start.2) | copy-done | bytes 393240
  32.3 1.5 %far_weights.1 = (f32[15,256,256]{2,1,0:T(8,128)S(1)}, f32[16,256]{1,0:T(8,128)S(1)}, f32[16,256]{1,0:T(8,128)S(1)}) custom-call(s32[8,128]{1,0:T(8,128)S(1)} %copy-done.6, bf16[256,768]{1,0:T(8,128)(2,1)S(1)} %order_queries.1.q_ref.refs_8_, bf16[2,256,384]{2,1,0:T(8,128)(2,1)S(1)} %copy-done, ...), custom_call_target="tpu_custom_call" | custom-call | flops 251658240 | bytes 1048576 | tf_op jit(solution)/shard_map/far_weights/pallas_call | solution.py:379
  33.7 0.0 copy-done.4
  33.7 1.8 %own_rows.1 = (f32[15,256,256]{2,1,0:T(8,128)S(1)}, f32[16,256]{1,0:T(8,128)S(1)}, f32[15,256,256]{2,1,0:T(8,128)S(1)}, f32[4,768]{1,0:T(4,128)S(1)}) custom-call(s32[8,128]{1,0:T(8,128)S(1)} %copy-done.6, bf16[256,768]{1,0:T(8,128)(2,1)S(1)} %copy-done.4, bf16[256,768]{1,0:T(8,128)(2,1)S(1)} %gather_grad.1.grad_ref.refs_4_, ...), custom_call_target="tpu_custom_call" | custom-call | flops 503316480 | bytes 1048576 | tf_op jit(solution)/shard_map/own_rows/pallas_call | solution.py:379
  35.6 2.9 %collective-permute-done.5.grad_ref.refs_9_ = bf16[256,768]{1,0:T(8,128)(2,1)S(1)} collective-permute-done((bf16[256,768]{1,0:T(8,128)(2,1)S(1)}, bf16[256,768]{1,0:T(8,128)(2,1)S(1)}, u32[]{:S(2)}, u32[]{:S(2)}) %collective-permute-start.5) | collective-permute-done | bytes 393248 | tf_op jit(solution)/shard_map/ppermute | solution.py:371
  38.5 0.0 copy-done.1
  38.5 0.0 copy-done.3
  38.5 0.7 %far_totals.1 = (f32[15,256,256]{2,1,0:T(8,128)S(1)}, f32[8,768]{1,0:T(8,128)S(1)}) custom-call(f32[15,256,256]{2,1,0:T(8,128)S(1)} %get-tuple-element.37.weight_ref.refs_5_, f32[16,256]{1,0:T(8,128)S(1)} %get-tuple-element.38.top_ref.refs_6_, f32[16,256]{1,0:T(8,128)S(1)} %get-tuple-element.39.sum_ref, f32[4,768]{1,0:T(4,128)S(1)} %get-tuple-element.40.own_ref, ...), custom_call_target="tpu_custom_call" | custom-call | flops 251658240 | bytes 1048576 | tf_op jit(solution)/shard_map/far_totals/pallas_call | solution.py:379
  39.3 0.1 collective-permute-start.6
  39.3 4.7 %collective-permute-done.6.refs_16_ = f32[8,768]{1,0:T(8,128)S(1)} collective-permute-done((f32[8,768]{1,0:T(8,128)S(1)}, f32[8,768]{1,0:T(8,128)S(1)}, u32[]{:S(2)}, u32[]{:S(2)}) %collective-permute-start.6) | collective-permute-done | bytes 24608 | tf_op jit(solution)/shard_map/ppermute | solution.py:491
  44.0 2.4 %first_grads.1 = (f32[256,768]{1,0:T(8,128)S(1)}, bf16[256,768]{1,0:T(8,128)(2,1)S(1)}, bf16[2,256,384]{2,1,0:T(8,128)(2,1)S(1)}, bf16[2,256,384]{2,1,0:T(8,128)(2,1)S(1)}) custom-call(f32[15,256,256]{2,1,0:T(8,128)S(1)} %get-tuple-element.33.refs_0_, f32[16,256]{1,0:T(8,128)S(1)} %get-tuple-element.34.refs_1_, ...), custom_call_target="tpu_custom_call" | custom-call | flops 1006632960 | bytes 1048576 | tf_op jit(solution)/shard_map/first_grads/pallas_call | solution.py:379
  46.4 0.1 collective-permute-start.7
  46.5 1.6 %collective-permute-start.8 = (bf16[2,256,384]{2,1,0:T(8,128)(2,1)S(1)}, bf16[2,256,384]{2,1,0:T(8,128)(2,1)S(1)}, u32[]{:S(2)}, u32[]{:S(2)}) collective-permute-start(bf16[2,256,384]{2,1,0:T(8,128)(2,1)S(1)} %get-tuple-element.48), channel_id=1, source_target_pairs={{0,1},{4,5},{2,3},{6,7},{1,0},{5,4},{3,2},{7,6},{8,9},{12,13},{10,... | collective-permute-start | bytes 1179656 | tf_op jit(solution)/shard_map/ppermute | solution.py:466
  48.1 2.9 %collective-permute-start.9 = (bf16[2,256,384]{2,1,0:T(8,128)(2,1)S(1)}, bf16[2,256,384]{2,1,0:T(8,128)(2,1)S(1)}, u32[]{:S(2)}, u32[]{:S(2)}) collective-permute-start(bf16[2,256,384]{2,1,0:T(8,128)(2,1)S(1)} %get-tuple-element.49), channel_id=1, source_target_pairs={{1,2},{5,6},{2,1},{6,5},{9,10},{13,14},{10,9},{14,13},{17,18},{21,... | collective-permute-start | bytes 1179656 | tf_op jit(solution)/shard_map/ppermute | solution.py:466
  51.0 1.5 %last_grads.1 = (f32[256,768]{1,0:T(8,128)S(1)}, f32[256,768]{1,0:T(8,128)S(1)}, bf16[2,256,384]{2,1,0:T(8,128)(2,1)S(1)}) custom-call(f32[15,256,256]{2,1,0:T(8,128)S(1)} %get-tuple-element.33.refs_0_, f32[16,256]{1,0:T(8,128)S(1)} %get-tuple-element.34.refs_1_, f32[15,256,256]{2,1,0:T(8,128)S(1)} %get-tuple-element.35.refs_2_, ...), custom_call_target="tpu_custom_call" | custom-call | flops 503316480 | bytes 1048576 | tf_op jit(solution)/shard_map/last_grads/pallas_call | solution.py:379
  52.5 1.6 %collective-permute-start.10 = (bf16[2,256,384]{2,1,0:T(8,128)(2,1)S(1)}, bf16[2,256,384]{2,1,0:T(8,128)(2,1)S(1)}, u32[]{:S(2)}, u32[]{:S(2)}) collective-permute-start(bf16[2,256,384]{2,1,0:T(8,128)(2,1)S(1)} %get-tuple-element.50), channel_id=1, source_target_pairs={{0,8},{8,0},{1,9},{9,1},{2,10},{10,2},{3,11},{11,3},{4,12},{12,4},... | collective-permute-start | bytes 1179656 | tf_op jit(solution)/shard_map/ppermute | solution.py:475
  54.1 9.1 %collective-permute-done.7.refs_1_ = bf16[256,768]{1,0:T(8,128)(2,1)S(1)} collective-permute-done((bf16[256,768]{1,0:T(8,128)(2,1)S(1)}, bf16[256,768]{1,0:T(8,128)(2,1)S(1)}, u32[]{:S(2)}, u32[]{:S(2)}) %collective-permute-start.7) | collective-permute-done | bytes 393248 | tf_op jit(solution)/shard_map/ppermute | solution.py:465
  63.2 0.9 %add_query.1 = bf16[256,768]{1,0:T(8,128)(2,1)} custom-call(s32[8,128]{1,0:T(8,128)S(1)} %copy-done.6, f32[256,768]{1,0:T(8,128)S(1)} %get-tuple-element.43.refs_0_, bf16[256,768]{1,0:T(8,128)(2,1)S(1)} %collective-permute-done.7.refs_1_), custom_call_target="tpu_custom_call" | custom-call | bytes 1048576 | tf_op jit(solution)/shard_map/add_query/pallas_call | solution.py:379
  64.1 0.0 collective-permute-done.8.refs_2_
  64.1 4.8 %collective-permute-done.9.refs_3_ = bf16[2,256,384]{2,1,0:T(8,128)(2,1)S(1)} collective-permute-done((bf16[2,256,384]{2,1,0:T(8,128)(2,1)S(1)}, bf16[2,256,384]{2,1,0:T(8,128)(2,1)S(1)}, u32[]{:S(2)}, u32[]{:S(2)}) %collective-permute-start.9) | collective-permute-done | bytes 393248 | tf_op jit(solution)/shard_map/ppermute | solution.py:466
  68.9 0.0 collective-permute-done.10.refs_4_
  68.9 1.1 %add_key.1 = (bf16[256,768]{1,0:T(8,128)(2,1)}, bf16[256,768]{1,0:T(8,128)(2,1)}) custom-call(s32[8,128]{1,0:T(8,128)S(1)} %copy-done.6, f32[256,768]{1,0:T(8,128)S(1)} %get-tuple-element.46.refs_0_, f32[256,768]{1,0:T(8,128)S(1)} %get-tuple-element.47.refs_1_, bf16[2,256,384]{2,1,0:T(8,128)(2,1)S(1)} %collective-permute-done.8.refs_2_, ...), custom_call_target="tpu_custom_call" | custom-call | bytes 1048576 | tf_op jit(solution)/shard_map/add_key/pallas_call | solution.py:379
Async XLA Ops:
  0.6 9.4 %collective-permute-start.1 = (bf16[128,1536]{1,0:T(8,128)(2,1)}, bf16[128,1536]{1,0:T(8,128)(2,1)S(1)}, u32[]{:S(2)}, u32[]{:S(2)}) collective-permute-start(bf16[128,1536]{1,0:T(8,128)(2,1)} %bitcast.8), channel_id=1, source_target_pairs={{0,16},{16,0},{1,17},{17,1},{2,18},{18,2},{3,19},{19,3},{4,20},{20... | collective-permute-start | bytes 1179656 | tf_op jit(solution)/shard_map/ppermute | solution.py:401
  0.7 29.4 %collective-permute-start = (bf16[256,768]{1,0:T(8,128)(2,1)}, bf16[256,768]{1,0:T(8,128)(2,1)S(1)}, u32[]{:S(2)}, u32[]{:S(2)}) collective-permute-start(bf16[256,768]{1,0:T(8,128)(2,1)} %bitcast.12), channel_id=1, source_target_pairs={{0,4},{1,5},{2,6},{3,7},{4,0},{5,1},{6,2},{7,3},{8,12},{9,13},{10,... | collective-permute-start | bytes 1179656 | tf_op jit(solution)/shard_map/ppermute | solution.py:371
  4.5 29.2 %copy-start.4 = (bf16[256,768]{1,0:T(8,128)(2,1)S(1)}, bf16[256,768]{1,0:T(8,128)(2,1)}, u32[]{:S(2)}) copy-start(bf16[256,768]{1,0:T(8,128)(2,1)} %get-tuple-element.30.q_ref.refs_3_) | copy-start | bytes 1179652
  4.5 34.0 %copy-start.1 = (bf16[2,256,384]{2,1,0:T(8,128)(2,1)S(1)}, bf16[2,256,384]{2,1,0:T(8,128)(2,1)}, u32[]{:S(2)}) copy-start(bf16[2,256,384]{2,1,0:T(8,128)(2,1)} %get-tuple-element.31.refs_0_.refs_10_) | copy-start | bytes 1179652
  4.5 34.0 %copy-start.3 = (bf16[2,256,384]{2,1,0:T(8,128)(2,1)S(1)}, bf16[2,256,384]{2,1,0:T(8,128)(2,1)}, u32[]{:S(2)}) copy-start(bf16[2,256,384]{2,1,0:T(8,128)(2,1)} %get-tuple-element.32.refs_3_.refs_13_) | copy-start | bytes 1179652
  4.5 25.7 %collective-permute-start.2 = (bf16[2,256,384]{2,1,0:T(8,128)(2,1)}, bf16[2,256,384]{2,1,0:T(8,128)(2,1)S(1)}, u32[]{:S(2)}, u32[]{:S(2)}) collective-permute-start(bf16[2,256,384]{2,1,0:T(8,128)(2,1)} %get-tuple-element.31.refs_0_.refs_10_), channel_id=1, source_target_pairs={{0,1},{4,5},{2,3},{6,7},{1,0},{5,4},{3,2},{7,6},{8,9},{12,13},{10,... | collective-permute-start | bytes 1179656 | tf_op jit(solution)/shard_map/ppermute | solution.py:418
  6.1 24.1 %collective-permute-start.3 = (bf16[2,256,384]{2,1,0:T(8,128)(2,1)}, bf16[2,256,384]{2,1,0:T(8,128)(2,1)S(1)}, u32[]{:S(2)}, u32[]{:S(2)}) collective-permute-start(bf16[2,256,384]{2,1,0:T(8,128)(2,1)} %get-tuple-element.31.refs_0_.refs_10_), channel_id=1, source_target_pairs={{1,2},{5,6},{2,1},{6,5},{9,10},{13,14},{10,9},{14,13},{17,18},{21,... | collective-permute-start | bytes 1179656 | tf_op jit(solution)/shard_map/ppermute | solution.py:418
  8.2 22.0 %collective-permute-start.4 = (bf16[2,256,384]{2,1,0:T(8,128)(2,1)}, bf16[2,256,384]{2,1,0:T(8,128)(2,1)S(1)}, u32[]{:S(2)}, u32[]{:S(2)}) collective-permute-start(bf16[2,256,384]{2,1,0:T(8,128)(2,1)} %get-tuple-element.32.refs_3_.refs_13_), channel_id=1, source_target_pairs={{0,8},{8,0},{1,9},{9,1},{2,10},{10,2},{3,11},{11,3},{4,12},{12,4},... | collective-permute-start | bytes 1179656 | tf_op jit(solution)/shard_map/ppermute | solution.py:419
  10.0 1.0 %copy-start.5 = (bf16[1,1,128,1536]{3,2,1,0:T(8,128)(2,1)S(1)}, bf16[1,1,128,1536]{3,2,1,0:T(8,128)(2,1)}, u32[]{:S(2)}) copy-start(bf16[1,1,128,1536]{3,2,1,0:T(8,128)(2,1)} %param.9) | copy-start | bytes 1179652
  11.0 0.7 copy-start.6
  11.8 26.7 %collective-permute-start.5 = (bf16[256,768]{1,0:T(8,128)(2,1)S(1)}, bf16[256,768]{1,0:T(8,128)(2,1)S(1)}, u32[]{:S(2)}, u32[]{:S(2)}) collective-permute-start(bf16[256,768]{1,0:T(8,128)(2,1)S(1)} %gather_grad.1.grad_ref.refs_4_), channel_id=1, source_target_pairs={{0,4},{1,5},{2,6},{3,7},{4,0},{5,1},{6,2},{7,3},{8,12},{9,13},{10,... | collective-permute-start | bytes 1179656 | tf_op jit(solution)/shard_map/ppermute | solution.py:371
  30.3 1.0 %copy-start = (bf16[2,256,384]{2,1,0:T(8,128)(2,1)S(1)}, bf16[2,256,384]{2,1,0:T(8,128)(2,1)}, u32[]{:S(2)}) copy-start(bf16[2,256,384]{2,1,0:T(8,128)(2,1)} %get-tuple-element.31.refs_0_.refs_10_) | copy-start | bytes 1179652
  31.3 1.0 %copy-start.2 = (bf16[2,256,384]{2,1,0:T(8,128)(2,1)S(1)}, bf16[2,256,384]{2,1,0:T(8,128)(2,1)}, u32[]{:S(2)}) copy-start(bf16[2,256,384]{2,1,0:T(8,128)(2,1)} %get-tuple-element.32.refs_3_.refs_13_) | copy-start | bytes 1179652
  39.3 4.8 %collective-permute-start.6 = (f32[8,768]{1,0:T(8,128)S(1)}, f32[8,768]{1,0:T(8,128)S(1)}, u32[]{:S(2)}, u32[]{:S(2)}) collective-permute-start(f32[8,768]{1,0:T(8,128)S(1)} %get-tuple-element.42.refs_15_), channel_id=1, source_target_pairs={{0,4},{1,5},{2,6},{3,7},{4,0},{5,1},{6,2},{7,3},{8,12},{9,13},{10,... | collective-permute-start | bytes 73736 | tf_op jit(solution)/shard_map/ppermute | solution.py:491
  46.4 16.8 %collective-permute-start.7 = (bf16[256,768]{1,0:T(8,128)(2,1)S(1)}, bf16[256,768]{1,0:T(8,128)(2,1)S(1)}, u32[]{:S(2)}, u32[]{:S(2)}) collective-permute-start(bf16[256,768]{1,0:T(8,128)(2,1)S(1)} %get-tuple-element.44), channel_id=1, source_target_pairs={{0,4},{1,5},{2,6},{3,7},{4,0},{5,1},{6,2},{7,3},{8,12},{9,13},{10,... | collective-permute-start | bytes 1179656 | tf_op jit(solution)/shard_map/ppermute | solution.py:465
  46.5 17.6 %collective-permute-start.8 = (bf16[2,256,384]{2,1,0:T(8,128)(2,1)S(1)}, bf16[2,256,384]{2,1,0:T(8,128)(2,1)S(1)}, u32[]{:S(2)}, u32[]{:S(2)}) collective-permute-start(bf16[2,256,384]{2,1,0:T(8,128)(2,1)S(1)} %get-tuple-element.48), channel_id=1, source_target_pairs={{0,1},{4,5},{2,3},{6,7},{1,0},{5,4},{3,2},{7,6},{8,9},{12,13},{10,... | collective-permute-start | bytes 1179656 | tf_op jit(solution)/shard_map/ppermute | solution.py:466
  48.1 20.8 %collective-permute-start.9 = (bf16[2,256,384]{2,1,0:T(8,128)(2,1)S(1)}, bf16[2,256,384]{2,1,0:T(8,128)(2,1)S(1)}, u32[]{:S(2)}, u32[]{:S(2)}) collective-permute-start(bf16[2,256,384]{2,1,0:T(8,128)(2,1)S(1)} %get-tuple-element.49), channel_id=1, source_target_pairs={{1,2},{5,6},{2,1},{6,5},{9,10},{13,14},{10,9},{14,13},{17,18},{21,... | collective-permute-start | bytes 1179656 | tf_op jit(solution)/shard_map/ppermute | solution.py:466
  52.5 16.4 %collective-permute-start.10 = (bf16[2,256,384]{2,1,0:T(8,128)(2,1)S(1)}, bf16[2,256,384]{2,1,0:T(8,128)(2,1)S(1)}, u32[]{:S(2)}, u32[]{:S(2)}) collective-permute-start(bf16[2,256,384]{2,1,0:T(8,128)(2,1)S(1)} %get-tuple-element.50), channel_id=1, source_target_pairs={{0,8},{8,0},{1,9},{9,1},{2,10},{10,2},{3,11},{11,3},{4,12},{12,4},... | collective-permute-start | bytes 1179656 | tf_op jit(solution)/shard_map/ppermute | solution.py:475

commit v4 on v3

--- a/solution.py
+++ b/solution.py
@@ -250,20 +250,24 @@
             log_totals.append(log_total)
             row_dots.append(row_dot)
 
-        def tile_grads(block, log_totals=log_totals, row_dots=row_dots):
+        def tile_grads(block, places, log_totals=log_totals, row_dots=row_dots):
             softmax, grad_scores = [], []
-            for (weight_ref, top_ref, slope_ref, _, _), log_total, row_dot in zip(
-                sets, log_totals, row_dots
-            ):
-                scale = jnp.exp2(top_ref[block : block + 1, :] - log_total)
+            for place in places:
+                weight_ref, top_ref, slope_ref, _, _ = sets[place]
+                scale = jnp.exp2(top_ref[block : block + 1, :] - log_totals[place])
                 part = weight_ref[block] * scale
                 softmax.append(part.astype(jnp.bfloat16))
-                grad_scores.append((part * (slope_ref[block] - row_dot)).astype(jnp.bfloat16))
+                part = part * (slope_ref[block] - row_dots[place])
+                grad_scores.append(part.astype(jnp.bfloat16))
             return jnp.concatenate(softmax, axis=1), jnp.concatenate(grad_scores, axis=1)
 
         q = jnp.concatenate([q_ref[:, cols] for _, _, _, q_ref, _ in sets], axis=0)
         grad = jnp.concatenate([grad_ref[:, cols] for _, _, _, _, grad_ref in sets], axis=0)
         yield kind, cols, q, grad, slots, tile_grads
+
+
+def add(total, term):
+    return term if total is None else total + term
 
 
 def first_grads_kernel(plan, *refs):
@@ -271,21 +275,27 @@
     take = lambda n: [refs.pop(0) for _ in range(n)]
     sets = [take(5) for _ in range(1 + plan.nr)]
     kv_refs, total_refs = take(2 + plan.nc + plan.nf), take(plan.n_totals)
-    dq_refs = take(1 + plan.nr)
+    dq_refs = take(plan.nr)
+    tile = plan.tile
+    everyone, far = range(1 + plan.nr), range(1, 1 + plan.nr)
     for kind, cols, q, grad, slots, tile_grads in head_grads(plan, sets, total_refs, kv_refs):
         query_grad = None
         for slot, (block, ref, at, _) in enumerate(slots):
-            softmax, grad_scores = tile_grads(block)
-            term = dot(ref[0, :, at], grad_scores, TN)
-            query_grad = term if query_grad is None else query_grad + term
-            if kind == 0 and slot > 0:
+            near = kind == 0 and slot > 0
+            if not near and not dq_refs:
+                continue
+            softmax, grad_scores = tile_grads(block, everyone if near else far)
+            if dq_refs:
+                far_scores = grad_scores[:, tile:] if near else grad_scores
+                query_grad = add(query_grad, dot(ref[0, :, at], far_scores, TN))
+            if near:
                 dk = dot(grad_scores, q, NN) * plan.scale
                 refs[slot - 1][0, :, at] = dk.astype(jnp.bfloat16)
                 refs[slot - 1][1, :, at] = dot(softmax, grad, NN).astype(jnp.bfloat16)
-        query_grad = jnp.transpose(query_grad * plan.scale)
+        if dq_refs:
+            query_grad = jnp.transpose(query_grad * plan.scale)
         for at, ref in enumerate(dq_refs):
-            rows = query_grad[at * plan.tile : (at + 1) * plan.tile]
-            ref[:, cols] = rows.astype(ref.dtype)
+            ref[:, cols] = query_grad[at * tile : (at + 1) * tile].astype(ref.dtype)
 
 
 def last_grads_kernel(plan, *refs):
@@ -293,10 +303,17 @@
     take = lambda n: [refs.pop(0) for _ in range(n)]
     sets = [take(5) for _ in range(1 + plan.nr)]
     kv_refs, total_refs = take(2 + plan.nc + plan.nf), take(plan.n_totals)
-    own_refs = take(2)
+    dq_ref, *own_refs = take(3)
+    tile = plan.tile
+    everyone, own = range(1 + plan.nr), range(1)
     for kind, cols, q, grad, slots, tile_grads in head_grads(plan, sets, total_refs, kv_refs):
-        for slot, (block, ref, at, _) in enumerate(slots if kind else slots[:1]):
-            softmax, grad_scores = tile_grads(block)
+        query_grad = None
+        for slot, (block, ref, at, _) in enumerate(slots):
+            near = kind == 0 and slot > 0
+            softmax, grad_scores = tile_grads(block, own if near else everyone)
+            query_grad = add(query_grad, dot(ref[0, :, at], grad_scores[:, :tile], TN))
+            if near:
+                continue
             dk = dot(grad_scores, q, NN) * plan.scale
             dv = dot(softmax, grad, NN)
             for i, out in enumerate((dk, dv)):
@@ -304,6 +321,7 @@
                     own_refs[i][:, cols] = out
                 else:
                     refs[slot - 1][i, :, at] = out.astype(jnp.bfloat16)
+        dq_ref[:, cols] = jnp.transpose(query_grad * plan.scale)
 
 
 def add_query_kernel(plan, table_ref, *refs):
@@ -457,18 +475,17 @@
     outs = call(
         first_grads_kernel,
         "first_grads",
-        [wide] + [low] * plan.nr + [packed] * plan.nc,
+        [low] * plan.nr + [packed] * plan.nc,
         2 * nq * matmul,
         *operands,
     )
-    own_dq, far_dq, plane_out = outs[0], outs[1:nq], outs[nq:]
+    far_dq, plane_out = outs[: plan.nr], outs[plan.nr :]
     back = [lax.ppermute(x, "tile", r) for x, r in zip(far_dq, row_routes)]
     back_plane = [lax.ppermute(x, "tile", r) for x, r in zip(plane_out, col_routes)]
-    operands[-1], _ = lax.optimization_barrier((operands[-1], own_dq))
-    own_dk, own_dv, *across_out = call(
+    own_dq, own_dk, own_dv, *across_out = call(
         last_grads_kernel,
         "last_grads",
-        [wide] * 2 + [packed] * plan.nf,
+        [wide] * 3 + [packed] * plan.nf,
         nq * matmul,
         *operands,
     )

time: 70.5 us -> 69.8 us (0.990)
  transfers between devices with their start and end apart: 11 -> 11, of which waited for: 5 -> 5; matrix products, arithmetic and copies ran while one was open for 0% -> 0% of each run, Pallas kernels for 13% -> 14%
where the time goes in v4:
time: 69.8 us; the launch traced here: 69.4 us
  waiting for transfers between devices  37.3 us (53%)
  starting transfers between devices  14.2 us (20%)
  Pallas kernels  13.3 us (19%)
  local copies, waits for them, and re-layouts  3.67 us (5%)
  between operations  0.8 us (1%)
    ppermute x2, waiting for transfers between devices, from_rows(): return [lax.ppermute(x, 'tile', route) for route in row_routes]  19.1 us
    pallas_call x9, Pallas kernels, call(): pl.pallas_call(functools.partial(kernel, plan), out_shape=out_shape, in_s...  9.95 us
    ppermute x1, waiting for transfers between devices, local(): back = [lax.ppermute(x, 'tile', r) for x, r in zip(far_dq, row_routes)]  8.67 us
    ppermute x2, waiting for transfers between devices, local(): lax.ppermute(x, 'tile', r)  4.84 us
    ppermute x1, waiting for transfers between devices, share_totals(): back = lax.ppermute(far[0], 'tile', row_routes[0])  4.71 us
    ppermute x2, starting transfers between devices, local(): lax.ppermute(x, 'tile', r)  4.45 us
    unnamed x14, local copies, waits for them, and re-layouts  3.67 us
    pallas_call x1, Pallas kernels, local(): pl.pallas_call(functools.partial(prepare_kernel, plan), out_shape=[table_...  3.39 us
  transfers between devices with their start and end apart: 11, of which 5 were waited for; matrix products, arithmetic and copies ran while one was open for 0% of the time, Pallas kernels for 14%

profile of v4, /device:TPU:24, one launch (start us, length us, event | category | flops | bytes accessed | tf_op | source)
XLA Modules:
  0.0 69.4 jit_solution(1011325953815769248)
XLA Ops:
  0.6 0.1 collective-permute-start.1
  0.7 0.4 collective-permute-start
  1.1 3.4 %prepare.1 = (s32[8,128]{1,0:T(8,128)}, bf16[2,256,384]{2,1,0:T(8,128)(2,1)}, bf16[2,256,384]{2,1,0:T(8,128)(2,1)}, bf16[256,768]{1,0:T(8,128)(2,1)}) custom-call(s32[6,3,9]{2,1,0:T(4,128)} %bitcast.15, s32[2,8]{1,0:T(2,128)} %counts_ref.1, bf16[256,768]{1,0:T(8,128)(2,1)} %bitcast.13, bf16[256,768]{1,0:T(8,128)(2,1)} %bitcast.10, bf16[256,768]{1,0:T(8,128)(2,1)} %bitcast.11), custom_call_target="tpu_custom_call" | custom-call | tf_op jit(solution)/shard_map/prepare/pallas_call | solution.py:423
  4.5 0.0 copy-start.4
  4.5 0.0 copy-start.1
  4.5 0.0 copy-start.3
  4.5 1.6 %collective-permute-start.4 = (bf16[2,256,384]{2,1,0:T(8,128)(2,1)}, bf16[2,256,384]{2,1,0:T(8,128)(2,1)S(1)}, u32[]{:S(2)}, u32[]{:S(2)}) collective-permute-start(bf16[2,256,384]{2,1,0:T(8,128)(2,1)} %get-tuple-element.31.refs_3_.refs_13_), channel_id=1, source_target_pairs={{0,8},{8,0},{1,9},{9,1},{2,10},{10,2},{3,11},{11,3},{4,12},{12,4},... | collective-permute-start | bytes 1179656 | tf_op jit(solution)/shard_map/ppermute | solution.py:437
  6.1 3.3 %collective-permute-start.3 = (bf16[2,256,384]{2,1,0:T(8,128)(2,1)}, bf16[2,256,384]{2,1,0:T(8,128)(2,1)S(1)}, u32[]{:S(2)}, u32[]{:S(2)}) collective-permute-start(bf16[2,256,384]{2,1,0:T(8,128)(2,1)} %get-tuple-element.30.refs_0_.refs_10_), channel_id=1, source_target_pairs={{1,2},{5,6},{2,1},{6,5},{9,10},{13,14},{10,9},{14,13},{17,18},{21,... | collective-permute-start | bytes 1179656 | tf_op jit(solution)/shard_map/ppermute | solution.py:436
  9.4 0.1 collective-permute-start.2
  9.5 0.0 collective-permute-done.1.refs_0_
  9.5 0.0 copy-start.5
  9.5 1.0 %copy-done.5 = bf16[1,1,128,1536]{3,2,1,0:T(8,128)(2,1)S(1)} copy-done((bf16[1,1,128,1536]{3,2,1,0:T(8,128)(2,1)S(1)}, bf16[1,1,128,1536]{3,2,1,0:T(8,128)(2,1)}, u32[]{:S(2)}) %copy-start.5) | copy-done | bytes 393240
  10.5 0.0 copy-start.6
  10.5 0.7 copy-done.6
  11.2 0.1 gather_grad.1.grad_ref.refs_4_
  11.3 2.7 %collective-permute-start.5 = (bf16[256,768]{1,0:T(8,128)(2,1)S(1)}, bf16[256,768]{1,0:T(8,128)(2,1)S(1)}, u32[]{:S(2)}, u32[]{:S(2)}) collective-permute-start(bf16[256,768]{1,0:T(8,128)(2,1)S(1)} %gather_grad.1.grad_ref.refs_4_), channel_id=1, source_target_pairs={{0,4},{1,5},{2,6},{3,7},{4,0},{5,1},{6,2},{7,3},{8,12},{9,13},{10,... | collective-permute-start | bytes 1179656 | tf_op jit(solution)/shard_map/ppermute | solution.py:389
  14.0 16.2 %collective-permute-done.q_ref = bf16[256,768]{1,0:T(8,128)(2,1)S(1)} collective-permute-done((bf16[256,768]{1,0:T(8,128)(2,1)}, bf16[256,768]{1,0:T(8,128)(2,1)S(1)}, u32[]{:S(2)}, u32[]{:S(2)}) %collective-permute-start) | collective-permute-done | bytes 393248 | tf_op jit(solution)/shard_map/ppermute | solution.py:389
  30.1 0.1 order_queries.1.q_ref.refs_8_
  30.2 0.0 collective-permute-done.4.refs_4_.refs_14_
  30.2 0.0 collective-permute-done.3.refs_2_.refs_12_
  30.3 0.0 collective-permute-done.2.refs_1_.refs_11_
  30.3 0.0 copy-start
  30.3 1.0 %copy-done = bf16[2,256,384]{2,1,0:T(8,128)(2,1)S(1)} copy-done((bf16[2,256,384]{2,1,0:T(8,128)(2,1)S(1)}, bf16[2,256,384]{2,1,0:T(8,128)(2,1)}, u32[]{:S(2)}) %copy-start) | copy-done | bytes 393240
  31.3 0.0 copy-start.2
  31.3 1.0 %copy-done.2 = bf16[2,256,384]{2,1,0:T(8,128)(2,1)S(1)} copy-done((bf16[2,256,384]{2,1,0:T(8,128)(2,1)S(1)}, bf16[2,256,384]{2,1,0:T(8,128)(2,1)}, u32[]{:S(2)}) %copy-start.2) | copy-done | bytes 393240
  32.3 1.5 %far_weights.1 = (f32[15,256,256]{2,1,0:T(8,128)S(1)}, f32[16,256]{1,0:T(8,128)S(1)}, f32[16,256]{1,0:T(8,128)S(1)}) custom-call(s32[8,128]{1,0:T(8,128)S(1)} %copy-done.6, bf16[256,768]{1,0:T(8,128)(2,1)S(1)} %order_queries.1.q_ref.refs_8_, bf16[2,256,384]{2,1,0:T(8,128)(2,1)S(1)} %copy-done, ...), custom_call_target="tpu_custom_call" | custom-call | flops 251658240 | bytes 1048576 | tf_op jit(solution)/shard_map/far_weights/pallas_call | solution.py:397
  33.7 0.0 copy-done.4
  33.7 1.9 %own_rows.1 = (f32[15,256,256]{2,1,0:T(8,128)S(1)}, f32[16,256]{1,0:T(8,128)S(1)}, f32[15,256,256]{2,1,0:T(8,128)S(1)}, f32[4,768]{1,0:T(4,128)S(1)}) custom-call(s32[8,128]{1,0:T(8,128)S(1)} %copy-done.6, bf16[256,768]{1,0:T(8,128)(2,1)S(1)} %copy-done.4, bf16[256,768]{1,0:T(8,128)(2,1)S(1)} %gather_grad.1.grad_ref.refs_4_, ...), custom_call_target="tpu_custom_call" | custom-call | flops 503316480 | bytes 1048576 | tf_op jit(solution)/shard_map/own_rows/pallas_call | solution.py:397
  35.6 2.9 %collective-permute-done.5.grad_ref.refs_9_ = bf16[256,768]{1,0:T(8,128)(2,1)S(1)} collective-permute-done((bf16[256,768]{1,0:T(8,128)(2,1)S(1)}, bf16[256,768]{1,0:T(8,128)(2,1)S(1)}, u32[]{:S(2)}, u32[]{:S(2)}) %collective-permute-start.5) | collective-permute-done | bytes 393248 | tf_op jit(solution)/shard_map/ppermute | solution.py:389
  38.5 0.0 copy-done.1
  38.5 0.0 copy-done.3
  38.5 0.7 %far_totals.1 = (f32[15,256,256]{2,1,0:T(8,128)S(1)}, f32[8,768]{1,0:T(8,128)S(1)}) custom-call(f32[15,256,256]{2,1,0:T(8,128)S(1)} %get-tuple-element.36.weight_ref.refs_5_, f32[16,256]{1,0:T(8,128)S(1)} %get-tuple-element.37.top_ref.refs_6_, f32[16,256]{1,0:T(8,128)S(1)} %get-tuple-element.38.sum_ref, f32[4,768]{1,0:T(4,128)S(1)} %get-tuple-element.39.own_ref, ...), custom_call_target="tpu_custom_call" | custom-call | flops 251658240 | bytes 1048576 | tf_op jit(solution)/shard_map/far_totals/pallas_call | solution.py:397
  39.3 0.1 collective-permute-start.6
  39.3 4.7 %collective-permute-done.6.refs_16_ = f32[8,768]{1,0:T(8,128)S(1)} collective-permute-done((f32[8,768]{1,0:T(8,128)S(1)}, f32[8,768]{1,0:T(8,128)S(1)}, u32[]{:S(2)}, u32[]{:S(2)}) %collective-permute-start.6) | collective-permute-done | bytes 24608 | tf_op jit(solution)/shard_map/ppermute | solution.py:508
  44.0 1.7 %first_grads.1 = (bf16[256,768]{1,0:T(8,128)(2,1)S(1)}, bf16[2,256,384]{2,1,0:T(8,128)(2,1)S(1)}, bf16[2,256,384]{2,1,0:T(8,128)(2,1)S(1)}) custom-call(f32[15,256,256]{2,1,0:T(8,128)S(1)} %get-tuple-element.32.refs_0_, f32[16,256]{1,0:T(8,128)S(1)} %get-tuple-element.33.refs_1_, f32[15,256,256]{2,1,0:T(8,128)S(1)} %get-tuple-element.34.refs_2_, ...), custom_call_target="tpu_custom_call" | custom-call | flops 1006632960 | bytes 1048576 | tf_op jit(solution)/shard_map/first_grads/pallas_call | solution.py:397
  45.8 0.1 collective-permute-start.7
  45.8 1.6 %collective-permute-start.8 = (bf16[2,256,384]{2,1,0:T(8,128)(2,1)S(1)}, bf16[2,256,384]{2,1,0:T(8,128)(2,1)S(1)}, u32[]{:S(2)}, u32[]{:S(2)}) collective-permute-start(bf16[2,256,384]{2,1,0:T(8,128)(2,1)S(1)} %get-tuple-element.46), channel_id=1, source_target_pairs={{0,1},{4,5},{2,3},{6,7},{1,0},{5,4},{3,2},{7,6},{8,9},{12,13},{10,... | collective-permute-start | bytes 1179656 | tf_op jit(solution)/shard_map/ppermute | solution.py:484
  47.4 2.9 %collective-permute-start.9 = (bf16[2,256,384]{2,1,0:T(8,128)(2,1)S(1)}, bf16[2,256,384]{2,1,0:T(8,128)(2,1)S(1)}, u32[]{:S(2)}, u32[]{:S(2)}) collective-permute-start(bf16[2,256,384]{2,1,0:T(8,128)(2,1)S(1)} %get-tuple-element.47), channel_id=1, source_target_pairs={{1,2},{5,6},{2,1},{6,5},{9,10},{13,14},{10,9},{14,13},{17,18},{21,... | collective-permute-start | bytes 1179656 | tf_op jit(solution)/shard_map/ppermute | solution.py:484
  50.3 2.0 %last_grads.1 = (f32[256,768]{1,0:T(8,128)S(1)}, f32[256,768]{1,0:T(8,128)S(1)}, f32[256,768]{1,0:T(8,128)S(1)}, bf16[2,256,384]{2,1,0:T(8,128)(2,1)S(1)}) custom-call(f32[15,256,256]{2,1,0:T(8,128)S(1)} %get-tuple-element.32.refs_0_, f32[16,256]{1,0:T(8,128)S(1)} %get-tuple-element.33.refs_1_, f32[15,256,256]{2,1,0:T(8,128)S(1)} %get-tuple-element.34.refs_2_, ...), custom_call_target="tpu_custom_call" | custom-call | flops 503316480 | bytes 1048576 | tf_op jit(solution)/shard_map/last_grads/pallas_call | solution.py:397
  52.3 1.6 %collective-permute-start.10 = (bf16[2,256,384]{2,1,0:T(8,128)(2,1)S(1)}, bf16[2,256,384]{2,1,0:T(8,128)(2,1)S(1)}, u32[]{:S(2)}, u32[]{:S(2)}) collective-permute-start(bf16[2,256,384]{2,1,0:T(8,128)(2,1)S(1)} %get-tuple-element.48), channel_id=1, source_target_pairs={{0,8},{8,0},{1,9},{9,1},{2,10},{10,2},{3,11},{11,3},{4,12},{12,4},... | collective-permute-start | bytes 1179656 | tf_op jit(solution)/shard_map/ppermute | solution.py:492
  53.9 8.7 %collective-permute-done.7.refs_1_ = bf16[256,768]{1,0:T(8,128)(2,1)S(1)} collective-permute-done((bf16[256,768]{1,0:T(8,128)(2,1)S(1)}, bf16[256,768]{1,0:T(8,128)(2,1)S(1)}, u32[]{:S(2)}, u32[]{:S(2)}) %collective-permute-start.7) | collective-permute-done | bytes 393248 | tf_op jit(solution)/shard_map/ppermute | solution.py:483
  62.5 0.9 %add_query.1 = bf16[256,768]{1,0:T(8,128)(2,1)} custom-call(s32[8,128]{1,0:T(8,128)S(1)} %copy-done.6, f32[256,768]{1,0:T(8,128)S(1)} %get-tuple-element.42.refs_0_, bf16[256,768]{1,0:T(8,128)(2,1)S(1)} %collective-permute-done.7.refs_1_), custom_call_target="tpu_custom_call" | custom-call | bytes 1048576 | tf_op jit(solution)/shard_map/add_query/pallas_call | solution.py:397
  63.4 0.0 collective-permute-done.8.refs_2_
  63.4 4.8 %collective-permute-done.9.refs_3_ = bf16[2,256,384]{2,1,0:T(8,128)(2,1)S(1)} collective-permute-done((bf16[2,256,384]{2,1,0:T(8,128)(2,1)S(1)}, bf16[2,256,384]{2,1,0:T(8,128)(2,1)S(1)}, u32[]{:S(2)}, u32[]{:S(2)}) %collective-permute-start.9) | collective-permute-done | bytes 393248 | tf_op jit(solution)/shard_map/ppermute | solution.py:484
  68.3 0.0 collective-permute-done.10.refs_4_
  68.3 1.1 %add_key.1 = (bf16[256,768]{1,0:T(8,128)(2,1)}, bf16[256,768]{1,0:T(8,128)(2,1)}) custom-call(s32[8,128]{1,0:T(8,128)S(1)} %copy-done.6, f32[256,768]{1,0:T(8,128)S(1)} %get-tuple-element.44.refs_0_, f32[256,768]{1,0:T(8,128)S(1)} %get-tuple-element.45.refs_1_, bf16[2,256,384]{2,1,0:T(8,128)(2,1)S(1)} %collective-permute-done.8.refs_2_, ...), custom_call_target="tpu_custom_call" | custom-call | bytes 1048576 | tf_op jit(solution)/shard_map/add_key/pallas_call | solution.py:397
Async XLA Ops:
  0.6 8.9 %collective-permute-start.1 = (bf16[128,1536]{1,0:T(8,128)(2,1)}, bf16[128,1536]{1,0:T(8,128)(2,1)S(1)}, u32[]{:S(2)}, u32[]{:S(2)}) collective-permute-start(bf16[128,1536]{1,0:T(8,128)(2,1)} %bitcast.8), channel_id=1, source_target_pairs={{0,16},{16,0},{1,17},{17,1},{2,18},{18,2},{3,19},{19,3},{4,20},{20... | collective-permute-start | bytes 1179656 | tf_op jit(solution)/shard_map/ppermute | solution.py:419
  0.7 29.4 %collective-permute-start = (bf16[256,768]{1,0:T(8,128)(2,1)}, bf16[256,768]{1,0:T(8,128)(2,1)S(1)}, u32[]{:S(2)}, u32[]{:S(2)}) collective-permute-start(bf16[256,768]{1,0:T(8,128)(2,1)} %bitcast.12), channel_id=1, source_target_pairs={{0,4},{1,5},{2,6},{3,7},{4,0},{5,1},{6,2},{7,3},{8,12},{9,13},{10,... | collective-permute-start | bytes 1179656 | tf_op jit(solution)/shard_map/ppermute | solution.py:389
  4.5 29.2 %copy-start.4 = (bf16[256,768]{1,0:T(8,128)(2,1)S(1)}, bf16[256,768]{1,0:T(8,128)(2,1)}, u32[]{:S(2)}) copy-start(bf16[256,768]{1,0:T(8,128)(2,1)} %get-tuple-element.29.q_ref.refs_3_) | copy-start | bytes 1179652
  4.5 34.0 %copy-start.1 = (bf16[2,256,384]{2,1,0:T(8,128)(2,1)S(1)}, bf16[2,256,384]{2,1,0:T(8,128)(2,1)}, u32[]{:S(2)}) copy-start(bf16[2,256,384]{2,1,0:T(8,128)(2,1)} %get-tuple-element.30.refs_0_.refs_10_) | copy-start | bytes 1179652
  4.5 34.0 %copy-start.3 = (bf16[2,256,384]{2,1,0:T(8,128)(2,1)S(1)}, bf16[2,256,384]{2,1,0:T(8,128)(2,1)}, u32[]{:S(2)}) copy-start(bf16[2,256,384]{2,1,0:T(8,128)(2,1)} %get-tuple-element.31.refs_3_.refs_13_) | copy-start | bytes 1179652
  4.5 25.7 %collective-permute-start.4 = (bf16[2,256,384]{2,1,0:T(8,128)(2,1)}, bf16[2,256,384]{2,1,0:T(8,128)(2,1)S(1)}, u32[]{:S(2)}, u32[]{:S(2)}) collective-permute-start(bf16[2,256,384]{2,1,0:T(8,128)(2,1)} %get-tuple-element.31.refs_3_.refs_13_), channel_id=1, source_target_pairs={{0,8},{8,0},{1,9},{9,1},{2,10},{10,2},{3,11},{11,3},{4,12},{12,4},... | collective-permute-start | bytes 1179656 | tf_op jit(solution)/shard_map/ppermute | solution.py:437
  6.1 24.1 %collective-permute-start.3 = (bf16[2,256,384]{2,1,0:T(8,128)(2,1)}, bf16[2,256,384]{2,1,0:T(8,128)(2,1)S(1)}, u32[]{:S(2)}, u32[]{:S(2)}) collective-permute-start(bf16[2,256,384]{2,1,0:T(8,128)(2,1)} %get-tuple-element.30.refs_0_.refs_10_), channel_id=1, source_target_pairs={{1,2},{5,6},{2,1},{6,5},{9,10},{13,14},{10,9},{14,13},{17,18},{21,... | collective-permute-start | bytes 1179656 | tf_op jit(solution)/shard_map/ppermute | solution.py:436
  9.4 20.8 %collective-permute-start.2 = (bf16[2,256,384]{2,1,0:T(8,128)(2,1)}, bf16[2,256,384]{2,1,0:T(8,128)(2,1)S(1)}, u32[]{:S(2)}, u32[]{:S(2)}) collective-permute-start(bf16[2,256,384]{2,1,0:T(8,128)(2,1)} %get-tuple-element.30.refs_0_.refs_10_), channel_id=1, source_target_pairs={{0,1},{4,5},{2,3},{6,7},{1,0},{5,4},{3,2},{7,6},{8,9},{12,13},{10,... | collective-permute-start | bytes 1179656 | tf_op jit(solution)/shard_map/ppermute | solution.py:436
  9.5 1.0 %copy-start.5 = (bf16[1,1,128,1536]{3,2,1,0:T(8,128)(2,1)S(1)}, bf16[1,1,128,1536]{3,2,1,0:T(8,128)(2,1)}, u32[]{:S(2)}) copy-start(bf16[1,1,128,1536]{3,2,1,0:T(8,128)(2,1)} %param.9) | copy-start | bytes 1179652
  10.5 0.7 copy-start.6
  11.3 27.2 %collective-permute-start.5 = (bf16[256,768]{1,0:T(8,128)(2,1)S(1)}, bf16[256,768]{1,0:T(8,128)(2,1)S(1)}, u32[]{:S(2)}, u32[]{:S(2)}) collective-permute-start(bf16[256,768]{1,0:T(8,128)(2,1)S(1)} %gather_grad.1.grad_ref.refs_4_), channel_id=1, source_target_pairs={{0,4},{1,5},{2,6},{3,7},{4,0},{5,1},{6,2},{7,3},{8,12},{9,13},{10,... | collective-permute-start | bytes 1179656 | tf_op jit(solution)/shard_map/ppermute | solution.py:389
  30.3 1.0 %copy-start = (bf16[2,256,384]{2,1,0:T(8,128)(2,1)S(1)}, bf16[2,256,384]{2,1,0:T(8,128)(2,1)}, u32[]{:S(2)}) copy-start(bf16[2,256,384]{2,1,0:T(8,128)(2,1)} %get-tuple-element.30.refs_0_.refs_10_) | copy-start | bytes 1179652
  31.3 1.0 %copy-start.2 = (bf16[2,256,384]{2,1,0:T(8,128)(2,1)S(1)}, bf16[2,256,384]{2,1,0:T(8,128)(2,1)}, u32[]{:S(2)}) copy-start(bf16[2,256,384]{2,1,0:T(8,128)(2,1)} %get-tuple-element.31.refs_3_.refs_13_) | copy-start | bytes 1179652
  39.3 4.8 %collective-permute-start.6 = (f32[8,768]{1,0:T(8,128)S(1)}, f32[8,768]{1,0:T(8,128)S(1)}, u32[]{:S(2)}, u32[]{:S(2)}) collective-permute-start(f32[8,768]{1,0:T(8,128)S(1)} %get-tuple-element.41.refs_15_), channel_id=1, source_target_pairs={{0,4},{1,5},{2,6},{3,7},{4,0},{5,1},{6,2},{7,3},{8,12},{9,13},{10,... | collective-permute-start | bytes 73736 | tf_op jit(solution)/shard_map/ppermute | solution.py:508
  45.8 16.8 %collective-permute-start.7 = (bf16[256,768]{1,0:T(8,128)(2,1)S(1)}, bf16[256,768]{1,0:T(8,128)(2,1)S(1)}, u32[]{:S(2)}, u32[]{:S(2)}) collective-permute-start(bf16[256,768]{1,0:T(8,128)(2,1)S(1)} %get-tuple-element.43), channel_id=1, source_target_pairs={{0,4},{1,5},{2,6},{3,7},{4,0},{5,1},{6,2},{7,3},{8,12},{9,13},{10,... | collective-permute-start | bytes 1179656 | tf_op jit(solution)/shard_map/ppermute | solution.py:483
  45.8 17.6 %collective-permute-start.8 = (bf16[2,256,384]{2,1,0:T(8,128)(2,1)S(1)}, bf16[2,256,384]{2,1,0:T(8,128)(2,1)S(1)}, u32[]{:S(2)}, u32[]{:S(2)}) collective-permute-start(bf16[2,256,384]{2,1,0:T(8,128)(2,1)S(1)} %get-tuple-element.46), channel_id=1, source_target_pairs={{0,1},{4,5},{2,3},{6,7},{1,0},{5,4},{3,2},{7,6},{8,9},{12,13},{10,... | collective-permute-start | bytes 1179656 | tf_op jit(solution)/shard_map/ppermute | solution.py:484
  47.4 20.8 %collective-permute-start.9 = (bf16[2,256,384]{2,1,0:T(8,128)(2,1)S(1)}, bf16[2,256,384]{2,1,0:T(8,128)(2,1)S(1)}, u32[]{:S(2)}, u32[]{:S(2)}) collective-permute-start(bf16[2,256,384]{2,1,0:T(8,128)(2,1)S(1)} %get-tuple-element.47), channel_id=1, source_target_pairs={{1,2},{5,6},{2,1},{6,5},{9,10},{13,14},{10,9},{14,13},{17,18},{21,... | collective-permute-start | bytes 1179656 | tf_op jit(solution)/shard_map/ppermute | solution.py:484
  52.3 16.0 %collective-permute-start.10 = (bf16[2,256,384]{2,1,0:T(8,128)(2,1)S(1)}, bf16[2,256,384]{2,1,0:T(8,128)(2,1)S(1)}, u32[]{:S(2)}, u32[]{:S(2)}) collective-permute-start(bf16[2,256,384]{2,1,0:T(8,128)(2,1)S(1)} %get-tuple-element.48), channel_id=1, source_target_pairs={{0,8},{8,0},{1,9},{9,1},{2,10},{10,2},{3,11},{11,3},{4,12},{12,4},... | collective-permute-start | bytes 1179656 | tf_op jit(solution)/shard_map/ppermute | solution.py:492

commit v5 on v4

--- a/solution.py
+++ b/solution.py
@@ -238,17 +238,54 @@
         total_ref[totals_at(plan, 1, pair, kind)] = totals(parts)
 
 
+def add(total, term):
+    return term if total is None else total + term
+
+
+def far_sums_kernel(plan, weight_ref, top_ref, slope_ref, total_ref, *refs):
+    *kv_refs, grad_ref, key_ref = refs
+    for pair, kind, cols, slots in windows(plan, kv_refs):
+        totals = total_ref[totals_at(plan, 1, pair, kind)]
+        log_total, row_dot = totals[0:1], totals[1:2]
+        grad_sum, key_sum = None, None
+        for block, ref, at, _ in slots:
+            softmax = weight_ref[block] * jnp.exp2(top_ref[block : block + 1, :] - log_total)
+            grad_scores = softmax * (slope_ref[block] - row_dot)
+            key = ref[0, :, at]
+            grad_sum = add(grad_sum, dot(key, grad_scores.astype(jnp.bfloat16), TN))
+            key_sum = add(key_sum, dot(key, softmax.astype(jnp.bfloat16), TN))
+        grad_ref[cols, :] = grad_sum
+        key_ref[cols, :] = key_sum
+
+
+def far_queries_kernel(plan, *refs):
+    refs = list(refs)
+    take = lambda n: [refs.pop(0) for _ in range(n)]
+    total_refs = take(plan.n_totals)
+    sets = [take(3) for _ in range(plan.nr)]
+    for place, (local_ref, grad_ref, key_ref) in enumerate(sets):
+        for pair in range(plan.pairs):
+            for kind in (0, 1):
+                cols = pl.ds((2 * pair + kind) * plan.hd, plan.hd)
+                log_total, row_dot = all_totals(plan, total_refs, 1 + place, pair, kind)
+                local = local_ref[totals_at(plan, 1, pair, kind)]
+                share = jnp.exp2(local[0:1] - log_total) * plan.scale
+                total = grad_ref[cols, :] + (local[1:2] - row_dot) * key_ref[cols, :]
+                refs[place][:, cols] = jnp.transpose(total * share).astype(refs[place].dtype)
+
+
+def all_totals(plan, total_refs, place, pair, kind):
+    parts = []
+    for ref, at in plan.totals_of[place]:
+        part = total_refs[ref][totals_at(plan, at, pair, kind)]
+        parts.append((part[0:1], part[1:2]))
+    return merge(parts)
+
+
 def head_grads(plan, sets, total_refs, kv_refs):
     for pair, kind, cols, slots in windows(plan, kv_refs):
-        log_totals, row_dots = [], []
-        for places in plan.totals_of:
-            parts = []
-            for ref, place in places:
-                part = total_refs[ref][totals_at(plan, place, pair, kind)]
-                parts.append((part[0:1], part[1:2]))
-            log_total, row_dot = merge(parts)
-            log_totals.append(log_total)
-            row_dots.append(row_dot)
+        totals = [all_totals(plan, total_refs, at, pair, kind) for at in range(len(sets))]
+        log_totals, row_dots = zip(*totals)
 
         def tile_grads(block, places, log_totals=log_totals, row_dots=row_dots):
             softmax, grad_scores = [], []
@@ -266,36 +303,19 @@
         yield kind, cols, q, grad, slots, tile_grads
 
 
-def add(total, term):
-    return term if total is None else total + term
-
-
 def first_grads_kernel(plan, *refs):
     refs = list(refs)
     take = lambda n: [refs.pop(0) for _ in range(n)]
     sets = [take(5) for _ in range(1 + plan.nr)]
     kv_refs, total_refs = take(2 + plan.nc + plan.nf), take(plan.n_totals)
-    dq_refs = take(plan.nr)
-    tile = plan.tile
-    everyone, far = range(1 + plan.nr), range(1, 1 + plan.nr)
     for kind, cols, q, grad, slots, tile_grads in head_grads(plan, sets, total_refs, kv_refs):
-        query_grad = None
-        for slot, (block, ref, at, _) in enumerate(slots):
-            near = kind == 0 and slot > 0
-            if not near and not dq_refs:
-                continue
-            softmax, grad_scores = tile_grads(block, everyone if near else far)
-            if dq_refs:
-                far_scores = grad_scores[:, tile:] if near else grad_scores
-                query_grad = add(query_grad, dot(ref[0, :, at], far_scores, TN))
-            if near:
-                dk = dot(grad_scores, q, NN) * plan.scale
-                refs[slot - 1][0, :, at] = dk.astype(jnp.bfloat16)
-                refs[slot - 1][1, :, at] = dot(softmax, grad, NN).astype(jnp.bfloat16)
-        if dq_refs:
-            query_grad = jnp.transpose(query_grad * plan.scale)
-        for at, ref in enumerate(dq_refs):
-            ref[:, cols] = query_grad[at * tile : (at + 1) * tile].astype(ref.dtype)
+        if kind == 1:
+            continue
+        for (block, _, at, _), out_ref in zip(slots[1:], refs):
+            softmax, grad_scores = tile_grads(block, range(1 + plan.nr))
+            dk = dot(grad_scores, q, NN) * plan.scale
+            out_ref[0, :, at] = dk.astype(jnp.bfloat16)
+            out_ref[1, :, at] = dot(softmax, grad, NN).astype(jnp.bfloat16)
 
 
 def last_grads_kernel(plan, *refs):
@@ -472,14 +492,28 @@
 
     nq = 1 + plan.nr
     operands = [ref for refs in sets for ref in refs] + kv + shared
-    outs = call(
-        first_grads_kernel,
-        "first_grads",
-        [low] * plan.nr + [packed] * plan.nc,
-        2 * nq * matmul,
-        *operands,
+    parts = []
+    for (weight, top, slope, _, _), total in zip(sets[1:], far_totals):
+        sums = call(
+            far_sums_kernel,
+            "far_sums",
+            [jax.ShapeDtypeStruct((width, tile), jnp.float32)] * 2,
+            2 * matmul,
+            *(weight, top, slope, total, *kv),
+        )
+        parts.append((total, *sums))
+    far_dq = call(
+        far_queries_kernel,
+        "far_queries",
+        [low] * plan.nr,
+        0,
+        *(*shared, *(ref for part in parts for ref in part)),
     )
-    far_dq, plane_out = outs[: plan.nr], outs[plan.nr :]
+    plane_out = call(
+        first_grads_kernel, "first_grads", [packed] * plan.nc, nq * matmul, *operands
+    )
+    ready = lax.optimization_barrier((*far_dq, *plane_out))
+    far_dq, plane_out = ready[: plan.nr], ready[plan.nr :]
     back = [lax.ppermute(x, "tile", r) for x, r in zip(far_dq, row_routes)]
     back_plane = [lax.ppermute(x, "tile", r) for x, r in zip(plane_out, col_routes)]
     own_dq, own_dk, own_dv, *across_out = call(

time: 69.8 us -> 69.5 us (level)
  waiting for transfers between devices: 37.3 us -> 36.3 us
  Pallas kernels: 13.3 us -> 14 us
    ppermute x1, waiting for transfers between devices: 4.71 us -> 3.76 us  [share_totals(): back = lax.ppermute(far[0], 'tile', row_routes[0])]
    pallas_call x9 -> x11, Pallas kernels: 9.95 us -> 10.6 us  [call(): pl.pallas_call(functools.partial(kernel, plan), out_shape=out_shape, in_s...]
  transfers between devices with their start and end apart: 11 -> 11, of which waited for: 5 -> 5; matrix products, arithmetic and copies ran while one was open for 0% -> 0% of each run, Pallas kernels for 14% -> 16%
where the time goes in v5:
time: 69.5 us; the launch traced here: 69 us
  waiting for transfers between devices  36.3 us (52%)
  starting transfers between devices  14.2 us (20%)
  Pallas kernels  14 us (20%)
  local copies, waits for them, and re-layouts  3.68 us (5%)
  between operations  0.81 us (1%)
    ppermute x2, waiting for transfers between devices, from_rows(): return [lax.ppermute(x, 'tile', route) for route in row_routes]  19.1 us
    pallas_call x11, Pallas kernels, call(): pl.pallas_call(functools.partial(kernel, plan), out_shape=out_shape, in_s...  10.6 us
    ppermute x1, waiting for transfers between devices, local(): back = [lax.ppermute(x, 'tile', r) for x, r in zip(far_dq, row_routes)]  8.62 us
    ppermute x2, waiting for transfers between devices, local(): lax.ppermute(x, 'tile', r)  4.83 us
    ppermute x2, starting transfers between devices, local(): lax.ppermute(x, 'tile', r)  4.45 us
    ppermute x1, waiting for transfers between devices, share_totals(): back = lax.ppermute(far[0], 'tile', row_routes[0])  3.76 us
    unnamed x14, local copies, waits for them, and re-layouts  3.68 us
    pallas_call x1, Pallas kernels, local(): pl.pallas_call(functools.partial(prepare_kernel, plan), out_shape=[table_...  3.39 us
  transfers between devices with their start and end apart: 11, of which 5 were waited for; matrix products, arithmetic and copies ran while one was open for 0% of the time, Pallas kernels for 16%

profile of v5, /device:TPU:24, one launch (start us, length us, event | category | flops | bytes accessed | tf_op | source)
XLA Modules:
  0.0 69.0 jit_solution(17727775352675294718)
XLA Ops:
  0.6 0.1 collective-permute-start.1
  0.7 0.4 collective-permute-start
  1.1 3.4 %prepare.1 = (s32[8,128]{1,0:T(8,128)}, bf16[2,256,384]{2,1,0:T(8,128)(2,1)}, bf16[2,256,384]{2,1,0:T(8,128)(2,1)}, bf16[256,768]{1,0:T(8,128)(2,1)}) custom-call(s32[6,3,9]{2,1,0:T(4,128)} %bitcast.15, s32[2,8]{1,0:T(2,128)} %counts_ref.1, bf16[256,768]{1,0:T(8,128)(2,1)} %bitcast.13, bf16[256,768]{1,0:T(8,128)(2,1)} %bitcast.10, bf16[256,768]{1,0:T(8,128)(2,1)} %bitcast.11), custom_call_target="tpu_custom_call" | custom-call | tf_op jit(solution)/shard_map/prepare/pallas_call | solution.py:443
  4.5 0.0 copy-start.4
  4.5 0.0 copy-start.1
  4.5 0.0 copy-start.3
  4.5 1.6 %collective-permute-start.4 = (bf16[2,256,384]{2,1,0:T(8,128)(2,1)}, bf16[2,256,384]{2,1,0:T(8,128)(2,1)S(1)}, u32[]{:S(2)}, u32[]{:S(2)}) collective-permute-start(bf16[2,256,384]{2,1,0:T(8,128)(2,1)} %get-tuple-element.35.refs_3_.refs_13_), channel_id=1, source_target_pairs={{0,8},{8,0},{1,9},{9,1},{2,10},{10,2},{3,11},{11,3},{4,12},{12,4},... | collective-permute-start | bytes 1179656 | tf_op jit(solution)/shard_map/ppermute | solution.py:457
  6.1 3.3 %collective-permute-start.3 = (bf16[2,256,384]{2,1,0:T(8,128)(2,1)}, bf16[2,256,384]{2,1,0:T(8,128)(2,1)S(1)}, u32[]{:S(2)}, u32[]{:S(2)}) collective-permute-start(bf16[2,256,384]{2,1,0:T(8,128)(2,1)} %get-tuple-element.34.refs_0_.refs_10_), channel_id=1, source_target_pairs={{1,2},{5,6},{2,1},{6,5},{9,10},{13,14},{10,9},{14,13},{17,18},{21,... | collective-permute-start | bytes 1179656 | tf_op jit(solution)/shard_map/ppermute | solution.py:456
  9.4 0.1 collective-permute-start.2
  9.5 0.0 collective-permute-done.1.refs_0_
  9.5 0.0 copy-start.5
  9.5 1.0 %copy-done.5 = bf16[1,1,128,1536]{3,2,1,0:T(8,128)(2,1)S(1)} copy-done((bf16[1,1,128,1536]{3,2,1,0:T(8,128)(2,1)S(1)}, bf16[1,1,128,1536]{3,2,1,0:T(8,128)(2,1)}, u32[]{:S(2)}) %copy-start.5) | copy-done | bytes 393240
  10.5 0.0 copy-start.6
  10.5 0.7 copy-done.6
  11.2 0.1 gather_grad.1.grad_ref.refs_4_
  11.3 2.7 %collective-permute-start.5 = (bf16[256,768]{1,0:T(8,128)(2,1)S(1)}, bf16[256,768]{1,0:T(8,128)(2,1)S(1)}, u32[]{:S(2)}, u32[]{:S(2)}) collective-permute-start(bf16[256,768]{1,0:T(8,128)(2,1)S(1)} %gather_grad.1.grad_ref.refs_4_), channel_id=1, source_target_pairs={{0,4},{1,5},{2,6},{3,7},{4,0},{5,1},{6,2},{7,3},{8,12},{9,13},{10,... | collective-permute-start | bytes 1179656 | tf_op jit(solution)/shard_map/ppermute | solution.py:409
  14.0 16.2 %collective-permute-done.q_ref = bf16[256,768]{1,0:T(8,128)(2,1)S(1)} collective-permute-done((bf16[256,768]{1,0:T(8,128)(2,1)}, bf16[256,768]{1,0:T(8,128)(2,1)S(1)}, u32[]{:S(2)}, u32[]{:S(2)}) %collective-permute-start) | collective-permute-done | bytes 393248 | tf_op jit(solution)/shard_map/ppermute | solution.py:409
  30.1 0.1 order_queries.1.q_ref.refs_8_
  30.2 0.0 collective-permute-done.4.refs_4_.refs_14_
  30.2 0.0 collective-permute-done.3.refs_2_.refs_12_
  30.3 0.0 collective-permute-done.2.refs_1_.refs_11_
  30.3 0.0 copy-start
  30.3 1.0 %copy-done = bf16[2,256,384]{2,1,0:T(8,128)(2,1)S(1)} copy-done((bf16[2,256,384]{2,1,0:T(8,128)(2,1)S(1)}, bf16[2,256,384]{2,1,0:T(8,128)(2,1)}, u32[]{:S(2)}) %copy-start) | copy-done | bytes 393240
  31.3 0.0 copy-start.2
  31.3 1.0 %copy-done.2 = bf16[2,256,384]{2,1,0:T(8,128)(2,1)S(1)} copy-done((bf16[2,256,384]{2,1,0:T(8,128)(2,1)S(1)}, bf16[2,256,384]{2,1,0:T(8,128)(2,1)}, u32[]{:S(2)}) %copy-start.2) | copy-done | bytes 393240
  32.3 1.5 %far_weights.1 = (f32[15,256,256]{2,1,0:T(8,128)S(1)}, f32[16,256]{1,0:T(8,128)S(1)}, f32[16,256]{1,0:T(8,128)S(1)}) custom-call(s32[8,128]{1,0:T(8,128)S(1)} %copy-done.6, bf16[256,768]{1,0:T(8,128)(2,1)S(1)} %order_queries.1.q_ref.refs_8_, bf16[2,256,384]{2,1,0:T(8,128)(2,1)S(1)} %copy-done, ...), custom_call_target="tpu_custom_call" | custom-call | flops 251658240 | bytes 1048576 | tf_op jit(solution)/shard_map/far_weights/pallas_call | solution.py:417
  33.7 0.0 copy-done.4
  33.7 1.9 %own_rows.1 = (f32[15,256,256]{2,1,0:T(8,128)S(1)}, f32[16,256]{1,0:T(8,128)S(1)}, f32[15,256,256]{2,1,0:T(8,128)S(1)}, f32[4,768]{1,0:T(4,128)S(1)}) custom-call(s32[8,128]{1,0:T(8,128)S(1)} %copy-done.6, bf16[256,768]{1,0:T(8,128)(2,1)S(1)} %copy-done.4, bf16[256,768]{1,0:T(8,128)(2,1)S(1)} %gather_grad.1.grad_ref.refs_4_, ...), custom_call_target="tpu_custom_call" | custom-call | flops 503316480 | bytes 1048576 | tf_op jit(solution)/shard_map/own_rows/pallas_call | solution.py:417
  35.6 2.9 %collective-permute-done.5.grad_ref.refs_9_ = bf16[256,768]{1,0:T(8,128)(2,1)S(1)} collective-permute-done((bf16[256,768]{1,0:T(8,128)(2,1)S(1)}, bf16[256,768]{1,0:T(8,128)(2,1)S(1)}, u32[]{:S(2)}, u32[]{:S(2)}) %collective-permute-start.5) | collective-permute-done | bytes 393248 | tf_op jit(solution)/shard_map/ppermute | solution.py:409
  38.5 0.0 copy-done.1
  38.5 0.0 copy-done.3
  38.5 0.7 %far_totals.1 = (f32[15,256,256]{2,1,0:T(8,128)S(1)}, f32[8,768]{1,0:T(8,128)S(1)}) custom-call(f32[15,256,256]{2,1,0:T(8,128)S(1)} %get-tuple-element.40.weight_ref.refs_5_, f32[16,256]{1,0:T(8,128)S(1)} %get-tuple-element.41.top_ref.refs_6_, f32[16,256]{1,0:T(8,128)S(1)} %get-tuple-element.42.sum_ref, f32[4,768]{1,0:T(4,128)S(1)} %get-tuple-element.43.own_ref, ...), custom_call_target="tpu_custom_call" | custom-call | flops 251658240 | bytes 1048576 | tf_op jit(solution)/shard_map/far_totals/pallas_call | solution.py:417
  39.3 0.1 collective-permute-start.6
  39.3 0.9 %far_sums.1 = (f32[768,256]{1,0:T(8,128)S(1)}, f32[768,256]{1,0:T(8,128)S(1)}) custom-call(f32[15,256,256]{2,1,0:T(8,128)S(1)} %get-tuple-element.40.weight_ref.refs_5_, f32[16,256]{1,0:T(8,128)S(1)} %get-tuple-element.41.top_ref.refs_6_, f32[15,256,256]{2,1,0:T(8,128)S(1)} %get-tuple-element.44.refs_7_.slope_ref, ...), custom_call_target="tpu_custom_call" | custom-call | flops 503316480 | bytes 1048576 | tf_op jit(solution)/shard_map/far_sums/pallas_call | solution.py:417
  40.3 3.8 %collective-permute-done.6.refs_16_.refs_1_ = f32[8,768]{1,0:T(8,128)S(1)} collective-permute-done((f32[8,768]{1,0:T(8,128)S(1)}, f32[8,768]{1,0:T(8,128)S(1)}, u32[]{:S(2)}, u32[]{:S(2)}) %collective-permute-start.6) | collective-permute-done | bytes 24608 | tf_op jit(solution)/shard_map/ppermute | solution.py:542
  44.1 0.2 far_queries.1
  44.3 1.1 %first_grads.1 = (bf16[2,256,384]{2,1,0:T(8,128)(2,1)S(1)}, bf16[2,256,384]{2,1,0:T(8,128)(2,1)S(1)}) custom-call(f32[15,256,256]{2,1,0:T(8,128)S(1)} %get-tuple-element.36.refs_0_, f32[16,256]{1,0:T(8,128)S(1)} %get-tuple-element.37.refs_1_, f32[15,256,256]{2,1,0:T(8,128)S(1)} %get-tuple-element.38.refs_2_, bf16[256,768]{1,0:T(8,128)(2,1)S(1)} %copy-done.4, ...), custom_call_target="tpu_custom_call" | custom-call | flops 503316480 | bytes 1048576 | tf_op jit(solution)/shard_map/first_grads/pallas_call | solution.py:417
  45.4 0.1 collective-permute-start.7
  45.5 1.6 %collective-permute-start.8 = (bf16[2,256,384]{2,1,0:T(8,128)(2,1)S(1)}, bf16[2,256,384]{2,1,0:T(8,128)(2,1)S(1)}, u32[]{:S(2)}, u32[]{:S(2)}) collective-permute-start(bf16[2,256,384]{2,1,0:T(8,128)(2,1)S(1)} %get-tuple-element.54), channel_id=1, source_target_pairs={{0,1},{4,5},{2,3},{6,7},{1,0},{5,4},{3,2},{7,6},{8,9},{12,13},{10,... | collective-permute-start | bytes 1179656 | tf_op jit(solution)/shard_map/ppermute | solution.py:518
  47.1 2.9 %collective-permute-start.9 = (bf16[2,256,384]{2,1,0:T(8,128)(2,1)S(1)}, bf16[2,256,384]{2,1,0:T(8,128)(2,1)S(1)}, u32[]{:S(2)}, u32[]{:S(2)}) collective-permute-start(bf16[2,256,384]{2,1,0:T(8,128)(2,1)S(1)} %get-tuple-element.55), channel_id=1, source_target_pairs={{1,2},{5,6},{2,1},{6,5},{9,10},{13,14},{10,9},{14,13},{17,18},{21,... | collective-permute-start | bytes 1179656 | tf_op jit(solution)/shard_map/ppermute | solution.py:518
  49.9 2.0 %last_grads.1 = (f32[256,768]{1,0:T(8,128)S(1)}, f32[256,768]{1,0:T(8,128)S(1)}, f32[256,768]{1,0:T(8,128)S(1)}, bf16[2,256,384]{2,1,0:T(8,128)(2,1)S(1)}) custom-call(f32[15,256,256]{2,1,0:T(8,128)S(1)} %get-tuple-element.36.refs_0_, f32[16,256]{1,0:T(8,128)S(1)} %get-tuple-element.37.refs_1_, f32[15,256,256]{2,1,0:T(8,128)S(1)} %get-tuple-element.38.refs_2_, ...), custom_call_target="tpu_custom_call" | custom-call | flops 503316480 | bytes 1048576 | tf_op jit(solution)/shard_map/last_grads/pallas_call | solution.py:417
  52.0 1.6 %collective-permute-start.10 = (bf16[2,256,384]{2,1,0:T(8,128)(2,1)S(1)}, bf16[2,256,384]{2,1,0:T(8,128)(2,1)S(1)}, u32[]{:S(2)}, u32[]{:S(2)}) collective-permute-start(bf16[2,256,384]{2,1,0:T(8,128)(2,1)S(1)} %get-tuple-element.56), channel_id=1, source_target_pairs={{0,8},{8,0},{1,9},{9,1},{2,10},{10,2},{3,11},{11,3},{4,12},{12,4},... | collective-permute-start | bytes 1179656 | tf_op jit(solution)/shard_map/ppermute | solution.py:526
  53.6 8.6 %collective-permute-done.7.refs_1_ = bf16[256,768]{1,0:T(8,128)(2,1)S(1)} collective-permute-done((bf16[256,768]{1,0:T(8,128)(2,1)S(1)}, bf16[256,768]{1,0:T(8,128)(2,1)S(1)}, u32[]{:S(2)}, u32[]{:S(2)}) %collective-permute-start.7) | collective-permute-done | bytes 393248 | tf_op jit(solution)/shard_map/ppermute | solution.py:517
  62.2 0.9 %add_query.1 = bf16[256,768]{1,0:T(8,128)(2,1)} custom-call(s32[8,128]{1,0:T(8,128)S(1)} %copy-done.6, f32[256,768]{1,0:T(8,128)S(1)} %get-tuple-element.46.refs_0_, bf16[256,768]{1,0:T(8,128)(2,1)S(1)} %collective-permute-done.7.refs_1_), custom_call_target="tpu_custom_call" | custom-call | bytes 1048576 | tf_op jit(solution)/shard_map/add_query/pallas_call | solution.py:417
  63.1 0.0 collective-permute-done.8.refs_2_
  63.1 4.8 %collective-permute-done.9.refs_3_ = bf16[2,256,384]{2,1,0:T(8,128)(2,1)S(1)} collective-permute-done((bf16[2,256,384]{2,1,0:T(8,128)(2,1)S(1)}, bf16[2,256,384]{2,1,0:T(8,128)(2,1)S(1)}, u32[]{:S(2)}, u32[]{:S(2)}) %collective-permute-start.9) | collective-permute-done | bytes 393248 | tf_op jit(solution)/shard_map/ppermute | solution.py:518
  67.9 0.0 collective-permute-done.10.refs_4_
  67.9 1.1 %add_key.1 = (bf16[256,768]{1,0:T(8,128)(2,1)}, bf16[256,768]{1,0:T(8,128)(2,1)}) custom-call(s32[8,128]{1,0:T(8,128)S(1)} %copy-done.6, f32[256,768]{1,0:T(8,128)S(1)} %get-tuple-element.52.refs_0_, f32[256,768]{1,0:T(8,128)S(1)} %get-tuple-element.53.refs_1_, bf16[2,256,384]{2,1,0:T(8,128)(2,1)S(1)} %collective-permute-done.8.refs_2_, ...), custom_call_target="tpu_custom_call" | custom-call | bytes 1048576 | tf_op jit(solution)/shard_map/add_key/pallas_call | solution.py:417
Async XLA Ops:
  0.6 8.9 %collective-permute-start.1 = (bf16[128,1536]{1,0:T(8,128)(2,1)}, bf16[128,1536]{1,0:T(8,128)(2,1)S(1)}, u32[]{:S(2)}, u32[]{:S(2)}) collective-permute-start(bf16[128,1536]{1,0:T(8,128)(2,1)} %bitcast.8), channel_id=1, source_target_pairs={{0,16},{16,0},{1,17},{17,1},{2,18},{18,2},{3,19},{19,3},{4,20},{20... | collective-permute-start | bytes 1179656 | tf_op jit(solution)/shard_map/ppermute | solution.py:439
  0.7 29.4 %collective-permute-start = (bf16[256,768]{1,0:T(8,128)(2,1)}, bf16[256,768]{1,0:T(8,128)(2,1)S(1)}, u32[]{:S(2)}, u32[]{:S(2)}) collective-permute-start(bf16[256,768]{1,0:T(8,128)(2,1)} %bitcast.12), channel_id=1, source_target_pairs={{0,4},{1,5},{2,6},{3,7},{4,0},{5,1},{6,2},{7,3},{8,12},{9,13},{10,... | collective-permute-start | bytes 1179656 | tf_op jit(solution)/shard_map/ppermute | solution.py:409
  4.5 29.2 %copy-start.4 = (bf16[256,768]{1,0:T(8,128)(2,1)S(1)}, bf16[256,768]{1,0:T(8,128)(2,1)}, u32[]{:S(2)}) copy-start(bf16[256,768]{1,0:T(8,128)(2,1)} %get-tuple-element.33.q_ref.refs_3_) | copy-start | bytes 1179652
  4.5 34.0 %copy-start.1 = (bf16[2,256,384]{2,1,0:T(8,128)(2,1)S(1)}, bf16[2,256,384]{2,1,0:T(8,128)(2,1)}, u32[]{:S(2)}) copy-start(bf16[2,256,384]{2,1,0:T(8,128)(2,1)} %get-tuple-element.34.refs_0_.refs_10_) | copy-start | bytes 1179652
  4.5 34.0 %copy-start.3 = (bf16[2,256,384]{2,1,0:T(8,128)(2,1)S(1)}, bf16[2,256,384]{2,1,0:T(8,128)(2,1)}, u32[]{:S(2)}) copy-start(bf16[2,256,384]{2,1,0:T(8,128)(2,1)} %get-tuple-element.35.refs_3_.refs_13_) | copy-start | bytes 1179652
  4.5 25.7 %collective-permute-start.4 = (bf16[2,256,384]{2,1,0:T(8,128)(2,1)}, bf16[2,256,384]{2,1,0:T(8,128)(2,1)S(1)}, u32[]{:S(2)}, u32[]{:S(2)}) collective-permute-start(bf16[2,256,384]{2,1,0:T(8,128)(2,1)} %get-tuple-element.35.refs_3_.refs_13_), channel_id=1, source_target_pairs={{0,8},{8,0},{1,9},{9,1},{2,10},{10,2},{3,11},{11,3},{4,12},{12,4},... | collective-permute-start | bytes 1179656 | tf_op jit(solution)/shard_map/ppermute | solution.py:457
  6.1 24.1 %collective-permute-start.3 = (bf16[2,256,384]{2,1,0:T(8,128)(2,1)}, bf16[2,256,384]{2,1,0:T(8,128)(2,1)S(1)}, u32[]{:S(2)}, u32[]{:S(2)}) collective-permute-start(bf16[2,256,384]{2,1,0:T(8,128)(2,1)} %get-tuple-element.34.refs_0_.refs_10_), channel_id=1, source_target_pairs={{1,2},{5,6},{2,1},{6,5},{9,10},{13,14},{10,9},{14,13},{17,18},{21,... | collective-permute-start | bytes 1179656 | tf_op jit(solution)/shard_map/ppermute | solution.py:456
  9.4 20.8 %collective-permute-start.2 = (bf16[2,256,384]{2,1,0:T(8,128)(2,1)}, bf16[2,256,384]{2,1,0:T(8,128)(2,1)S(1)}, u32[]{:S(2)}, u32[]{:S(2)}) collective-permute-start(bf16[2,256,384]{2,1,0:T(8,128)(2,1)} %get-tuple-element.34.refs_0_.refs_10_), channel_id=1, source_target_pairs={{0,1},{4,5},{2,3},{6,7},{1,0},{5,4},{3,2},{7,6},{8,9},{12,13},{10,... | collective-permute-start | bytes 1179656 | tf_op jit(solution)/shard_map/ppermute | solution.py:456
  9.5 1.0 %copy-start.5 = (bf16[1,1,128,1536]{3,2,1,0:T(8,128)(2,1)S(1)}, bf16[1,1,128,1536]{3,2,1,0:T(8,128)(2,1)}, u32[]{:S(2)}) copy-start(bf16[1,1,128,1536]{3,2,1,0:T(8,128)(2,1)} %param.9) | copy-start | bytes 1179652
  10.5 0.7 copy-start.6
  11.3 27.2 %collective-permute-start.5 = (bf16[256,768]{1,0:T(8,128)(2,1)S(1)}, bf16[256,768]{1,0:T(8,128)(2,1)S(1)}, u32[]{:S(2)}, u32[]{:S(2)}) collective-permute-start(bf16[256,768]{1,0:T(8,128)(2,1)S(1)} %gather_grad.1.grad_ref.refs_4_), channel_id=1, source_target_pairs={{0,4},{1,5},{2,6},{3,7},{4,0},{5,1},{6,2},{7,3},{8,12},{9,13},{10,... | collective-permute-start | bytes 1179656 | tf_op jit(solution)/shard_map/ppermute | solution.py:409
  30.3 1.0 %copy-start = (bf16[2,256,384]{2,1,0:T(8,128)(2,1)S(1)}, bf16[2,256,384]{2,1,0:T(8,128)(2,1)}, u32[]{:S(2)}) copy-start(bf16[2,256,384]{2,1,0:T(8,128)(2,1)} %get-tuple-element.34.refs_0_.refs_10_) | copy-start | bytes 1179652
  31.3 1.0 %copy-start.2 = (bf16[2,256,384]{2,1,0:T(8,128)(2,1)S(1)}, bf16[2,256,384]{2,1,0:T(8,128)(2,1)}, u32[]{:S(2)}) copy-start(bf16[2,256,384]{2,1,0:T(8,128)(2,1)} %get-tuple-element.35.refs_3_.refs_13_) | copy-start | bytes 1179652
  39.3 4.8 %collective-permute-start.6 = (f32[8,768]{1,0:T(8,128)S(1)}, f32[8,768]{1,0:T(8,128)S(1)}, u32[]{:S(2)}, u32[]{:S(2)}) collective-permute-start(f32[8,768]{1,0:T(8,128)S(1)} %get-tuple-element.45.refs_15_.total_ref.refs_0_.refs_2_), channel_id=1, source_target_pairs={{0,4},{1,5},{2,6},{3,7},{4,0},{5,1},{6,2},{7,3},{8,12},{9,13},{10,... | collective-permute-start | bytes 73736 | tf_op jit(solution)/shard_map/ppermute | solution.py:542
  45.4 16.8 %collective-permute-start.7 = (bf16[256,768]{1,0:T(8,128)(2,1)S(1)}, bf16[256,768]{1,0:T(8,128)(2,1)S(1)}, u32[]{:S(2)}, u32[]{:S(2)}) collective-permute-start(bf16[256,768]{1,0:T(8,128)(2,1)S(1)} %far_queries.1), channel_id=1, source_target_pairs={{0,4},{1,5},{2,6},{3,7},{4,0},{5,1},{6,2},{7,3},{8,12},{9,13},{10,... | collective-permute-start | bytes 1179656 | tf_op jit(solution)/shard_map/ppermute | solution.py:517
  45.5 17.6 %collective-permute-start.8 = (bf16[2,256,384]{2,1,0:T(8,128)(2,1)S(1)}, bf16[2,256,384]{2,1,0:T(8,128)(2,1)S(1)}, u32[]{:S(2)}, u32[]{:S(2)}) collective-permute-start(bf16[2,256,384]{2,1,0:T(8,128)(2,1)S(1)} %get-tuple-element.54), channel_id=1, source_target_pairs={{0,1},{4,5},{2,3},{6,7},{1,0},{5,4},{3,2},{7,6},{8,9},{12,13},{10,... | collective-permute-start | bytes 1179656 | tf_op jit(solution)/shard_map/ppermute | solution.py:518
  47.1 20.8 %collective-permute-start.9 = (bf16[2,256,384]{2,1,0:T(8,128)(2,1)S(1)}, bf16[2,256,384]{2,1,0:T(8,128)(2,1)S(1)}, u32[]{:S(2)}, u32[]{:S(2)}) collective-permute-start(bf16[2,256,384]{2,1,0:T(8,128)(2,1)S(1)} %get-tuple-element.55), channel_id=1, source_target_pairs={{1,2},{5,6},{2,1},{6,5},{9,10},{13,14},{10,9},{14,13},{17,18},{21,... | collective-permute-start | bytes 1179656 | tf_op jit(solution)/shard_map/ppermute | solution.py:518
  52.0 15.9 %collective-permute-start.10 = (bf16[2,256,384]{2,1,0:T(8,128)(2,1)S(1)}, bf16[2,256,384]{2,1,0:T(8,128)(2,1)S(1)}, u32[]{:S(2)}, u32[]{:S(2)}) collective-permute-start(bf16[2,256,384]{2,1,0:T(8,128)(2,1)S(1)} %get-tuple-element.56), channel_id=1, source_target_pairs={{0,8},{8,0},{1,9},{9,1},{2,10},{10,2},{3,11},{11,3},{4,12},{12,4},... | collective-permute-start | bytes 1179656 | tf_op jit(solution)/shard_map/ppermute | solution.py:526

commit v6 on v5

--- a/solution.py
+++ b/solution.py
@@ -225,17 +225,41 @@
             sum_ref[block : block + 1, :] = total
 
 
-def far_totals_kernel(plan, weight_ref, top_ref, sum_ref, own_ref, grad_ref, *refs):
-    *kv_refs, slope_ref, total_ref = refs
+def far_values_kernel(plan, weight_ref, top_ref, sum_ref, *refs):
+    *kv_refs, log_ref, mean_ref = refs
+    for pair, kind, cols, slots in windows(plan, kv_refs):
+        tops = [top_ref[block : block + 1, :] for block, _, _, _ in slots]
+        top = functools.reduce(jnp.maximum, tops)
+        total, low_total, values = None, None, None
+        for slot_top, (block, ref, at, _) in zip(tops, slots):
+            scale = jnp.exp2(slot_top - top)
+            low = weight_ref[block].astype(jnp.bfloat16)
+            low_sum = jnp.sum(low.astype(jnp.float32), axis=0, keepdims=True)
+            total = add(total, scale * sum_ref[block : block + 1, :])
+            low_total = add(low_total, scale * low_sum)
+            values = add(values, scale * dot(ref[1, :, at], low, TN))
+        log_total = top + jnp.log(total) * LOG2E
+        log_ref[totals_at(plan, 0, pair, kind)] = jnp.concatenate([log_total] * 2, axis=0)
+        mean_ref[cols, :] = values / low_total
+
+
+def far_totals_kernel(plan, log_ref, mean_ref, own_ref, grad_ref, total_ref):
     total_ref[0:4, :] = own_ref[...]
-    for pair, kind, cols, slots in windows(plan, kv_refs):
-        parts = []
+    for pair in range(plan.pairs):
+        for kind in (0, 1):
+            cols = pl.ds((2 * pair + kind) * plan.hd, plan.hd)
+            grad = jnp.transpose(grad_ref[:, cols].astype(jnp.float32))
+            row_dot = jnp.sum(mean_ref[cols, :] * grad, axis=0, keepdims=True)
+            log_total = log_ref[totals_at(plan, 0, pair, kind)][0:1]
+            total = jnp.concatenate([log_total, row_dot], axis=0)
+            total_ref[totals_at(plan, 1, pair, kind)] = total
+
+
+def far_slopes_kernel(plan, grad_ref, *refs):
+    *kv_refs, slope_ref = refs
+    for _, _, cols, slots in windows(plan, kv_refs):
         for block, ref, at, _ in slots:
-            slope = dot(ref[1, :, at], grad_ref[:, cols], NT)
-            slope_ref[block] = slope
-            cross = jnp.sum(weight_ref[block] * slope, axis=0, keepdims=True)
-            parts.append((top_ref[block : block + 1, :], sum_ref[block : block + 1, :], cross))
-        total_ref[totals_at(plan, 1, pair, kind)] = totals(parts)
+            slope_ref[block] = dot(ref[1, :, at], grad_ref[:, cols], NT)
 
 
 def add(total, term):
@@ -359,10 +383,12 @@
     take = lambda n: [refs.pop(0) for _ in range(n)]
     flips, hd = table_rows(plan)[-1], plan.hd
     own, near = take(2), (take(plan.nc), take(plan.nf))
+    out_refs, (buffer, sems) = take(2), refs
+    copies = []
     for pair in range(plan.pairs):
         cols = [pl.ds((2 * pair + kind) * hd, hd) for kind in (0, 1)]
         near_at = pl.ds(pair * hd, hd)
-        for i, out_ref in enumerate(refs):
+        for i, out_ref in enumerate(out_refs):
             parts = []
             for kind in (0, 1):
                 total = own[i][:, cols[kind]]
@@ -370,7 +396,13 @@
                     total = total + ref[i, :, near_at].astype(jnp.float32)
                 parts.append(total)
             for at, head in zip(cols, in_order(table_ref, flips + pair, *parts)):
-                out_ref[:, at] = head.astype(out_ref.dtype)
+                buffer[i, :, at] = head.astype(buffer.dtype)
+            whole = pl.ds(2 * pair * hd, 2 * hd)
+            sem = sems.at[len(copies)]
+            copies.append(pltpu.make_async_copy(buffer.at[i, :, whole], out_ref.at[:, whole], sem))
+            copies[-1].start()
+    for copy in copies:
+        copy.wait()
 
 
 class Plan:
@@ -429,6 +461,7 @@
     low = jax.ShapeDtypeStruct((tile, width), jnp.bfloat16)
     wide = jax.ShapeDtypeStruct((tile, width), jnp.float32)
     packed = jax.ShapeDtypeStruct((2, tile, pairs * hd), jnp.bfloat16)
+    wide_turned = jax.ShapeDtypeStruct((width, tile), jnp.float32)
     blocks = block_count(plan)
     block_shape = jax.ShapeDtypeStruct((blocks, tile, tile), jnp.float32)
     rows_shape = jax.ShapeDtypeStruct((-(-blocks // 8) * 8, tile), jnp.float32)
@@ -478,13 +511,22 @@
             matmul,
             *(table, queries, *kv),
         )
-        slope, total = call(
+        log_total, mean = call(
+            far_values_kernel,
+            "far_values",
+            [totals_shape(plan, 1), wide_turned],
+            matmul,
+            *(weight, top, total, *kv),
+        )
+        (total,) = call(
             far_totals_kernel,
             "far_totals",
-            [block_shape, totals_shape(plan, 2)],
-            matmul,
-            *(weight, top, total, own_total, far, *kv),
+            [totals_shape(plan, 2)],
+            0,
+            *(log_total, mean, own_total, far),
         )
+        far, _ = lax.optimization_barrier((far, total))
+        (slope,) = call(far_slopes_kernel, "far_slopes", [block_shape], matmul, far, *kv)
         sets.append((weight, top, slope, queries, far))
         far_totals.append(total)
     shared, plan.totals_of = share_totals(own_total, far_totals, row_routes)
@@ -497,7 +539,7 @@
         sums = call(
             far_sums_kernel,
             "far_sums",
-            [jax.ShapeDtypeStruct((width, tile), jnp.float32)] * 2,
+            [wide_turned] * 2,
             2 * matmul,
             *(weight, top, slope, total, *kv),
         )
@@ -525,13 +567,20 @@
     )
     back_across = [lax.ppermute(x, "frame", r) for x, r in zip(across_out, frame_routes)]
     (dq,) = call(add_query_kernel, "add_query", [low], 0, table, own_dq, *back)
-    dk, dv = call(
-        add_key_kernel,
-        "add_key",
-        [low] * 2,
-        0,
-        *(table, own_dk, own_dv, *back_plane, *back_across),
-    )
+    operands = [table, own_dk, own_dv, *back_plane, *back_across]
+    dk, dv = pl.pallas_call(
+        functools.partial(add_key_kernel, plan),
+        out_shape=[low] * 2,
+        in_specs=[vm] * len(operands),
+        out_specs=[hbm] * 2,
+        scratch_shapes=[
+            pltpu.VMEM((2, tile, width), jnp.bfloat16),
+            pltpu.SemaphoreType.DMA((2 * pairs,)),
+        ],
+        compiler_params=params(),
+        cost_estimate=pl.CostEstimate(flops=0, bytes_accessed=BYTES, transcendentals=0),
+        name="add_key",
+    )(*operands)
     return dq[None, None], dk[None, None], dv[None, None]
 
 

time: 69.5 us -> 69.2 us (level)
  waiting for transfers between devices: 36.3 us -> 35.2 us
  Pallas kernels: 14 us -> 14.8 us
    pallas_call x0 -> x1, Pallas kernels: none -> 1.01 us  [local(): pl.pallas_call(functools.partial(add_key_kernel, plan), out_shape=[low] *...]
    ppermute x2, waiting for transfers between devices: 19.1 us -> 18.3 us  [from_rows(): return [lax.ppermute(x, 'tile', route) for route in row_routes]]
    pallas_call x11 -> x12, Pallas kernels: 10.6 us -> 10.4 us  [call(): pl.pallas_call(functools.partial(kernel, plan), out_shape=out_shape, in_s...]
    unnamed x14 -> x16, local copies, waits for them, and re-layouts: 3.68 us -> 3.68 us
  transfers between devices with their start and end apart: 11 -> 11, of which waited for: 5 -> 5; matrix products, arithmetic and copies ran while one was open for 0% -> 0% of each run, Pallas kernels for 16% -> 18%
where the time goes in v6:
time: 69.2 us; the launch traced here: 68.7 us
  waiting for transfers between devices  35.2 us (51%)
  Pallas kernels  14.8 us (21%)
  starting transfers between devices  14.2 us (21%)
  local copies, waits for them, and re-layouts  3.68 us (5%)
  between operations  0.84 us (1%)
    ppermute x2, waiting for transfers between devices, from_rows(): return [lax.ppermute(x, 'tile', route) for route in row_routes]  18.3 us
    pallas_call x12, Pallas kernels, call(): pl.pallas_call(functools.partial(kernel, plan), out_shape=out_shape, in_s...  10.4 us
    ppermute x1, waiting for transfers between devices, local(): back = [lax.ppermute(x, 'tile', r) for x, r in zip(far_dq, row_routes)]  9.02 us
    ppermute x2, waiting for transfers between devices, local(): lax.ppermute(x, 'tile', r)  4.76 us
    ppermute x2, starting transfers between devices, local(): lax.ppermute(x, 'tile', r)  4.45 us
    unnamed x16, local copies, waits for them, and re-layouts  3.68 us
    pallas_call x1, Pallas kernels, local(): pl.pallas_call(functools.partial(prepare_kernel, plan), out_shape=[table_...  3.39 us
    ppermute x2, starting transfers between devices, local(): near_plane = [lax.ppermute(plane_kv, 'tile', route) for route in col_routes]  3.34 us
  transfers between devices with their start and end apart: 11, of which 5 were waited for; matrix products, arithmetic and copies ran while one was open for 0% of the time, Pallas kernels for 18%

profile of v6, /device:TPU:24, one launch (start us, length us, event | category | flops | bytes accessed | tf_op | source)
XLA Modules:
  0.0 68.7 jit_solution(8630755601832849974)
XLA Ops:
  0.6 0.1 collective-permute-start.1
  0.7 0.4 collective-permute-start
  1.1 3.4 %prepare.1 = (s32[8,128]{1,0:T(8,128)}, bf16[2,256,384]{2,1,0:T(8,128)(2,1)}, bf16[2,256,384]{2,1,0:T(8,128)(2,1)}, bf16[256,768]{1,0:T(8,128)(2,1)}) custom-call(s32[6,3,9]{2,1,0:T(4,128)} %bitcast.15, s32[2,8]{1,0:T(2,128)} %counts_ref.1, bf16[256,768]{1,0:T(8,128)(2,1)} %bitcast.13, bf16[256,768]{1,0:T(8,128)(2,1)} %bitcast.10, bf16[256,768]{1,0:T(8,128)(2,1)} %bitcast.11), custom_call_target="tpu_custom_call" | custom-call | tf_op jit(solution)/shard_map/prepare/pallas_call | solution.py:476
  4.5 0.0 copy-start.1
  4.5 0.0 copy-start.3
  4.5 1.6 %collective-permute-start.4 = (bf16[2,256,384]{2,1,0:T(8,128)(2,1)}, bf16[2,256,384]{2,1,0:T(8,128)(2,1)S(1)}, u32[]{:S(2)}, u32[]{:S(2)}) collective-permute-start(bf16[2,256,384]{2,1,0:T(8,128)(2,1)} %get-tuple-element.36.refs_3_.refs_13_), channel_id=1, source_target_pairs={{0,8},{8,0},{1,9},{9,1},{2,10},{10,2},{3,11},{11,3},{4,12},{12,4},... | collective-permute-start | bytes 1179656 | tf_op jit(solution)/shard_map/ppermute | solution.py:490
  6.1 3.3 %collective-permute-start.3 = (bf16[2,256,384]{2,1,0:T(8,128)(2,1)}, bf16[2,256,384]{2,1,0:T(8,128)(2,1)S(1)}, u32[]{:S(2)}, u32[]{:S(2)}) collective-permute-start(bf16[2,256,384]{2,1,0:T(8,128)(2,1)} %get-tuple-element.35.refs_0_.refs_10_), channel_id=1, source_target_pairs={{1,2},{5,6},{2,1},{6,5},{9,10},{13,14},{10,9},{14,13},{17,18},{21,... | collective-permute-start | bytes 1179656 | tf_op jit(solution)/shard_map/ppermute | solution.py:489
  9.4 0.1 collective-permute-start.2
  9.5 0.0 collective-permute-done.1.refs_0_
  9.5 0.0 copy-start.5
  9.5 1.0 %copy-done.5 = bf16[1,1,128,1536]{3,2,1,0:T(8,128)(2,1)S(1)} copy-done((bf16[1,1,128,1536]{3,2,1,0:T(8,128)(2,1)S(1)}, bf16[1,1,128,1536]{3,2,1,0:T(8,128)(2,1)}, u32[]{:S(2)}) %copy-start.5) | copy-done | bytes 393240
  10.5 0.0 copy-start.6
  10.5 0.7 copy-done.6
  11.2 0.1 gather_grad.1.grad_ref.refs_4_
  11.3 2.7 %collective-permute-start.5 = (bf16[256,768]{1,0:T(8,128)(2,1)S(1)}, bf16[256,768]{1,0:T(8,128)(2,1)S(1)}, u32[]{:S(2)}, u32[]{:S(2)}) collective-permute-start(bf16[256,768]{1,0:T(8,128)(2,1)S(1)} %gather_grad.1.grad_ref.refs_4_), channel_id=1, source_target_pairs={{0,4},{1,5},{2,6},{3,7},{4,0},{5,1},{6,2},{7,3},{8,12},{9,13},{10,... | collective-permute-start | bytes 1179656 | tf_op jit(solution)/shard_map/ppermute | solution.py:441
  14.0 16.2 %collective-permute-done.q_ref = bf16[256,768]{1,0:T(8,128)(2,1)S(1)} collective-permute-done((bf16[256,768]{1,0:T(8,128)(2,1)}, bf16[256,768]{1,0:T(8,128)(2,1)S(1)}, u32[]{:S(2)}, u32[]{:S(2)}) %collective-permute-start) | collective-permute-done | bytes 393248 | tf_op jit(solution)/shard_map/ppermute | solution.py:441
  30.1 0.0 copy-start.4
  30.1 0.1 order_queries.1.q_ref.refs_8_
  30.2 0.0 collective-permute-done.4.refs_4_.refs_14_
  30.2 0.0 collective-permute-done.3.refs_2_.refs_12_
  30.3 0.0 collective-permute-done.2.refs_1_.refs_11_
  30.3 0.0 copy-start
  30.3 1.0 %copy-done = bf16[2,256,384]{2,1,0:T(8,128)(2,1)S(1)} copy-done((bf16[2,256,384]{2,1,0:T(8,128)(2,1)S(1)}, bf16[2,256,384]{2,1,0:T(8,128)(2,1)}, u32[]{:S(2)}) %copy-start) | copy-done | bytes 393240
  31.3 0.0 copy-start.2
  31.3 1.0 %copy-done.2 = bf16[2,256,384]{2,1,0:T(8,128)(2,1)S(1)} copy-done((bf16[2,256,384]{2,1,0:T(8,128)(2,1)S(1)}, bf16[2,256,384]{2,1,0:T(8,128)(2,1)}, u32[]{:S(2)}) %copy-start.2) | copy-done | bytes 393240
  32.3 1.5 %far_weights.1 = (f32[15,256,256]{2,1,0:T(8,128)S(1)}, f32[16,256]{1,0:T(8,128)S(1)}, f32[16,256]{1,0:T(8,128)S(1)}) custom-call(s32[8,128]{1,0:T(8,128)S(1)} %copy-done.6, bf16[256,768]{1,0:T(8,128)(2,1)S(1)} %order_queries.1.q_ref.refs_8_, bf16[2,256,384]{2,1,0:T(8,128)(2,1)S(1)} %copy-done, ...), custom_call_target="tpu_custom_call" | custom-call | flops 251658240 | bytes 1048576 | tf_op jit(solution)/shard_map/far_weights/pallas_call | solution.py:449
  33.7 0.0 copy-done.1
  33.7 0.0 copy-done.3
  33.7 0.7 %far_values.1 = (f32[4,768]{1,0:T(4,128)S(1)}, f32[768,256]{1,0:T(8,128)S(1)}) custom-call(f32[15,256,256]{2,1,0:T(8,128)S(1)} %get-tuple-element.41.weight_ref.refs_5_, f32[16,256]{1,0:T(8,128)S(1)} %get-tuple-element.42.top_ref.refs_6_, f32[16,256]{1,0:T(8,128)S(1)} %get-tuple-element.43.sum_ref, bf16[2,256,384]{2,1,0:T(8,128)(2,1)S(1)} %copy-done.1, ...), custom_call_target="tpu_custom_call" | custom-call | flops 251658240 | bytes 1048576 | tf_op jit(solution)/shard_map/far_values/pallas_call | solution.py:449
  34.5 0.0 copy-done.4
  34.5 1.9 %own_rows.1 = (f32[15,256,256]{2,1,0:T(8,128)S(1)}, f32[16,256]{1,0:T(8,128)S(1)}, f32[15,256,256]{2,1,0:T(8,128)S(1)}, f32[4,768]{1,0:T(4,128)S(1)}) custom-call(s32[8,128]{1,0:T(8,128)S(1)} %copy-done.6, bf16[256,768]{1,0:T(8,128)(2,1)S(1)} %copy-done.4, bf16[256,768]{1,0:T(8,128)(2,1)S(1)} %gather_grad.1.grad_ref.refs_4_, ...), custom_call_target="tpu_custom_call" | custom-call | flops 503316480 | bytes 1048576 | tf_op jit(solution)/shard_map/own_rows/pallas_call | solution.py:449
  36.4 2.1 %collective-permute-done.5.grad_ref.refs_9_ = bf16[256,768]{1,0:T(8,128)(2,1)S(1)} collective-permute-done((bf16[256,768]{1,0:T(8,128)(2,1)S(1)}, bf16[256,768]{1,0:T(8,128)(2,1)S(1)}, u32[]{:S(2)}, u32[]{:S(2)}) %collective-permute-start.5) | collective-permute-done | bytes 393248 | tf_op jit(solution)/shard_map/ppermute | solution.py:441
  38.5 0.2 far_totals.1.refs_15_.total_ref.refs_0_.refs_2_
  38.7 0.1 collective-permute-start.6
  38.8 0.7 far_slopes.1.refs_7_.slope_ref
  39.5 0.9 %far_sums.1 = (f32[768,256]{1,0:T(8,128)S(1)}, f32[768,256]{1,0:T(8,128)S(1)}) custom-call(f32[15,256,256]{2,1,0:T(8,128)S(1)} %get-tuple-element.41.weight_ref.refs_5_, f32[16,256]{1,0:T(8,128)S(1)} %get-tuple-element.42.top_ref.refs_6_, f32[15,256,256]{2,1,0:T(8,128)S(1)} %far_slopes.1.refs_7_.slope_ref, ...), custom_call_target="tpu_custom_call" | custom-call | flops 503316480 | bytes 1048576 | tf_op jit(solution)/shard_map/far_sums/pallas_call | solution.py:449
  40.4 3.1 %collective-permute-done.6.refs_16_.refs_1_ = f32[8,768]{1,0:T(8,128)S(1)} collective-permute-done((f32[8,768]{1,0:T(8,128)S(1)}, f32[8,768]{1,0:T(8,128)S(1)}, u32[]{:S(2)}, u32[]{:S(2)}) %collective-permute-start.6) | collective-permute-done | bytes 24608 | tf_op jit(solution)/shard_map/ppermute | solution.py:591
  43.5 0.2 far_queries.1
  43.7 1.1 %first_grads.1 = (bf16[2,256,384]{2,1,0:T(8,128)(2,1)S(1)}, bf16[2,256,384]{2,1,0:T(8,128)(2,1)S(1)}) custom-call(f32[15,256,256]{2,1,0:T(8,128)S(1)} %get-tuple-element.37.refs_0_, f32[16,256]{1,0:T(8,128)S(1)} %get-tuple-element.38.refs_1_, f32[15,256,256]{2,1,0:T(8,128)S(1)} %get-tuple-element.39.refs_2_, bf16[256,768]{1,0:T(8,128)(2,1)S(1)} %copy-done.4, ...), custom_call_target="tpu_custom_call" | custom-call | flops 503316480 | bytes 1048576 | tf_op jit(solution)/shard_map/first_grads/pallas_call | solution.py:449
  44.9 0.0 copy-start.7
  44.9 0.1 collective-permute-start.7
  45.0 1.6 %collective-permute-start.8 = (bf16[2,256,384]{2,1,0:T(8,128)(2,1)S(1)}, bf16[2,256,384]{2,1,0:T(8,128)(2,1)S(1)}, u32[]{:S(2)}, u32[]{:S(2)}) collective-permute-start(bf16[2,256,384]{2,1,0:T(8,128)(2,1)S(1)} %get-tuple-element.56), channel_id=1, source_target_pairs={{0,1},{4,5},{2,3},{6,7},{1,0},{5,4},{3,2},{7,6},{8,9},{12,13},{10,... | collective-permute-start | bytes 1179656 | tf_op jit(solution)/shard_map/ppermute | solution.py:560
  46.6 2.8 %collective-permute-start.9 = (bf16[2,256,384]{2,1,0:T(8,128)(2,1)S(1)}, bf16[2,256,384]{2,1,0:T(8,128)(2,1)S(1)}, u32[]{:S(2)}, u32[]{:S(2)}) collective-permute-start(bf16[2,256,384]{2,1,0:T(8,128)(2,1)S(1)} %get-tuple-element.57), channel_id=1, source_target_pairs={{1,2},{5,6},{2,1},{6,5},{9,10},{13,14},{10,9},{14,13},{17,18},{21,... | collective-permute-start | bytes 1179656 | tf_op jit(solution)/shard_map/ppermute | solution.py:560
  49.4 2.1 %last_grads.1 = (f32[256,768]{1,0:T(8,128)S(1)}, f32[256,768]{1,0:T(8,128)S(1)}, f32[256,768]{1,0:T(8,128)S(1)}, bf16[2,256,384]{2,1,0:T(8,128)(2,1)S(1)}) custom-call(f32[15,256,256]{2,1,0:T(8,128)S(1)} %get-tuple-element.37.refs_0_, f32[16,256]{1,0:T(8,128)S(1)} %get-tuple-element.38.refs_1_, f32[15,256,256]{2,1,0:T(8,128)S(1)} %get-tuple-element.39.refs_2_, ...), custom_call_target="tpu_custom_call" | custom-call | flops 503316480 | bytes 1048576 | tf_op jit(solution)/shard_map/last_grads/pallas_call | solution.py:449
  51.5 1.6 %collective-permute-start.10 = (bf16[2,256,384]{2,1,0:T(8,128)(2,1)S(1)}, bf16[2,256,384]{2,1,0:T(8,128)(2,1)S(1)}, u32[]{:S(2)}, u32[]{:S(2)}) collective-permute-start(bf16[2,256,384]{2,1,0:T(8,128)(2,1)S(1)} %get-tuple-element.58), channel_id=1, source_target_pairs={{0,8},{8,0},{1,9},{9,1},{2,10},{10,2},{3,11},{11,3},{4,12},{12,4},... | collective-permute-start | bytes 1179656 | tf_op jit(solution)/shard_map/ppermute | solution.py:568
  53.1 9.0 %collective-permute-done.7.refs_1_ = bf16[256,768]{1,0:T(8,128)(2,1)S(1)} collective-permute-done((bf16[256,768]{1,0:T(8,128)(2,1)S(1)}, bf16[256,768]{1,0:T(8,128)(2,1)S(1)}, u32[]{:S(2)}, u32[]{:S(2)}) %collective-permute-start.7) | collective-permute-done | bytes 393248 | tf_op jit(solution)/shard_map/ppermute | solution.py:559
  62.1 0.0 copy-done.7
  62.1 0.9 %add_query.1 = bf16[256,768]{1,0:T(8,128)(2,1)} custom-call(s32[8,128]{1,0:T(8,128)S(1)} %copy-done.7, f32[256,768]{1,0:T(8,128)S(1)} %get-tuple-element.48.refs_0_, bf16[256,768]{1,0:T(8,128)(2,1)S(1)} %collective-permute-done.7.refs_1_), custom_call_target="tpu_custom_call" | custom-call | bytes 1048576 | tf_op jit(solution)/shard_map/add_query/pallas_call | solution.py:449
  63.0 0.0 collective-permute-done.8.refs_2_
  63.0 4.8 %collective-permute-done.9.refs_3_ = bf16[2,256,384]{2,1,0:T(8,128)(2,1)S(1)} collective-permute-done((bf16[2,256,384]{2,1,0:T(8,128)(2,1)S(1)}, bf16[2,256,384]{2,1,0:T(8,128)(2,1)S(1)}, u32[]{:S(2)}, u32[]{:S(2)}) %collective-permute-start.9) | collective-permute-done | bytes 393248 | tf_op jit(solution)/shard_map/ppermute | solution.py:560
  67.7 0.0 collective-permute-done.10.refs_4_
  67.7 1.0 %add_key.1 = (bf16[256,768]{1,0:T(8,128)(2,1)}, bf16[256,768]{1,0:T(8,128)(2,1)}) custom-call(s32[8,128]{1,0:T(8,128)S(1)} %copy-done.7, f32[256,768]{1,0:T(8,128)S(1)} %get-tuple-element.54.refs_0_, f32[256,768]{1,0:T(8,128)S(1)} %get-tuple-element.55.refs_1_, bf16[2,256,384]{2,1,0:T(8,128)(2,1)S(1)} %collective-permute-done.8.refs_2_, ...), custom_call_target="tpu_custom_call" | custom-call | bytes 1048576 | tf_op jit(solution)/shard_map/add_key/pallas_call | solution.py:571
Async XLA Ops:
  0.6 8.8 %collective-permute-start.1 = (bf16[128,1536]{1,0:T(8,128)(2,1)}, bf16[128,1536]{1,0:T(8,128)(2,1)S(1)}, u32[]{:S(2)}, u32[]{:S(2)}) collective-permute-start(bf16[128,1536]{1,0:T(8,128)(2,1)} %bitcast.8), channel_id=1, source_target_pairs={{0,16},{16,0},{1,17},{17,1},{2,18},{18,2},{3,19},{19,3},{4,20},{20... | collective-permute-start | bytes 1179656 | tf_op jit(solution)/shard_map/ppermute | solution.py:472
  0.7 29.4 %collective-permute-start = (bf16[256,768]{1,0:T(8,128)(2,1)}, bf16[256,768]{1,0:T(8,128)(2,1)S(1)}, u32[]{:S(2)}, u32[]{:S(2)}) collective-permute-start(bf16[256,768]{1,0:T(8,128)(2,1)} %bitcast.12), channel_id=1, source_target_pairs={{0,4},{1,5},{2,6},{3,7},{4,0},{5,1},{6,2},{7,3},{8,12},{9,13},{10,... | collective-permute-start | bytes 1179656 | tf_op jit(solution)/shard_map/ppermute | solution.py:441
  4.5 29.2 %copy-start.1 = (bf16[2,256,384]{2,1,0:T(8,128)(2,1)S(1)}, bf16[2,256,384]{2,1,0:T(8,128)(2,1)}, u32[]{:S(2)}) copy-start(bf16[2,256,384]{2,1,0:T(8,128)(2,1)} %get-tuple-element.35.refs_0_.refs_10_) | copy-start | bytes 1179652
  4.5 29.2 %copy-start.3 = (bf16[2,256,384]{2,1,0:T(8,128)(2,1)S(1)}, bf16[2,256,384]{2,1,0:T(8,128)(2,1)}, u32[]{:S(2)}) copy-start(bf16[2,256,384]{2,1,0:T(8,128)(2,1)} %get-tuple-element.36.refs_3_.refs_13_) | copy-start | bytes 1179652
  4.5 25.7 %collective-permute-start.4 = (bf16[2,256,384]{2,1,0:T(8,128)(2,1)}, bf16[2,256,384]{2,1,0:T(8,128)(2,1)S(1)}, u32[]{:S(2)}, u32[]{:S(2)}) collective-permute-start(bf16[2,256,384]{2,1,0:T(8,128)(2,1)} %get-tuple-element.36.refs_3_.refs_13_), channel_id=1, source_target_pairs={{0,8},{8,0},{1,9},{9,1},{2,10},{10,2},{3,11},{11,3},{4,12},{12,4},... | collective-permute-start | bytes 1179656 | tf_op jit(solution)/shard_map/ppermute | solution.py:490
  6.1 24.1 %collective-permute-start.3 = (bf16[2,256,384]{2,1,0:T(8,128)(2,1)}, bf16[2,256,384]{2,1,0:T(8,128)(2,1)S(1)}, u32[]{:S(2)}, u32[]{:S(2)}) collective-permute-start(bf16[2,256,384]{2,1,0:T(8,128)(2,1)} %get-tuple-element.35.refs_0_.refs_10_), channel_id=1, source_target_pairs={{1,2},{5,6},{2,1},{6,5},{9,10},{13,14},{10,9},{14,13},{17,18},{21,... | collective-permute-start | bytes 1179656 | tf_op jit(solution)/shard_map/ppermute | solution.py:489
  9.4 20.9 %collective-permute-start.2 = (bf16[2,256,384]{2,1,0:T(8,128)(2,1)}, bf16[2,256,384]{2,1,0:T(8,128)(2,1)S(1)}, u32[]{:S(2)}, u32[]{:S(2)}) collective-permute-start(bf16[2,256,384]{2,1,0:T(8,128)(2,1)} %get-tuple-element.35.refs_0_.refs_10_), channel_id=1, source_target_pairs={{0,1},{4,5},{2,3},{6,7},{1,0},{5,4},{3,2},{7,6},{8,9},{12,13},{10,... | collective-permute-start | bytes 1179656 | tf_op jit(solution)/shard_map/ppermute | solution.py:489
  9.5 1.0 %copy-start.5 = (bf16[1,1,128,1536]{3,2,1,0:T(8,128)(2,1)S(1)}, bf16[1,1,128,1536]{3,2,1,0:T(8,128)(2,1)}, u32[]{:S(2)}) copy-start(bf16[1,1,128,1536]{3,2,1,0:T(8,128)(2,1)} %param.9) | copy-start | bytes 1179652
  10.5 0.7 copy-start.6
  11.3 27.2 %collective-permute-start.5 = (bf16[256,768]{1,0:T(8,128)(2,1)S(1)}, bf16[256,768]{1,0:T(8,128)(2,1)S(1)}, u32[]{:S(2)}, u32[]{:S(2)}) collective-permute-start(bf16[256,768]{1,0:T(8,128)(2,1)S(1)} %gather_grad.1.grad_ref.refs_4_), channel_id=1, source_target_pairs={{0,4},{1,5},{2,6},{3,7},{4,0},{5,1},{6,2},{7,3},{8,12},{9,13},{10,... | collective-permute-start | bytes 1179656 | tf_op jit(solution)/shard_map/ppermute | solution.py:441
  30.1 4.4 %copy-start.4 = (bf16[256,768]{1,0:T(8,128)(2,1)S(1)}, bf16[256,768]{1,0:T(8,128)(2,1)}, u32[]{:S(2)}) copy-start(bf16[256,768]{1,0:T(8,128)(2,1)} %get-tuple-element.34.q_ref.refs_3_) | copy-start | bytes 1179652
  30.3 1.0 %copy-start = (bf16[2,256,384]{2,1,0:T(8,128)(2,1)S(1)}, bf16[2,256,384]{2,1,0:T(8,128)(2,1)}, u32[]{:S(2)}) copy-start(bf16[2,256,384]{2,1,0:T(8,128)(2,1)} %get-tuple-element.35.refs_0_.refs_10_) | copy-start | bytes 1179652
  31.3 1.0 %copy-start.2 = (bf16[2,256,384]{2,1,0:T(8,128)(2,1)S(1)}, bf16[2,256,384]{2,1,0:T(8,128)(2,1)}, u32[]{:S(2)}) copy-start(bf16[2,256,384]{2,1,0:T(8,128)(2,1)} %get-tuple-element.36.refs_3_.refs_13_) | copy-start | bytes 1179652
  38.7 4.8 %collective-permute-start.6 = (f32[8,768]{1,0:T(8,128)S(1)}, f32[8,768]{1,0:T(8,128)S(1)}, u32[]{:S(2)}, u32[]{:S(2)}) collective-permute-start(f32[8,768]{1,0:T(8,128)S(1)} %far_totals.1.refs_15_.total_ref.refs_0_.refs_2_), channel_id=1, source_target_pairs={{0,4},{1,5},{2,6},{3,7},{4,0},{5,1},{6,2},{7,3},{8,12},{9,13},{10,... | collective-permute-start | bytes 73736 | tf_op jit(solution)/shard_map/ppermute | solution.py:591
  44.9 17.2 %copy-start.7 = (s32[8,128]{1,0:T(8,128)S(1)}, s32[8,128]{1,0:T(8,128)}, u32[]{:S(2)}) copy-start(s32[8,128]{1,0:T(8,128)} %get-tuple-element.33.table_ref) | copy-start | bytes 12292
  44.9 17.2 %collective-permute-start.7 = (bf16[256,768]{1,0:T(8,128)(2,1)S(1)}, bf16[256,768]{1,0:T(8,128)(2,1)S(1)}, u32[]{:S(2)}, u32[]{:S(2)}) collective-permute-start(bf16[256,768]{1,0:T(8,128)(2,1)S(1)} %far_queries.1), channel_id=1, source_target_pairs={{0,4},{1,5},{2,6},{3,7},{4,0},{5,1},{6,2},{7,3},{8,12},{9,13},{10,... | collective-permute-start | bytes 1179656 | tf_op jit(solution)/shard_map/ppermute | solution.py:559
  45.0 18.0 %collective-permute-start.8 = (bf16[2,256,384]{2,1,0:T(8,128)(2,1)S(1)}, bf16[2,256,384]{2,1,0:T(8,128)(2,1)S(1)}, u32[]{:S(2)}, u32[]{:S(2)}) collective-permute-start(bf16[2,256,384]{2,1,0:T(8,128)(2,1)S(1)} %get-tuple-element.56), channel_id=1, source_target_pairs={{0,1},{4,5},{2,3},{6,7},{1,0},{5,4},{3,2},{7,6},{8,9},{12,13},{10,... | collective-permute-start | bytes 1179656 | tf_op jit(solution)/shard_map/ppermute | solution.py:560
  46.6 21.2 %collective-permute-start.9 = (bf16[2,256,384]{2,1,0:T(8,128)(2,1)S(1)}, bf16[2,256,384]{2,1,0:T(8,128)(2,1)S(1)}, u32[]{:S(2)}, u32[]{:S(2)}) collective-permute-start(bf16[2,256,384]{2,1,0:T(8,128)(2,1)S(1)} %get-tuple-element.57), channel_id=1, source_target_pairs={{1,2},{5,6},{2,1},{6,5},{9,10},{13,14},{10,9},{14,13},{17,18},{21,... | collective-permute-start | bytes 1179656 | tf_op jit(solution)/shard_map/ppermute | solution.py:560
  51.5 16.2 %collective-permute-start.10 = (bf16[2,256,384]{2,1,0:T(8,128)(2,1)S(1)}, bf16[2,256,384]{2,1,0:T(8,128)(2,1)S(1)}, u32[]{:S(2)}, u32[]{:S(2)}) collective-permute-start(bf16[2,256,384]{2,1,0:T(8,128)(2,1)S(1)} %get-tuple-element.58), channel_id=1, source_target_pairs={{0,8},{8,0},{1,9},{9,1},{2,10},{10,2},{3,11},{11,3},{4,12},{12,4},... | collective-permute-start | bytes 1179656 | tf_op jit(solution)/shard_map/ppermute | solution.py:568

commit v7 on v6

--- a/solution.py
+++ b/solution.py
@@ -340,6 +340,13 @@
             dk = dot(grad_scores, q, NN) * plan.scale
             out_ref[0, :, at] = dk.astype(jnp.bfloat16)
             out_ref[1, :, at] = dot(softmax, grad, NN).astype(jnp.bfloat16)
+
+
+def send_kernel(plan, *refs, split):
+    refs, plane_refs = refs[: len(refs) - plan.nc], refs[len(refs) - plan.nc :]
+    refs, dq_refs = refs[: len(refs) - plan.nr], refs[len(refs) - plan.nr :]
+    far_queries_kernel(plan, *refs[:split], *dq_refs)
+    first_grads_kernel(plan, *refs[split:], *plane_refs)
 
 
 def last_grads_kernel(plan, *refs):
@@ -544,18 +551,15 @@
             *(weight, top, slope, total, *kv),
         )
         parts.append((total, *sums))
-    far_dq = call(
-        far_queries_kernel,
-        "far_queries",
-        [low] * plan.nr,
-        0,
-        *(*shared, *(ref for part in parts for ref in part)),
+    sums_operands = [*shared, *(ref for part in parts for ref in part)]
+    outs = call(
+        functools.partial(send_kernel, split=len(sums_operands)),
+        "first_grads",
+        [low] * plan.nr + [packed] * plan.nc,
+        nq * matmul,
+        *(*sums_operands, *operands),
     )
-    plane_out = call(
-        first_grads_kernel, "first_grads", [packed] * plan.nc, nq * matmul, *operands
-    )
-    ready = lax.optimization_barrier((*far_dq, *plane_out))
-    far_dq, plane_out = ready[: plan.nr], ready[plan.nr :]
+    far_dq, plane_out = outs[: plan.nr], outs[plan.nr :]
     back = [lax.ppermute(x, "tile", r) for x, r in zip(far_dq, row_routes)]
     back_plane = [lax.ppermute(x, "tile", r) for x, r in zip(plane_out, col_routes)]
     own_dq, own_dk, own_dv, *across_out = call(

time: 69.2 us -> 69.2 us (level)
    pallas_call x12 -> x11, Pallas kernels: 10.4 us -> 10.2 us  [call(): pl.pallas_call(functools.partial(kernel, plan), out_shape=out_shape, in_s...]
where the time goes in v7:
time: 69.2 us; the launch traced here: 68.7 us
  waiting for transfers between devices  35.2 us (51%)
  Pallas kernels  14.6 us (21%)
  starting transfers between devices  14.4 us (21%)
  local copies, waits for them, and re-layouts  3.68 us (5%)
  between operations  0.83 us (1%)
    ppermute x2, waiting for transfers between devices, from_rows(): return [lax.ppermute(x, 'tile', route) for route in row_routes]  18.3 us
    pallas_call x11, Pallas kernels, call(): pl.pallas_call(functools.partial(kernel, plan), out_shape=out_shape, in_s...  10.2 us
    ppermute x1, waiting for transfers between devices, local(): back = [lax.ppermute(x, 'tile', r) for x, r in zip(far_dq, row_routes)]  8.89 us
    ppermute x2, waiting for transfers between devices, local(): lax.ppermute(x, 'tile', r)  4.9 us
    ppermute x2, starting transfers between devices, local(): lax.ppermute(x, 'tile', r)  4.58 us
    unnamed x16, local copies, waits for them, and re-layouts  3.68 us
    pallas_call x1, Pallas kernels, local(): pl.pallas_call(functools.partial(prepare_kernel, plan), out_shape=[table_...  3.39 us
    ppermute x2, starting transfers between devices, local(): near_plane = [lax.ppermute(plane_kv, 'tile', route) for route in col_routes]  3.34 us
  transfers between devices with their start and end apart: 11, of which 5 were waited for; matrix products, arithmetic and copies ran while one was open for 0% of the time, Pallas kernels for 18%

profile of v7, /device:TPU:24, one launch (start us, length us, event | category | flops | bytes accessed | tf_op | source)
XLA Modules:
  0.0 68.7 jit_solution(14124263154020220753)
XLA Ops:
  0.6 0.1 collective-permute-start.1
  0.7 0.4 collective-permute-start
  1.1 3.4 %prepare.1 = (s32[8,128]{1,0:T(8,128)}, bf16[2,256,384]{2,1,0:T(8,128)(2,1)}, bf16[2,256,384]{2,1,0:T(8,128)(2,1)}, bf16[256,768]{1,0:T(8,128)(2,1)}) custom-call(s32[6,3,9]{2,1,0:T(4,128)} %bitcast.15, s32[2,8]{1,0:T(2,128)} %counts_ref.1, bf16[256,768]{1,0:T(8,128)(2,1)} %bitcast.13, bf16[256,768]{1,0:T(8,128)(2,1)} %bitcast.10, bf16[256,768]{1,0:T(8,128)(2,1)} %bitcast.11), custom_call_target="tpu_custom_call" | custom-call | tf_op jit(solution)/shard_map/prepare/pallas_call | solution.py:483
  4.5 0.0 copy-start.1
  4.5 0.0 copy-start.3
  4.5 1.6 %collective-permute-start.4 = (bf16[2,256,384]{2,1,0:T(8,128)(2,1)}, bf16[2,256,384]{2,1,0:T(8,128)(2,1)S(1)}, u32[]{:S(2)}, u32[]{:S(2)}) collective-permute-start(bf16[2,256,384]{2,1,0:T(8,128)(2,1)} %get-tuple-element.34.refs_3_.refs_13_.refs_18_), channel_id=1, source_target_pairs={{0,8},{8,0},{1,9},{9,1},{2,10},{10,2},{3,11},{11,3},{4,12},{12,4},... | collective-permute-start | bytes 1179656 | tf_op jit(solution)/shard_map/ppermute | solution.py:497
  6.1 3.3 %collective-permute-start.3 = (bf16[2,256,384]{2,1,0:T(8,128)(2,1)}, bf16[2,256,384]{2,1,0:T(8,128)(2,1)S(1)}, u32[]{:S(2)}, u32[]{:S(2)}) collective-permute-start(bf16[2,256,384]{2,1,0:T(8,128)(2,1)} %get-tuple-element.33.refs_0_.refs_10_.refs_15_), channel_id=1, source_target_pairs={{1,2},{5,6},{2,1},{6,5},{9,10},{13,14},{10,9},{14,13},{17,18},{21,... | collective-permute-start | bytes 1179656 | tf_op jit(solution)/shard_map/ppermute | solution.py:496
  9.4 0.1 collective-permute-start.2
  9.5 0.0 collective-permute-done.1.refs_0_
  9.5 0.0 copy-start.5
  9.5 1.0 %copy-done.5 = bf16[1,1,128,1536]{3,2,1,0:T(8,128)(2,1)S(1)} copy-done((bf16[1,1,128,1536]{3,2,1,0:T(8,128)(2,1)S(1)}, bf16[1,1,128,1536]{3,2,1,0:T(8,128)(2,1)}, u32[]{:S(2)}) %copy-start.5) | copy-done | bytes 393240
  10.5 0.0 copy-start.6
  10.5 0.7 copy-done.6
  11.2 0.1 gather_grad.1.grad_ref.refs_4_.refs_9_
  11.3 2.7 %collective-permute-start.5 = (bf16[256,768]{1,0:T(8,128)(2,1)S(1)}, bf16[256,768]{1,0:T(8,128)(2,1)S(1)}, u32[]{:S(2)}, u32[]{:S(2)}) collective-permute-start(bf16[256,768]{1,0:T(8,128)(2,1)S(1)} %gather_grad.1.grad_ref.refs_4_.refs_9_), channel_id=1, source_target_pairs={{0,4},{1,5},{2,6},{3,7},{4,0},{5,1},{6,2},{7,3},{8,12},{9,13},{10,... | collective-permute-start | bytes 1179656 | tf_op jit(solution)/shard_map/ppermute | solution.py:448
  14.0 16.2 %collective-permute-done.q_ref = bf16[256,768]{1,0:T(8,128)(2,1)S(1)} collective-permute-done((bf16[256,768]{1,0:T(8,128)(2,1)}, bf16[256,768]{1,0:T(8,128)(2,1)S(1)}, u32[]{:S(2)}, u32[]{:S(2)}) %collective-permute-start) | collective-permute-done | bytes 393248 | tf_op jit(solution)/shard_map/ppermute | solution.py:448
  30.1 0.0 copy-start.4
  30.1 0.1 order_queries.1.q_ref.refs_8_.refs_13_
  30.2 0.0 collective-permute-done.4.refs_4_.refs_14_.refs_19_
  30.2 0.0 collective-permute-done.3.refs_2_.refs_12_.refs_17_
  30.3 0.0 collective-permute-done.2.refs_1_.refs_11_.refs_16_
  30.3 0.0 copy-start
  30.3 1.0 %copy-done = bf16[2,256,384]{2,1,0:T(8,128)(2,1)S(1)} copy-done((bf16[2,256,384]{2,1,0:T(8,128)(2,1)S(1)}, bf16[2,256,384]{2,1,0:T(8,128)(2,1)}, u32[]{:S(2)}) %copy-start) | copy-done | bytes 393240
  31.3 0.0 copy-start.2
  31.3 1.0 %copy-done.2 = bf16[2,256,384]{2,1,0:T(8,128)(2,1)S(1)} copy-done((bf16[2,256,384]{2,1,0:T(8,128)(2,1)S(1)}, bf16[2,256,384]{2,1,0:T(8,128)(2,1)}, u32[]{:S(2)}) %copy-start.2) | copy-done | bytes 393240
  32.3 1.5 %far_weights.1 = (f32[15,256,256]{2,1,0:T(8,128)S(1)}, f32[16,256]{1,0:T(8,128)S(1)}, f32[16,256]{1,0:T(8,128)S(1)}) custom-call(s32[8,128]{1,0:T(8,128)S(1)} %copy-done.6, bf16[256,768]{1,0:T(8,128)(2,1)S(1)} %order_queries.1.q_ref.refs_8_.refs_13_, bf16[2,256,384]{2,1,0:T(8,128)(2,1)S(1)} %copy-done, ...), custom_call_target="tpu_custom_call" | custom-call | flops 251658240 | bytes 1048576 | tf_op jit(solution)/shard_map/far_weights/pallas_call | solution.py:456
  33.7 0.0 copy-done.1
  33.7 0.0 copy-done.3
  33.7 0.7 %far_values.1 = (f32[4,768]{1,0:T(4,128)S(1)}, f32[768,256]{1,0:T(8,128)S(1)}) custom-call(f32[15,256,256]{2,1,0:T(8,128)S(1)} %get-tuple-element.39.weight_ref.refs_5_.refs_10_, f32[16,256]{1,0:T(8,128)S(1)} %get-tuple-element.40.top_ref.refs_6_.refs_11_, f32[16,256]{1,0:T(8,128)S(1)} %get-tuple-element.41.sum_ref, bf16[2,256,384]{2,1,0:T(8,128)(2,1)S(1)} %copy-done.1, ...), custom_call_target="tpu_custom_call" | custom-call | flops 251658240 | bytes 1048576 | tf_op jit(solution)/shard_map/far_values/pallas_call | solution.py:456
  34.5 0.0 copy-done.4
  34.5 1.9 %own_rows.1 = (f32[15,256,256]{2,1,0:T(8,128)S(1)}, f32[16,256]{1,0:T(8,128)S(1)}, f32[15,256,256]{2,1,0:T(8,128)S(1)}, f32[4,768]{1,0:T(4,128)S(1)}) custom-call(s32[8,128]{1,0:T(8,128)S(1)} %copy-done.6, bf16[256,768]{1,0:T(8,128)(2,1)S(1)} %copy-done.4, bf16[256,768]{1,0:T(8,128)(2,1)S(1)} %gather_grad.1.grad_ref.refs_4_.refs_9_, ...), custom_call_target="tpu_custom_call" | custom-call | flops 503316480 | bytes 1048576 | tf_op jit(solution)/shard_map/own_rows/pallas_call | solution.py:456
  36.4 2.1 %collective-permute-done.5.grad_ref.refs_9_.refs_14_ = bf16[256,768]{1,0:T(8,128)(2,1)S(1)} collective-permute-done((bf16[256,768]{1,0:T(8,128)(2,1)S(1)}, bf16[256,768]{1,0:T(8,128)(2,1)S(1)}, u32[]{:S(2)}, u32[]{:S(2)}) %collective-permute-start.5) | collective-permute-done | bytes 393248 | tf_op jit(solution)/shard_map/ppermute | solution.py:448
  38.5 0.2 far_totals.1.refs_15_.total_ref.refs_0_.refs_2_.refs_20_
  38.7 0.1 collective-permute-start.6
  38.8 0.7 far_slopes.1.refs_7_.slope_ref.refs_12_
  39.5 0.9 %far_sums.1 = (f32[768,256]{1,0:T(8,128)S(1)}, f32[768,256]{1,0:T(8,128)S(1)}) custom-call(f32[15,256,256]{2,1,0:T(8,128)S(1)} %get-tuple-element.39.weight_ref.refs_5_.refs_10_, f32[16,256]{1,0:T(8,128)S(1)} %get-tuple-element.40.top_ref.refs_6_.refs_11_, f32[15,256,256]{2,1,0:T(8,128)S(1)} %far_slopes.1.refs_7_.slope_ref.refs_12_, ...), custom_call_target="tpu_custom_call" | custom-call | flops 503316480 | bytes 1048576 | tf_op jit(solution)/shard_map/far_sums/pallas_call | solution.py:456
  40.4 3.1 %collective-permute-done.6.refs_16_.refs_1_.refs_21_ = f32[8,768]{1,0:T(8,128)S(1)} collective-permute-done((f32[8,768]{1,0:T(8,128)S(1)}, f32[8,768]{1,0:T(8,128)S(1)}, u32[]{:S(2)}, u32[]{:S(2)}) %collective-permute-start.6) | collective-permute-done | bytes 24608 | tf_op jit(solution)/shard_map/ppermute | solution.py:595
  43.5 1.2 %first_grads.1 = (bf16[256,768]{1,0:T(8,128)(2,1)S(1)}, bf16[2,256,384]{2,1,0:T(8,128)(2,1)S(1)}, bf16[2,256,384]{2,1,0:T(8,128)(2,1)S(1)}) custom-call(f32[8,768]{1,0:T(8,128)S(1)} %far_totals.1.refs_15_.total_ref.refs_0_.refs_2_.refs_20_, f32[8,768]{1,0:T(8,128)S(1)} %collective-permute-done.6.refs_16_.refs_1_.refs_21_, ...), custom_call_target="tpu_custom_call" | custom-call | flops 503316480 | bytes 1048576 | tf_op jit(solution)/shard_map/first_grads/pallas_call | solution.py:456
  44.7 0.1 collective-permute-start.7
  44.8 1.6 %collective-permute-start.8 = (bf16[2,256,384]{2,1,0:T(8,128)(2,1)S(1)}, bf16[2,256,384]{2,1,0:T(8,128)(2,1)S(1)}, u32[]{:S(2)}, u32[]{:S(2)}) collective-permute-start(bf16[2,256,384]{2,1,0:T(8,128)(2,1)S(1)} %get-tuple-element.52), channel_id=1, source_target_pairs={{0,1},{4,5},{2,3},{6,7},{1,0},{5,4},{3,2},{7,6},{8,9},{12,13},{10,... | collective-permute-start | bytes 1179656 | tf_op jit(solution)/shard_map/ppermute | solution.py:564
  46.4 0.0 copy-start.7
  46.4 3.0 %collective-permute-start.9 = (bf16[2,256,384]{2,1,0:T(8,128)(2,1)S(1)}, bf16[2,256,384]{2,1,0:T(8,128)(2,1)S(1)}, u32[]{:S(2)}, u32[]{:S(2)}) collective-permute-start(bf16[2,256,384]{2,1,0:T(8,128)(2,1)S(1)} %get-tuple-element.53), channel_id=1, source_target_pairs={{1,2},{5,6},{2,1},{6,5},{9,10},{13,14},{10,9},{14,13},{17,18},{21,... | collective-permute-start | bytes 1179656 | tf_op jit(solution)/shard_map/ppermute | solution.py:564
  49.4 2.1 %last_grads.1 = (f32[256,768]{1,0:T(8,128)S(1)}, f32[256,768]{1,0:T(8,128)S(1)}, f32[256,768]{1,0:T(8,128)S(1)}, bf16[2,256,384]{2,1,0:T(8,128)(2,1)S(1)}) custom-call(f32[15,256,256]{2,1,0:T(8,128)S(1)} %get-tuple-element.35.refs_0_.refs_5_, f32[16,256]{1,0:T(8,128)S(1)} %get-tuple-element.36.refs_1_.refs_6_, ...), custom_call_target="tpu_custom_call" | custom-call | flops 503316480 | bytes 1048576 | tf_op jit(solution)/shard_map/last_grads/pallas_call | solution.py:456
  51.5 1.6 %collective-permute-start.10 = (bf16[2,256,384]{2,1,0:T(8,128)(2,1)S(1)}, bf16[2,256,384]{2,1,0:T(8,128)(2,1)S(1)}, u32[]{:S(2)}, u32[]{:S(2)}) collective-permute-start(bf16[2,256,384]{2,1,0:T(8,128)(2,1)S(1)} %get-tuple-element.54), channel_id=1, source_target_pairs={{0,8},{8,0},{1,9},{9,1},{2,10},{10,2},{3,11},{11,3},{4,12},{12,4},... | collective-permute-start | bytes 1179656 | tf_op jit(solution)/shard_map/ppermute | solution.py:572
  53.0 8.9 %collective-permute-done.7.refs_1_ = bf16[256,768]{1,0:T(8,128)(2,1)S(1)} collective-permute-done((bf16[256,768]{1,0:T(8,128)(2,1)S(1)}, bf16[256,768]{1,0:T(8,128)(2,1)S(1)}, u32[]{:S(2)}, u32[]{:S(2)}) %collective-permute-start.7) | collective-permute-done | bytes 393248 | tf_op jit(solution)/shard_map/ppermute | solution.py:563
  61.9 0.0 copy-done.7
  61.9 0.9 %add_query.1 = bf16[256,768]{1,0:T(8,128)(2,1)} custom-call(s32[8,128]{1,0:T(8,128)S(1)} %copy-done.7, f32[256,768]{1,0:T(8,128)S(1)} %get-tuple-element.46.refs_0_, bf16[256,768]{1,0:T(8,128)(2,1)S(1)} %collective-permute-done.7.refs_1_), custom_call_target="tpu_custom_call" | custom-call | bytes 1048576 | tf_op jit(solution)/shard_map/add_query/pallas_call | solution.py:456
  62.8 0.0 collective-permute-done.8.refs_2_
  62.8 4.9 %collective-permute-done.9.refs_3_ = bf16[2,256,384]{2,1,0:T(8,128)(2,1)S(1)} collective-permute-done((bf16[2,256,384]{2,1,0:T(8,128)(2,1)S(1)}, bf16[2,256,384]{2,1,0:T(8,128)(2,1)S(1)}, u32[]{:S(2)}, u32[]{:S(2)}) %collective-permute-start.9) | collective-permute-done | bytes 393248 | tf_op jit(solution)/shard_map/ppermute | solution.py:564
  67.7 0.0 collective-permute-done.10.refs_4_
  67.7 1.0 %add_key.1 = (bf16[256,768]{1,0:T(8,128)(2,1)}, bf16[256,768]{1,0:T(8,128)(2,1)}) custom-call(s32[8,128]{1,0:T(8,128)S(1)} %copy-done.7, f32[256,768]{1,0:T(8,128)S(1)} %get-tuple-element.50.refs_0_, f32[256,768]{1,0:T(8,128)S(1)} %get-tuple-element.51.refs_1_, bf16[2,256,384]{2,1,0:T(8,128)(2,1)S(1)} %collective-permute-done.8.refs_2_, ...), custom_call_target="tpu_custom_call" | custom-call | bytes 1048576 | tf_op jit(solution)/shard_map/add_key/pallas_call | solution.py:575
Async XLA Ops:
  0.6 8.8 %collective-permute-start.1 = (bf16[128,1536]{1,0:T(8,128)(2,1)}, bf16[128,1536]{1,0:T(8,128)(2,1)S(1)}, u32[]{:S(2)}, u32[]{:S(2)}) collective-permute-start(bf16[128,1536]{1,0:T(8,128)(2,1)} %bitcast.8), channel_id=1, source_target_pairs={{0,16},{16,0},{1,17},{17,1},{2,18},{18,2},{3,19},{19,3},{4,20},{20... | collective-permute-start | bytes 1179656 | tf_op jit(solution)/shard_map/ppermute | solution.py:479
  0.7 29.4 %collective-permute-start = (bf16[256,768]{1,0:T(8,128)(2,1)}, bf16[256,768]{1,0:T(8,128)(2,1)S(1)}, u32[]{:S(2)}, u32[]{:S(2)}) collective-permute-start(bf16[256,768]{1,0:T(8,128)(2,1)} %bitcast.12), channel_id=1, source_target_pairs={{0,4},{1,5},{2,6},{3,7},{4,0},{5,1},{6,2},{7,3},{8,12},{9,13},{10,... | collective-permute-start | bytes 1179656 | tf_op jit(solution)/shard_map/ppermute | solution.py:448
  4.5 29.2 %copy-start.1 = (bf16[2,256,384]{2,1,0:T(8,128)(2,1)S(1)}, bf16[2,256,384]{2,1,0:T(8,128)(2,1)}, u32[]{:S(2)}) copy-start(bf16[2,256,384]{2,1,0:T(8,128)(2,1)} %get-tuple-element.33.refs_0_.refs_10_.refs_15_) | copy-start | bytes 1179652
  4.5 29.2 %copy-start.3 = (bf16[2,256,384]{2,1,0:T(8,128)(2,1)S(1)}, bf16[2,256,384]{2,1,0:T(8,128)(2,1)}, u32[]{:S(2)}) copy-start(bf16[2,256,384]{2,1,0:T(8,128)(2,1)} %get-tuple-element.34.refs_3_.refs_13_.refs_18_) | copy-start | bytes 1179652
  4.5 25.7 %collective-permute-start.4 = (bf16[2,256,384]{2,1,0:T(8,128)(2,1)}, bf16[2,256,384]{2,1,0:T(8,128)(2,1)S(1)}, u32[]{:S(2)}, u32[]{:S(2)}) collective-permute-start(bf16[2,256,384]{2,1,0:T(8,128)(2,1)} %get-tuple-element.34.refs_3_.refs_13_.refs_18_), channel_id=1, source_target_pairs={{0,8},{8,0},{1,9},{9,1},{2,10},{10,2},{3,11},{11,3},{4,12},{12,4},... | collective-permute-start | bytes 1179656 | tf_op jit(solution)/shard_map/ppermute | solution.py:497
  6.1 24.1 %collective-permute-start.3 = (bf16[2,256,384]{2,1,0:T(8,128)(2,1)}, bf16[2,256,384]{2,1,0:T(8,128)(2,1)S(1)}, u32[]{:S(2)}, u32[]{:S(2)}) collective-permute-start(bf16[2,256,384]{2,1,0:T(8,128)(2,1)} %get-tuple-element.33.refs_0_.refs_10_.refs_15_), channel_id=1, source_target_pairs={{1,2},{5,6},{2,1},{6,5},{9,10},{13,14},{10,9},{14,13},{17,18},{21,... | collective-permute-start | bytes 1179656 | tf_op jit(solution)/shard_map/ppermute | solution.py:496
  9.4 20.9 %collective-permute-start.2 = (bf16[2,256,384]{2,1,0:T(8,128)(2,1)}, bf16[2,256,384]{2,1,0:T(8,128)(2,1)S(1)}, u32[]{:S(2)}, u32[]{:S(2)}) collective-permute-start(bf16[2,256,384]{2,1,0:T(8,128)(2,1)} %get-tuple-element.33.refs_0_.refs_10_.refs_15_), channel_id=1, source_target_pairs={{0,1},{4,5},{2,3},{6,7},{1,0},{5,4},{3,2},{7,6},{8,9},{12,13},{10,... | collective-permute-start | bytes 1179656 | tf_op jit(solution)/shard_map/ppermute | solution.py:496
  9.5 1.0 %copy-start.5 = (bf16[1,1,128,1536]{3,2,1,0:T(8,128)(2,1)S(1)}, bf16[1,1,128,1536]{3,2,1,0:T(8,128)(2,1)}, u32[]{:S(2)}) copy-start(bf16[1,1,128,1536]{3,2,1,0:T(8,128)(2,1)} %param.9) | copy-start | bytes 1179652
  10.5 0.7 copy-start.6
  11.3 27.2 %collective-permute-start.5 = (bf16[256,768]{1,0:T(8,128)(2,1)S(1)}, bf16[256,768]{1,0:T(8,128)(2,1)S(1)}, u32[]{:S(2)}, u32[]{:S(2)}) collective-permute-start(bf16[256,768]{1,0:T(8,128)(2,1)S(1)} %gather_grad.1.grad_ref.refs_4_.refs_9_), channel_id=1, source_target_pairs={{0,4},{1,5},{2,6},{3,7},{4,0},{5,1},{6,2},{7,3},{8,12},{9,13},{10,... | collective-permute-start | bytes 1179656 | tf_op jit(solution)/shard_map/ppermute | solution.py:448
  30.1 4.4 %copy-start.4 = (bf16[256,768]{1,0:T(8,128)(2,1)S(1)}, bf16[256,768]{1,0:T(8,128)(2,1)}, u32[]{:S(2)}) copy-start(bf16[256,768]{1,0:T(8,128)(2,1)} %get-tuple-element.32.q_ref.refs_3_.refs_8_) | copy-start | bytes 1179652
  30.3 1.0 %copy-start = (bf16[2,256,384]{2,1,0:T(8,128)(2,1)S(1)}, bf16[2,256,384]{2,1,0:T(8,128)(2,1)}, u32[]{:S(2)}) copy-start(bf16[2,256,384]{2,1,0:T(8,128)(2,1)} %get-tuple-element.33.refs_0_.refs_10_.refs_15_) | copy-start | bytes 1179652
  31.3 1.0 %copy-start.2 = (bf16[2,256,384]{2,1,0:T(8,128)(2,1)S(1)}, bf16[2,256,384]{2,1,0:T(8,128)(2,1)}, u32[]{:S(2)}) copy-start(bf16[2,256,384]{2,1,0:T(8,128)(2,1)} %get-tuple-element.34.refs_3_.refs_13_.refs_18_) | copy-start | bytes 1179652
  38.7 4.8 %collective-permute-start.6 = (f32[8,768]{1,0:T(8,128)S(1)}, f32[8,768]{1,0:T(8,128)S(1)}, u32[]{:S(2)}, u32[]{:S(2)}) collective-permute-start(f32[8,768]{1,0:T(8,128)S(1)} %far_totals.1.refs_15_.total_ref.refs_0_.refs_2_.refs_20_), channel_id=1, source_target_pairs={{0,4},{1,5},{2,6},{3,7},{4,0},{5,1},{6,2},{7,3},{8,12},{9,13},{10,... | collective-permute-start | bytes 73736 | tf_op jit(solution)/shard_map/ppermute | solution.py:595
  44.7 17.2 %collective-permute-start.7 = (bf16[256,768]{1,0:T(8,128)(2,1)S(1)}, bf16[256,768]{1,0:T(8,128)(2,1)S(1)}, u32[]{:S(2)}, u32[]{:S(2)}) collective-permute-start(bf16[256,768]{1,0:T(8,128)(2,1)S(1)} %get-tuple-element.49), channel_id=1, source_target_pairs={{0,4},{1,5},{2,6},{3,7},{4,0},{5,1},{6,2},{7,3},{8,12},{9,13},{10,... | collective-permute-start | bytes 1179656 | tf_op jit(solution)/shard_map/ppermute | solution.py:563
  44.8 18.0 %collective-permute-start.8 = (bf16[2,256,384]{2,1,0:T(8,128)(2,1)S(1)}, bf16[2,256,384]{2,1,0:T(8,128)(2,1)S(1)}, u32[]{:S(2)}, u32[]{:S(2)}) collective-permute-start(bf16[2,256,384]{2,1,0:T(8,128)(2,1)S(1)} %get-tuple-element.52), channel_id=1, source_target_pairs={{0,1},{4,5},{2,3},{6,7},{1,0},{5,4},{3,2},{7,6},{8,9},{12,13},{10,... | collective-permute-start | bytes 1179656 | tf_op jit(solution)/shard_map/ppermute | solution.py:564
  46.4 15.5 %copy-start.7 = (s32[8,128]{1,0:T(8,128)S(1)}, s32[8,128]{1,0:T(8,128)}, u32[]{:S(2)}) copy-start(s32[8,128]{1,0:T(8,128)} %get-tuple-element.31.table_ref) | copy-start | bytes 12292
  46.4 21.3 %collective-permute-start.9 = (bf16[2,256,384]{2,1,0:T(8,128)(2,1)S(1)}, bf16[2,256,384]{2,1,0:T(8,128)(2,1)S(1)}, u32[]{:S(2)}, u32[]{:S(2)}) collective-permute-start(bf16[2,256,384]{2,1,0:T(8,128)(2,1)S(1)} %get-tuple-element.53), channel_id=1, source_target_pairs={{1,2},{5,6},{2,1},{6,5},{9,10},{13,14},{10,9},{14,13},{17,18},{21,... | collective-permute-start | bytes 1179656 | tf_op jit(solution)/shard_map/ppermute | solution.py:564
  51.5 16.2 %collective-permute-start.10 = (bf16[2,256,384]{2,1,0:T(8,128)(2,1)S(1)}, bf16[2,256,384]{2,1,0:T(8,128)(2,1)S(1)}, u32[]{:S(2)}, u32[]{:S(2)}) collective-permute-start(bf16[2,256,384]{2,1,0:T(8,128)(2,1)S(1)} %get-tuple-element.54), channel_id=1, source_target_pairs={{0,8},{8,0},{1,9},{9,1},{2,10},{10,2},{3,11},{11,3},{4,12},{12,4},... | collective-permute-start | bytes 1179656 | tf_op jit(solution)/shard_map/ppermute | solution.py:572
